TPU v7x, 32 devices: a whole 2x2x4 slice. The times are simulated.
32 devices in a mesh: dp: 8 (over y, x, core), tensor: 4 (over z).
Axes of the slice: x: 2, y: 2, z: 4, core: 2. Of those that a mesh axis runs over, the one named last changes fastest.
Arguments:
- inputs: bfloat16 [2048, 1024], P(('dp', 'tensor')), may hold values from -6 to 6
- first_gain: float32 [1024], replicated, may hold values from 0.1 to 1.9
- entry_projection_weight: bfloat16 [3, 1024, 1024], P(None, 'dp', 'tensor'), may hold values from -0.1875 to 0.1875
- conv_weight: float32 [3, 1024], replicated, may hold values from -3 to 3
- out_weight: bfloat16 [1024, 1024], P('tensor', 'dp'), may hold values from -0.1875 to 0.1875
- second_gain: float32 [1024], replicated, may hold values from 0.1 to 1.9
- gate_up_weight: bfloat16 [2, 1024, 4608], P(None, 'dp', 'tensor'), may hold values from -0.1875 to 0.1875
- down_weight: bfloat16 [4608, 1024], P('tensor', 'dp'), may hold values from -0.09375 to 0.09375
- cotangent: bfloat16 [2048, 1024], P(('dp', 'tensor')), may hold values from -6 to 6
- lengths: int32 [4], replicated, may hold values from 1 to 1024, 2048 in all
Outputs:
- output: bfloat16 [2048, 1024], P(('dp', 'tensor'))
- input_grad: float32 [2048, 1024], P(('dp', 'tensor'))
- first_gain_grad: float32 [1024], replicated
- in_weight_grad: float32 [3, 1024, 1024], P(None, 'dp', 'tensor')
- filter_weight_gradient: float32 [3, 1024], replicated
- out_weight_grad: float32 [1024, 1024], P('tensor', 'dp')
- second_gain_grad: float32 [1024], replicated
- gate_up_grad: float32 [2, 1024, 4608], P(None, 'dp', 'tensor')
- down_grad: float32 [4608, 1024], P('tensor', 'dp')
Inputs may be any that keep to these rules, and one draw needn't show every extreme that they name: lengths of the 4 sequences packed end to end in token order; they sum to 2048, and the longest is exactly 1024.
All inputs are finite; a program needn't handle non-finite values.
Results may differ from a plain program's by a relative error of at most 0.012.
Values may be sent and summed in bfloat16 or wider, within the bound.
A program may use at most 128 MiB of HBM per device.

v0:
```python
import jax
import jax.numpy as jnp
from jax import lax
from jax.sharding import PartitionSpec as P

EPS = 1e-05


def passed_along(block, axis, distance):
    devices = range(lax.axis_size(axis))
    route = [(i - distance, i) for i in devices if i - distance in devices]
    return lax.ppermute(block, axis, route)


def rms_norm(values, gain):
    return values * lax.rsqrt(jnp.mean(values * values, axis=-1, keepdims=True) + EPS) * gain


def rms_back(values, gain, grad_out):
    scale = lax.rsqrt(jnp.mean(values * values, axis=-1, keepdims=True) + EPS)
    normal = values * scale
    weighted = gain * grad_out
    grad_in = scale * (weighted - normal * jnp.mean(normal * weighted, axis=-1, keepdims=True))
    return (grad_in, jnp.sum(normal * grad_out, axis=0))


def times_trans(left, right):
    return lax.dot_general(
        left, right, (((1,), (1,)), ((), ())), preferred_element_type=jnp.float32
    )


def trans_times(left, right):
    return lax.dot_general(
        left, right, (((0,), (0,)), ((), ())), preferred_element_type=jnp.float32
    )


def shards(
    inputs,
    first_gain,
    entry_projection_weight,
    conv_weight,
    out_weight,
    second_gain,
    gate_up_weight,
    down_weight,
    cotangent,
    lengths,
):
    own_rows = inputs.shape[0]
    group_rows = own_rows * lax.axis_size("tensor")
    channels = entry_projection_weight.shape[2]
    column = lax.axis_index("tensor") * channels
    start = lax.axis_index("dp") * group_rows
    ends = jnp.cumsum(lengths)
    places = start - 2 + jnp.arange(group_rows + 4, dtype=jnp.int32)
    segment = jnp.sum((places[:, None] >= ends[None, :]).astype(jnp.int32), axis=1)
    first_all = jnp.logical_and(segment[2:] == segment[1:-1], places[2:] >= 1).astype(jnp.float32)[
        :, None
    ]
    second_all = jnp.logical_and(segment[2:] == segment[:-2], places[2:] >= 2).astype(jnp.float32)[
        :, None
    ]
    first_keep = first_all[:group_rows]
    second_keep = second_all[:group_rows]
    kernel = lax.dynamic_slice_in_dim(conv_weight, column, channels, 1)
    residual = inputs.astype(jnp.float32)
    normed = lax.all_gather(
        rms_norm(residual, first_gain).astype(jnp.bfloat16), "tensor", axis=0, tiled=True
    )
    in_full, out_full, gate_up_full, down_full = (
        lax.all_gather(entry_projection_weight, "dp", axis=1, tiled=True),
        lax.all_gather(out_weight, "dp", axis=1, tiled=True),
        lax.all_gather(gate_up_weight, "dp", axis=1, tiled=True),
        lax.all_gather(down_weight, "dp", axis=1, tiled=True),
    )
    projected = jnp.einsum("td,kdc->ktc", normed, in_full, preferred_element_type=jnp.float32)
    input_gate_value = projected[0]
    c_value = projected[1]
    v_value = projected[2]
    product = (input_gate_value * v_value).astype(jnp.bfloat16)
    before = passed_along(product[-2:], "dp", 1)
    extended = jnp.concatenate([before, product], axis=0).astype(jnp.float32)
    mixed = (
        kernel[2] * extended[2:]
        + kernel[1] * first_keep * extended[1:-1]
        + kernel[0] * second_keep * extended[:-2]
    )
    gated = (c_value * mixed).astype(jnp.bfloat16)
    mixer_part = jnp.dot(gated, out_full, preferred_element_type=jnp.float32)
    middle = residual + lax.psum_scatter(mixer_part, "tensor", scatter_dimension=0, tiled=True)
    hidden_in = lax.all_gather(
        rms_norm(middle, second_gain).astype(jnp.bfloat16), "tensor", axis=0, tiled=True
    )
    gate_up = jnp.einsum("td,kdf->ktf", hidden_in, gate_up_full, preferred_element_type=jnp.float32)
    gate_value = gate_up[0]
    up_value = gate_up[1]
    sigmoid = jax.nn.sigmoid(gate_value)
    swish = gate_value * sigmoid
    hidden = (swish * up_value).astype(jnp.bfloat16)
    ffn_part = jnp.dot(hidden, down_full, preferred_element_type=jnp.float32)
    output = (
        middle
        + lax.psum_scatter(
            ffn_part.astype(jnp.bfloat16), "tensor", scatter_dimension=0, tiled=True
        ).astype(jnp.float32)
    ).astype(jnp.bfloat16)
    in_full, out_full, gate_up_full, down_full = (
        lax.all_gather(entry_projection_weight, "dp", axis=1, tiled=True),
        lax.all_gather(out_weight, "dp", axis=1, tiled=True),
        lax.all_gather(gate_up_weight, "dp", axis=1, tiled=True),
        lax.all_gather(down_weight, "dp", axis=1, tiled=True),
    )
    grad_rows = lax.all_gather(cotangent, "tensor", axis=0, tiled=True)
    grad_hidden = times_trans(grad_rows, down_full)
    down_part = trans_times(hidden, grad_rows)
    grad_gate = (grad_hidden * up_value * sigmoid * (1.0 + gate_value * (1.0 - sigmoid))).astype(
        jnp.bfloat16
    )
    grad_up = (grad_hidden * swish).astype(jnp.bfloat16)
    gate_up_stack = jnp.stack([grad_gate, grad_up])
    gate_up_part = jnp.einsum(
        "td,ktf->kdf", hidden_in, gate_up_stack, preferred_element_type=jnp.float32
    )
    hidden_back = jnp.einsum(
        "ktf,kdf->td", gate_up_stack, gate_up_full, preferred_element_type=jnp.float32
    )
    grad_hin = lax.psum_scatter(hidden_back, "tensor", scatter_dimension=0, tiled=True)
    second_back, second_part = rms_back(middle, second_gain, grad_hin)
    grad_middle = cotangent.astype(jnp.float32) + second_back
    branch_rows = lax.all_gather(grad_middle.astype(jnp.bfloat16), "tensor", axis=0, tiled=True)
    grad_gated = times_trans(branch_rows, out_full)
    out_part = trans_times(gated, branch_rows)
    output_gate_gradient = (grad_gated * mixed).astype(jnp.bfloat16)
    grad_mixed = (grad_gated * c_value).astype(jnp.bfloat16)
    after = passed_along(grad_mixed[:2], "dp", -1)
    grad_ext = jnp.concatenate([grad_mixed, after], axis=0).astype(jnp.float32)
    mixed_wide = grad_ext[:-2]
    kernel_part = jnp.stack(
        [
            jnp.sum(second_keep * extended[:-2] * mixed_wide, axis=0),
            jnp.sum(first_keep * extended[1:-1] * mixed_wide, axis=0),
            jnp.sum(extended[2:] * mixed_wide, axis=0),
        ]
    )
    kernel_full = lax.dynamic_update_slice_in_dim(
        jnp.zeros(conv_weight.shape, jnp.float32), kernel_part, column, 1
    )
    elementwise_product_gradient = (
        kernel[2] * grad_ext[:-2]
        + kernel[1] * first_all[1:-1] * grad_ext[1:-1]
        + kernel[0] * second_all[2:] * grad_ext[2:]
    )
    input_gate_gradient = (elementwise_product_gradient * v_value).astype(jnp.bfloat16)
    value_branch_gradient = (elementwise_product_gradient * input_gate_value).astype(jnp.bfloat16)
    stacked_projection_outputs = jnp.stack(
        [input_gate_gradient, output_gate_gradient, value_branch_gradient]
    )
    in_part = jnp.einsum(
        "td,ktc->kdc", normed, stacked_projection_outputs, preferred_element_type=jnp.float32
    )
    normed_back = jnp.einsum(
        "ktc,kdc->td", stacked_projection_outputs, in_full, preferred_element_type=jnp.float32
    )
    grad_normed = lax.psum_scatter(
        normed_back.astype(jnp.bfloat16), "tensor", scatter_dimension=0, tiled=True
    ).astype(jnp.float32)
    first_back, first_part = rms_back(residual, first_gain, grad_normed)
    input_grad = grad_middle + first_back
    in_grad, out_grad, gate_up_grad, down_grad = (
        lax.psum_scatter(in_part, "dp", scatter_dimension=1, tiled=True),
        lax.psum_scatter(out_part, "dp", scatter_dimension=1, tiled=True),
        lax.psum_scatter(gate_up_part, "dp", scatter_dimension=1, tiled=True),
        lax.psum_scatter(down_part, "dp", scatter_dimension=1, tiled=True),
    )
    first_gain_grad, second_gain_grad, conv_grad = lax.psum(
        (first_part, second_part, kernel_full), ("dp", "tensor")
    )
    return (
        output,
        input_grad,
        first_gain_grad,
        in_grad,
        conv_grad,
        out_grad,
        second_gain_grad,
        gate_up_grad,
        down_grad,
    )


def solution(mesh):
    in_specs = (
        P(("dp", "tensor"), None),
        P(),
        P(None, "dp", "tensor"),
        P(),
        P("tensor", "dp"),
        P(),
        P(None, "dp", "tensor"),
        P("tensor", "dp"),
        P(("dp", "tensor"), None),
        P(),
    )
    out_specs = (
        P(("dp", "tensor"), None),
        P(("dp", "tensor"), None),
        P(),
        P(None, "dp", "tensor"),
        P(),
        P("tensor", "dp"),
        P(),
        P(None, "dp", "tensor"),
        P("tensor", "dp"),
    )
    return jax.shard_map(shards, mesh=mesh, in_specs=in_specs, out_specs=out_specs, check_vma=False)
```

profile of v0, /device:TPU:0, one launch (start us, length us, event | category | flops | bytes accessed | tf_op | source)
XLA Modules:
  0.0 489.5 jit_solution(4341568830876603250)
XLA Ops:
  7.2 0.7 all-gather.4.cloned.1.call-update
  8.0 0.8 reduce-window.8
  8.8 0.1 convert_reduce_fusion
  8.9 11.7 %all_gather.30 = bf16[256,1024]{1,0:T(8,128)(2,1)S(1)} all-gather(bf16[256,128]{1,0:T(8,128)(2,1)} %param.14), channel_id=1, replica_groups=mesh['dp'=8,'tensor'=4] {'dp'}, dimensions={1}, use_global_device_ids=true | all-gather | bytes 589824 | tf_op jit(solution)/shard_map/all_gather | solution.py:74
  20.6 1.1 fusion.18
  21.8 1.0 fusion.15
  22.8 16.4 %all_gather.28 = bf16[256,1024]{1,0:T(8,128)(2,1)S(1)} all-gather(bf16[64,1024]{1,0:T(8,128)(2,1)S(1)} %fusion.15), channel_id=1, replica_groups=mesh['dp'=8,'tensor'=4] {'tensor'}, dimensions={0}, use_global_device_ids=true | all-gather | bytes 655360 | tf_op jit(solution)/shard_map/all_gather | solution.py:69
  39.2 0.1 fusion.25
  39.3 0.7 fusion.35
  39.9 2.0 convolution_bitcast_fusion.5
  42.0 1.3 collective-permute-start
  43.3 0.9 fusion.34
  44.2 0.9 multiply_convert_fusion.8
  45.1 1.3 fusion.37
  46.4 0.0 all-gather.6.cloned.1.call-start
  46.5 0.7 all-gather.6.cloned.1.call-update
  47.2 0.5 all-gather.8.cloned.1.call-update
  47.8 21.5 %all_gather.34 = bf16[256,1024]{1,0:T(8,128)(2,1)} all-gather(bf16[64,1024]{1,0:T(8,128)(2,1)S(1)} %copy-done.13), channel_id=1, replica_groups=mesh['dp'=8,'tensor'=4] {'tensor'}, dimensions={0}, use_global_device_ids=true | all-gather | bytes 655360 | tf_op jit(solution)/shard_map/all_gather | solution.py:115
  69.3 13.1 %reduce-scatter.9.cloned.1.call-done = f32[64,1024]{1,0:T(8,128)} async-done(((f32[256,1024]{1,0:T(8,128)}), f32[64,1024]{1,0:T(8,128)}) %reduce-scatter.9.cloned.1.call-update) | async-done | bytes 262160 | tf_op jit(solution)/shard_map/reduce_scatter | solution.py:92
  82.4 1.1 multiply_reduce_fusion.5
  83.5 0.1 multiply_convert_fusion.7
  83.6 16.7 %all_gather.31 = bf16[256,1024]{1,0:T(8,128)(2,1)} all-gather(bf16[64,1024]{1,0:T(8,128)(2,1)S(1)} %multiply_convert_fusion.7), channel_id=1, replica_groups=mesh['dp'=8,'tensor'=4] {'tensor'}, dimensions={0}, use_global_device_ids=true | all-gather | bytes 655360 | tf_op jit(solution)/shard_map/all_gather | solution.py:93
  100.3 22.1 %all-gather.6.cloned.1.call-done = bf16[2,1024,1152]{2,1,0:T(8,128)(2,1)} async-done(((bf16[2,128,1152]{2,1,0:T(8,128)(2,1)}), bf16[2,1024,1152]{2,1,0:T(8,128)(2,1)}) %all-gather.6.cloned.1.call-update) | async-done | bytes 4718608 | tf_op jit(solution)/shard_map/all_gather | solution.py:75
  122.4 3.9 convolution_bitcast_fusion.1
  126.2 27.4 %all-gather.8.cloned.1.call-done = bf16[1152,1024]{1,0:T(8,128)(2,1)} async-done(((bf16[1152,128]{1,0:T(8,128)(2,1)}), bf16[1152,1024]{1,0:T(8,128)(2,1)}) %all-gather.8.cloned.1.call-update) | async-done | bytes 2359312 | tf_op jit(solution)/shard_map/all_gather | solution.py:76
  153.6 4.1 fusion.3
  157.7 0.8 copy-done.18
  158.5 0.2 copy-done.20
  158.7 2.4 convolution_bitcast_fusion.4
  161.2 27.2 %reduce-scatter.13.cloned.1.call-done = f32[64,1024]{1,0:T(8,128)} async-done(((f32[256,1024]{1,0:T(8,128)}), f32[64,1024]{1,0:T(8,128)}) %reduce-scatter.13.cloned.1.call-update) | async-done | bytes 262160 | tf_op jit(solution)/shard_map/reduce_scatter | solution.py:129
  188.4 1.2 multiply_reduce_fusion
  189.6 0.5 copy-done.47
  190.1 1.1 fusion.32
  191.3 15.9 %all_gather.35 = bf16[256,1024]{1,0:T(8,128)(2,1)S(1)} all-gather(bf16[64,1024]{1,0:T(8,128)(2,1)S(1)} %fusion.32), channel_id=1, replica_groups=mesh['dp'=8,'tensor'=4] {'tensor'}, dimensions={0}, use_global_device_ids=true | all-gather | bytes 655360 | tf_op jit(solution)/shard_map/all_gather | solution.py:132
  207.2 0.3 fusion.38
  207.6 0.1 fusion.22
  207.7 1.4 collective-permute-start.1
  209.1 1.7 collective-permute-done.1
  210.9 0.8 multiply_reduce_fusion.3
  211.8 1.4 fusion
  213.3 0.0 reduce-scatter.11.cloned.1.call-start
  213.4 3.4 convolution_convert_fusion
  216.8 0.0 reduce-scatter.17.cloned.1.call-start
  216.9 2.3 convolution_bitcast_fusion.2
  219.2 0.0 reduce-scatter.21.cloned.1.call-start
  219.2 1.0 copy-done.3
  220.2 0.2 copy-done.19
  220.4 6.2 %convolution_bitcast_fusion = f32[2,1024,1152]{1,2,0:T(8,128)} fusion(bf16[1,256,1152]{2,1,0:T(8,128)(2,1)} %copy-done.20, bf16[1,256,1152]{2,1,0:T(8,128)(2,1)S(1)} %copy-done.19, bf16[256,1024]{1,0:T(8,128)(2,1)S(1)} %copy-done.3), kind=kOutput, calls=%fused_computation | convolution fusion | flops 1208549376 | bytes 11141120 | tf_op jit(solution)/shard_map/td,ktf->kdf/dot_general | solution.py:123
  226.6 0.0 reduce-scatter.19.cloned.1.call-start
  226.6 0.8 copy-done.16
  227.4 1.3 fusion.39
  228.8 0.0 reduce-scatter.23.cloned.1.call-start
  228.8 3.0 fusion.40
  231.9 0.6 copy-done.42
  232.6 1.5 reduce-scatter.15.cloned.1.call-done
  234.1 1.1 fusion.17
  235.2 39.3 %all-reduce = (f32[1024]{0:T(1024)}, f32[3,1024]{1,0:T(4,128)}, f32[1024]{0:T(1024)}) all-reduce(f32[1024]{0:T(1024)S(1)} %get-tuple-element.32, f32[3,1024]{1,0:T(4,128)S(1)} %maximum_dynamic-update-slice_fusion, f32[1024]{0:T(1024)S(1)} %get-tuple-element.30), channel_id=1, replica_groups=mesh['dp'=8,'tensor'=4] {'dp','tensor'}, use_global_device_ids=true, to_apply=%region_11.12 | all-reduce | flops 5120 | bytes 40960 | tf_op jit(solution)/shard_map/psum | solution.py:177
  274.6 1.9 fusion.14
  276.5 27.7 %reduce-scatter.17.cloned.1.call-done = f32[3,128,256]{1,2,0:T(8,128)} async-done(((f32[3,1024,256]{1,2,0:T(8,128)}), f32[3,128,256]{1,2,0:T(8,128)}) %reduce-scatter.17.cloned.1.call-update) | async-done | bytes 393232 | tf_op jit(solution)/shard_map/reduce_scatter | solution.py:172
  304.2 1.9 copy.25
  306.1 78.5 %reduce-scatter.21.cloned.1.call-done = f32[2,128,1152]{1,2,0:T(8,128)} async-done(((f32[2,1024,1152]{1,2,0:T(8,128)}), f32[2,128,1152]{1,2,0:T(8,128)}) %reduce-scatter.21.cloned.1.call-update) | async-done | bytes 1179664 | tf_op jit(solution)/shard_map/reduce_scatter | solution.py:174
  384.6 2.7 copy.26
  387.3 37.3 %reduce-scatter.19.cloned.1.call-done = f32[256,128]{1,0:T(8,128)} async-done(((f32[256,1024]{1,0:T(8,128)}), f32[256,128]{1,0:T(8,128)}) %reduce-scatter.19.cloned.1.call-update) | async-done | bytes 131088 | tf_op jit(solution)/shard_map/reduce_scatter | solution.py:173
  424.6 58.3 %reduce-scatter.23.cloned.1.call-done = f32[1152,128]{1,0:T(8,128)} async-done(((f32[1152,1024]{1,0:T(8,128)}), f32[1152,128]{1,0:T(8,128)}) %reduce-scatter.23.cloned.1.call-update) | async-done | bytes 589840 | tf_op jit(solution)/shard_map/reduce_scatter | solution.py:175
  (120 shorter events, 0.7 us)
Async XLA Ops:
  7.2 32.7 %all-gather.4.cloned.1.call-start = ((), (), s32[]{:S(2)}) async-start(), calls=%async_computation.8 | async-start | bytes 1769472 | tf_op jit(solution)/shard_map/all_gather | solution.py:73
  7.9 74.5 %reduce-scatter.9.cloned.1.call-start = ((), (), s32[]{:S(2)}) async-start(), calls=%async_computation.9 | async-start | bytes 1310720 | tf_op jit(solution)/shard_map/reduce_scatter | solution.py:92
  20.6 24.5 %copy-start.4 = (bf16[256,1024]{1,0:T(8,128)(2,1)}, bf16[256,1024]{1,0:T(8,128)(2,1)S(1)}, u32[]{:S(2)}) copy-start(bf16[256,1024]{1,0:T(8,128)(2,1)S(1)} %all_gather.30) | copy-start | bytes 1572868
  21.8 17.5 %copy-start.40 = (f32[64]{0:T(128)}, f32[64]{0:T(128)S(1)}, u32[]{:S(2)}) copy-start(f32[64]{0:T(128)S(1)} %add_rsqrt_fusion.1) | copy-start | bytes 772
  39.2 2.8 copy-start.6
  39.9 4.3 copy-start.33
  39.9 4.3 copy-start.35
  42.0 2.2 collective-permute-start
  44.2 0.9 copy-start.27
  44.2 0.9 copy-start.29
  44.2 0.9 copy-start.31
  45.1 2.1 copy-start.15
  45.1 2.7 copy-start.13
  46.4 36.0 %copy-start.8 = (bf16[64,1024]{1,0:T(8,128)(2,1)S(1)}, bf16[64,1024]{1,0:T(8,128)(2,1)}, u32[]{:S(2)}) copy-start(bf16[64,1024]{1,0:T(8,128)(2,1)} %param.10) | copy-start | bytes 393220
  46.4 37.1 %copy-start.25 = (f32[1024]{0:T(1024)S(1)}, f32[1024]{0:T(1024)}, u32[]{:S(2)}) copy-start(f32[1024]{0:T(1024)} %param.15) | copy-start | bytes 12292
  46.4 75.9 %all-gather.6.cloned.1.call-start = ((), (), s32[]{:S(2)}) async-start(), calls=%async_computation.10 | async-start | bytes 5308416 | tf_op jit(solution)/shard_map/all_gather | solution.py:75
  47.2 106.4 %all-gather.8.cloned.1.call-start = ((), (), s32[]{:S(2)}) async-start(), calls=%async_computation.11 | async-start | bytes 2654208 | tf_op jit(solution)/shard_map/all_gather | solution.py:76
  47.8 140.6 %reduce-scatter.13.cloned.1.call-start = ((), (), s32[]{:S(2)}) async-start(), calls=%async_computation.13 | async-start | bytes 1310720 | tf_op jit(solution)/shard_map/reduce_scatter | solution.py:129
  83.5 16.8 %copy-start.1 = (f32[64,1024]{1,0:T(8,128)}, f32[64,1024]{1,0:T(8,128)S(1)}, u32[]{:S(2)}) copy-start(f32[64,1024]{1,0:T(8,128)S(1)} %get-tuple-element.40) | copy-start | bytes 786436
  83.5 16.8 %copy-start.37 = (f32[64]{0:T(128)}, f32[64]{0:T(128)S(1)}, u32[]{:S(2)}) copy-start(f32[64]{0:T(128)S(1)} %add_rsqrt_fusion) | copy-start | bytes 772
  153.6 5.1 %copy-start = (bf16[2,1024,1152]{2,1,0:T(8,128)(2,1)S(1)}, bf16[2,1024,1152]{2,1,0:T(8,128)(2,1)}, u32[]{:S(2)}) copy-start(bf16[2,1024,1152]{2,1,0:T(8,128)(2,1)} %all-gather.6.cloned.1.call-done) | copy-start | bytes 14155780
  157.7 0.8 copy-start.18
  157.7 1.0 copy-start.20
  158.7 29.7 %copy-start.2 = (f32[64,1024]{1,0:T(8,128)S(1)}, f32[64,1024]{1,0:T(8,128)}, u32[]{:S(2)}) copy-start(f32[64,1024]{1,0:T(8,128)} %copy-done.1) | copy-start | bytes 786436
  158.7 29.7 %copy-start.38 = (f32[64]{0:T(128)S(1)}, f32[64]{0:T(128)}, u32[]{:S(2)}) copy-start(f32[64]{0:T(128)} %copy-done.37) | copy-start | bytes 772
  161.1 29.0 %copy-start.14 = (bf16[64,1024]{1,0:T(8,128)(2,1)S(1)}, bf16[64,1024]{1,0:T(8,128)(2,1)}, u32[]{:S(2)}) copy-start(bf16[64,1024]{1,0:T(8,128)(2,1)} %param.18) | copy-start | bytes 393220
  161.1 46.1 %copy-start.5 = (bf16[256,1024]{1,0:T(8,128)(2,1)S(1)}, bf16[256,1024]{1,0:T(8,128)(2,1)}, u32[]{:S(2)}) copy-start(bf16[256,1024]{1,0:T(8,128)(2,1)} %copy-done.4) | copy-start | bytes 1572868
  161.1 46.4 %copy-start.17 = (f32[256,256]{1,0:T(8,128)S(1)}, f32[256,256]{1,0:T(8,128)}, u32[]{:S(2)}) copy-start(f32[256,256]{1,0:T(8,128)} %get-tuple-element.42) | copy-start | bytes 786436
  161.1 73.0 %reduce-scatter.15.cloned.1.call-start = ((), (), s32[]{:S(2)}) async-start(), calls=%async_computation.14 | async-start | bytes 655360 | tf_op jit(solution)/shard_map/reduce_scatter | solution.py:166
  189.6 0.5 copy-start.47
  191.2 19.6 %copy-start.28 = (f32[1,256]{1,0:T(1,128)S(1)}, f32[1,256]{1,0:T(1,128)}, u32[]{:S(2)}) copy-start(f32[1,256]{1,0:T(1,128)} %copy-done.27) | copy-start | bytes 3076
  191.2 19.6 %copy-start.30 = (f32[1,256]{1,0:T(1,128)S(1)}, f32[1,256]{1,0:T(1,128)}, u32[]{:S(2)}) copy-start(f32[1,256]{1,0:T(1,128)} %copy-done.29) | copy-start | bytes 3076
  191.2 19.6 %copy-start.32 = (f32[1,256]{1,0:T(1,128)S(1)}, f32[1,256]{1,0:T(1,128)}, u32[]{:S(2)}) copy-start(f32[1,256]{1,0:T(1,128)} %copy-done.31) | copy-start | bytes 3076
  191.2 19.6 %copy-start.34 = (f32[256]{0:T(256)S(1)}, f32[256]{0:T(256)}, u32[]{:S(2)}) copy-start(f32[256]{0:T(256)} %copy-done.33) | copy-start | bytes 3076
  191.2 19.6 %copy-start.36 = (f32[256]{0:T(256)S(1)}, f32[256]{0:T(256)}, u32[]{:S(2)}) copy-start(f32[256]{0:T(256)} %copy-done.35) | copy-start | bytes 3076
  191.3 19.6 %copy-start.45 = (f32[256]{0:T(256)S(1)}, f32[256]{0:T(256)}, u32[]{:S(2)}) copy-start(f32[256]{0:T(256)} %get-tuple-element.57) | copy-start | bytes 3076
  191.3 19.6 %copy-start.46 = (f32[256]{0:T(256)S(1)}, f32[256]{0:T(256)}, u32[]{:S(2)}) copy-start(f32[256]{0:T(256)} %get-tuple-element.62) | copy-start | bytes 3076
  207.6 4.2 copy-start.23
  207.7 4.2 copy-start.11
  207.7 3.2 collective-permute-start.1
  211.8 1.5 copy-start.21
  211.8 1.5 copy-start.12
  213.3 61.3 %reduce-scatter.11.cloned.1.call-start = ((), (), s32[]{:S(2)}) async-start(), calls=%async_computation.12 | async-start | bytes 655360 | tf_op jit(solution)/shard_map/reduce_scatter | solution.py:105
  213.3 3.5 copy-start.7
  213.3 3.5 copy-start.22
  213.4 3.5 copy-start.24
  216.8 87.4 %reduce-scatter.17.cloned.1.call-start = ((), (), s32[]{:S(2)}) async-start(), calls=%async_computation.15 | async-start | bytes 3538944 | tf_op jit(solution)/shard_map/reduce_scatter | solution.py:172
  219.1 1.0 copy-start.3
  219.1 1.2 copy-start.19
  219.2 165.5 %reduce-scatter.21.cloned.1.call-start = ((), (), s32[]{:S(2)}) async-start(), calls=%async_computation.17 | async-start | bytes 10616832 | tf_op jit(solution)/shard_map/reduce_scatter | solution.py:174
  226.5 0.9 copy-start.16
  226.6 2.3 copy-start.10
  226.6 198.1 %reduce-scatter.19.cloned.1.call-start = ((), (), s32[]{:S(2)}) async-start(), calls=%async_computation.16 | async-start | bytes 1179648 | tf_op jit(solution)/shard_map/reduce_scatter | solution.py:173
  228.8 254.2 %reduce-scatter.23.cloned.1.call-start = ((), (), s32[]{:S(2)}) async-start(), calls=%async_computation.18 | async-start | bytes 5308416 | tf_op jit(solution)/shard_map/reduce_scatter | solution.py:175
  231.9 0.7 copy-start.42
  231.9 0.7 copy-start.43
  231.9 0.7 copy-start.44
  231.9 2.2 copy-start.26
  231.9 2.2 copy-start.41
  231.9 42.7 %copy-start.9 = (f32[64,1024]{1,0:T(8,128)S(1)}, f32[64,1024]{1,0:T(8,128)}, u32[]{:S(2)}) copy-start(f32[64,1024]{1,0:T(8,128)} %reduce-scatter.13.cloned.1.call-done) | copy-start | bytes 786436
  231.9 42.7 %copy-start.39 = (f32[64]{0:T(128)S(1)}, f32[64]{0:T(128)}, u32[]{:S(2)}) copy-start(f32[64]{0:T(128)} %copy-done.37) | copy-start | bytes 772
  231.9 42.7 %copy-start.48 = (f32[64]{0:T(128)S(1)}, f32[64]{0:T(128)}, u32[]{:S(2)}) copy-start(f32[64]{0:T(128)} %copy-done.47) | copy-start | bytes 772
Sparse Core Ops, SparseCore 0:
  9.9 28.3 all-gather.3
  46.6 35.7 reduce-scatter.8
  84.4 37.8 all-gather.5
  124.2 29.3 all-gather.7
  161.2 27.1 reduce-scatter.12
  213.4 20.6 reduce-scatter.14
  236.4 19.9 reduce-scatter.10
  259.8 44.4 reduce-scatter.16
  308.1 76.4 reduce-scatter.20
  388.6 36.0 reduce-scatter.18
  429.0 53.8 reduce-scatter.22
where the time goes:
time: 490 us; the launch traced here: 489 us
  waiting for transfers between devices  297 us (61%)
  blocking collectives  121 us (25%)
  matrix products  31.5 us (6%)
  between operations  14.5 us (3%)
  other arithmetic  11.5 us (2%)
  local copies, waits for them, and re-layouts  10.4 us (2%)
    reduce_scatter x1, waiting for transfers between devices, shards(): lax.psum_scatter(gate_up_part, 'dp', scatter_dimension=1, tiled=True)  78.5 us
    reduce_scatter x1, waiting for transfers between devices, shards(): lax.psum_scatter(down_part, 'dp', scatter_dimension=1, tiled=True)  58.3 us
    psum x1, blocking collectives, shards(): lax.psum((first_part, second_part, kernel_full), ('dp', 'tensor'))  39.3 us
    reduce_scatter x1, waiting for transfers between devices, shards(): lax.psum_scatter(out_part, 'dp', scatter_dimension=1, tiled=True)  37.3 us
    reduce_scatter x1, waiting for transfers between devices, shards(): lax.psum_scatter(in_part, 'dp', scatter_dimension=1, tiled=True)  27.7 us
    all_gather x1, waiting for transfers between devices, shards(): lax.all_gather(down_weight, 'dp', axis=1, tiled=True)  27.4 us
    reduce_scatter x1, waiting for transfers between devices, shards(): lax.psum_scatter(hidden_back, 'tensor', scatter_dimension=0, tiled=True)  27.2 us
    all_gather x1, waiting for transfers between devices, shards(): lax.all_gather(gate_up_weight, 'dp', axis=1, tiled=True)  22.1 us
  transfers between devices with their start and end apart: 13, of which 10 were waited for; matrix products, arithmetic and copies ran while one was open for 7% of the time, Pallas kernels for 0%

commit v1 on v0

v1 whole, which is shorter than its diff:
```python
import jax
import jax.numpy as jnp
from jax import lax
from jax.sharding import PartitionSpec as P

EPS = 1e-05


def passed_along(block, axis, distance):
    devices = range(lax.axis_size(axis))
    route = [(i - distance, i) for i in devices if i - distance in devices]
    return lax.ppermute(block, axis, route)


def rms_norm(values, gain):
    return values * lax.rsqrt(jnp.mean(values * values, axis=-1, keepdims=True) + EPS) * gain


def rms_back(values, gain, grad_out):
    scale = lax.rsqrt(jnp.mean(values * values, axis=-1, keepdims=True) + EPS)
    normal = values * scale
    weighted = gain * grad_out
    grad_in = scale * (weighted - normal * jnp.mean(normal * weighted, axis=-1, keepdims=True))
    return (grad_in, jnp.sum(normal * grad_out, axis=0))


def times_trans(left, right):
    return lax.dot_general(
        left, right, (((1,), (1,)), ((), ())), preferred_element_type=jnp.float32
    )


def trans_times(left, right):
    return lax.dot_general(
        left, right, (((0,), (0,)), ((), ())), preferred_element_type=jnp.float32
    )


def swapped(block, axis, mask):
    devices = range(lax.axis_size(axis))
    return lax.ppermute(block, axis, [(i, i ^ mask) for i in devices])


def xor_order(blocks, index):
    bit = 1
    while bit < len(blocks):
        flag = (index & bit) > 0
        blocks = [jnp.where(flag, blocks[j ^ bit], blocks[j]) for j in range(len(blocks))]
        bit *= 2
    return blocks


def order_of(count):
    return list(range(0, count, 2)) + list(range(1, count, 2))


def to_relative(values):
    count = lax.axis_size("dp")
    blocks = xor_order(jnp.split(values, count, axis=-1), lax.axis_index("dp"))
    return jnp.concatenate([blocks[j] for j in order_of(count)], axis=-1)


def to_absolute(values):
    count = lax.axis_size("dp")
    places = jnp.split(values, count, axis=-1)
    blocks = [None] * count
    for place, j in enumerate(order_of(count)):
        blocks[j] = places[place]
    return jnp.concatenate(xor_order(blocks, lax.axis_index("dp")), axis=-1)


def gather_weight(shard, axis, cut):
    count = lax.axis_size("dp")
    if count == 8:
        over_x = swapped(shard, "dp", 2)
        over_y = swapped(shard, "dp", 4)
        first, _ = jnp.split(over_x, 2, axis=cut)
        _, second = jnp.split(over_y, 2, axis=cut)
        corner = jnp.concatenate(
            [swapped(first, "dp", 4), swapped(second, "dp", 2)], axis=cut
        )
        near = jnp.concatenate([shard, over_x, over_y, corner], axis=axis)
    else:
        near = shard
        bit = 2
        while bit < count:
            near = jnp.concatenate([near, swapped(near, "dp", bit)], axis=axis)
            bit *= 2
    return near, swapped(near, "dp", 1)


def wide(values):
    return values.astype(jnp.float32)


def narrow(values):
    return values.astype(jnp.bfloat16)


def scatter_weight(near, far, axis, cut):
    count = lax.axis_size("dp")
    total = wide(near) + wide(swapped(narrow(far), "dp", 1))
    if count == 8:
        own, for_x, for_y, corner = jnp.split(total, 4, axis=axis)
        first, second = jnp.split(narrow(corner), 2, axis=cut)
        got_first = wide(swapped(first, "dp", 2))
        got_second = wide(swapped(second, "dp", 4))
        y_first, y_second = jnp.split(for_y, 2, axis=cut)
        x_first, x_second = jnp.split(for_x, 2, axis=cut)
        for_y = jnp.concatenate([narrow(y_first + got_first), narrow(y_second)], axis=cut)
        for_x = jnp.concatenate([narrow(x_first), narrow(x_second + got_second)], axis=cut)
        return own + wide(swapped(for_x, "dp", 2)) + wide(swapped(for_y, "dp", 4))
    bit = count // 2
    while bit > 1:
        keep, send = jnp.split(total, 2, axis=axis)
        total = keep + wide(swapped(narrow(send), "dp", bit))
        bit //= 2
    return total


def gather_rows(rows):
    return [rows] + [swapped(rows, "tensor", j) for j in range(1, lax.axis_size("tensor"))]


def scatter_rows(blocks):
    total = blocks[0]
    for j in range(1, len(blocks)):
        total = total + wide(swapped(narrow(blocks[j]), "tensor", j))
    return total


def in_token_order(blocks):
    return jnp.concatenate(xor_order(blocks, lax.axis_index("tensor")), axis=0)


def for_owners(rows):
    blocks = jnp.split(rows, lax.axis_size("tensor"), axis=0)
    return xor_order(blocks, lax.axis_index("tensor"))


def summed_over(values, axis):
    count = lax.axis_size(axis)
    if count <= 8:
        blocks = [values] + [swapped(values, axis, j) for j in range(1, count)]
        blocks = xor_order(blocks, lax.axis_index(axis))
        return sum(blocks[1:], blocks[0])
    return lax.psum(values, axis)


def dot(left, right):
    return jnp.dot(left, right, preferred_element_type=jnp.float32)


def halves(values):
    return jnp.split(values, 2, axis=-1)


def shards(
    inputs,
    first_gain,
    entry_projection_weight,
    conv_weight,
    out_weight,
    second_gain,
    gate_up_weight,
    down_weight,
    cotangent,
    lengths,
):
    own_rows = inputs.shape[0]
    group_rows = own_rows * lax.axis_size("tensor")
    channels = entry_projection_weight.shape[2]
    column = lax.axis_index("tensor") * channels
    start = lax.axis_index("dp") * group_rows
    ends = jnp.sum(
        jnp.where(
            jnp.arange(lengths.shape[0])[:, None] >= jnp.arange(lengths.shape[0])[None, :],
            lengths[None, :],
            0,
        ),
        axis=1,
    )
    places = start - 2 + jnp.arange(group_rows + 4, dtype=jnp.int32)
    segment = jnp.sum((places[:, None] >= ends[None, :]).astype(jnp.int32), axis=1)
    first_all = jnp.logical_and(segment[2:] == segment[1:-1], places[2:] >= 1).astype(jnp.float32)[
        :, None
    ]
    second_all = jnp.logical_and(segment[2:] == segment[:-2], places[2:] >= 2).astype(jnp.float32)[
        :, None
    ]
    first_keep = first_all[:group_rows]
    second_keep = second_all[:group_rows]
    kernel = lax.dynamic_slice_in_dim(conv_weight, column, channels, 1)
    residual = wide(to_relative(inputs))
    first_gain = to_relative(first_gain)
    second_gain = to_relative(second_gain)
    cotangent = to_relative(cotangent)

    normed = in_token_order(gather_rows(narrow(rms_norm(residual, first_gain))))
    in_near, in_far = gather_weight(entry_projection_weight, 1, 2)
    out_near, out_far = gather_weight(out_weight, 1, 0)
    gate_up_near, gate_up_far = gather_weight(gate_up_weight, 1, 0)
    down_near, down_far = gather_weight(down_weight, 1, 0)
    grad_rows = jnp.concatenate(gather_rows(cotangent), axis=0)

    normed_near, normed_far = halves(normed)
    projected = [dot(normed_near, in_near[k]) + dot(normed_far, in_far[k]) for k in range(3)]
    input_gate_value, c_value, v_value = projected
    product = narrow(input_gate_value * v_value)
    before = passed_along(product[-2:], "dp", 1)
    extended = wide(jnp.concatenate([before, product], axis=0))
    mixed = (
        kernel[2] * extended[2:]
        + kernel[1] * first_keep * extended[1:-1]
        + kernel[0] * second_keep * extended[:-2]
    )
    gated = narrow(c_value * mixed)
    mixer_part = jnp.concatenate([dot(gated, out_near), dot(gated, out_far)], axis=1)
    middle = residual + scatter_rows(for_owners(mixer_part))
    hidden_in = jnp.concatenate(
        gather_rows(narrow(rms_norm(middle, second_gain))), axis=0
    )
    hidden_near, hidden_far = halves(hidden_in)
    gate_value = dot(hidden_near, gate_up_near[0]) + dot(hidden_far, gate_up_far[0])
    up_value = dot(hidden_near, gate_up_near[1]) + dot(hidden_far, gate_up_far[1])
    sigmoid = jax.nn.sigmoid(gate_value)
    swish = gate_value * sigmoid
    hidden = narrow(swish * up_value)
    grad_near, grad_far = halves(grad_rows)
    down_part_far = narrow(trans_times(hidden, grad_far))
    down_part_near = narrow(trans_times(hidden, grad_near))
    grad_hidden = times_trans(grad_near, down_near) + times_trans(grad_far, down_far)
    grad_gate = narrow(grad_hidden * up_value * sigmoid * (1.0 + gate_value * (1.0 - sigmoid)))
    grad_up = narrow(grad_hidden * swish)
    hidden_back = jnp.concatenate(
        [
            times_trans(grad_gate, half[0]) + times_trans(grad_up, half[1])
            for half in (gate_up_near, gate_up_far)
        ],
        axis=1,
    )
    grad_hin = scatter_rows(jnp.split(hidden_back, lax.axis_size("tensor"), axis=0))
    gate_up_part_far = jnp.stack(
        [narrow(trans_times(hidden_far, grad)) for grad in (grad_gate, grad_up)]
    )
    gate_up_part_near = jnp.stack(
        [narrow(trans_times(hidden_near, grad)) for grad in (grad_gate, grad_up)]
    )
    ffn_part = jnp.concatenate([dot(hidden, down_near), dot(hidden, down_far)], axis=1)
    output = narrow(
        middle + scatter_rows(jnp.split(ffn_part, lax.axis_size("tensor"), axis=0))
    )
    second_back, second_part = rms_back(middle, second_gain, grad_hin)
    grad_middle = wide(cotangent) + second_back
    branch_rows = in_token_order(gather_rows(narrow(grad_middle)))
    branch_near, branch_far = halves(branch_rows)
    grad_gated = times_trans(branch_near, out_near) + times_trans(branch_far, out_far)
    out_part_far = narrow(trans_times(gated, branch_far))
    out_part_near = narrow(trans_times(gated, branch_near))
    output_gate_gradient = narrow(grad_gated * mixed)
    grad_mixed = narrow(grad_gated * c_value)
    after = passed_along(grad_mixed[:2], "dp", -1)
    grad_ext = wide(jnp.concatenate([grad_mixed, after], axis=0))
    mixed_wide = grad_ext[:-2]
    kernel_part = jnp.stack(
        [
            jnp.sum(second_keep * extended[:-2] * mixed_wide, axis=0),
            jnp.sum(first_keep * extended[1:-1] * mixed_wide, axis=0),
            jnp.sum(extended[2:] * mixed_wide, axis=0),
        ]
    )
    kernel_full = lax.dynamic_update_slice_in_dim(
        jnp.zeros(conv_weight.shape, jnp.float32), kernel_part, column, 1
    )
    elementwise_product_gradient = (
        kernel[2] * grad_ext[:-2]
        + kernel[1] * first_all[1:-1] * grad_ext[1:-1]
        + kernel[0] * second_all[2:] * grad_ext[2:]
    )
    input_gate_gradient = narrow(elementwise_product_gradient * v_value)
    value_branch_gradient = narrow(elementwise_product_gradient * input_gate_value)
    grads = [input_gate_gradient, output_gate_gradient, value_branch_gradient]
    in_part_far = jnp.stack([narrow(trans_times(normed_far, grad)) for grad in grads])
    in_part_near = jnp.stack([narrow(trans_times(normed_near, grad)) for grad in grads])
    normed_back = jnp.concatenate(
        [
            sum(times_trans(grads[k], half[k]) for k in range(3))
            for half in (in_near, in_far)
        ],
        axis=1,
    )
    grad_normed = scatter_rows(for_owners(normed_back))
    first_back, first_part = rms_back(residual, first_gain, grad_normed)
    input_grad = grad_middle + first_back
    down_grad = scatter_weight(down_part_near, down_part_far, 1, 0)
    gate_up_grad = scatter_weight(gate_up_part_near, gate_up_part_far, 1, 0)
    out_grad = scatter_weight(out_part_near, out_part_far, 1, 0)
    in_grad = scatter_weight(in_part_near, in_part_far, 1, 2)
    small = jnp.concatenate(
        [to_absolute(first_part)[None], to_absolute(second_part)[None], kernel_full], axis=0
    )
    small = summed_over(summed_over(small, "tensor"), "dp")
    return (
        to_absolute(output),
        to_absolute(input_grad),
        small[0],
        in_grad,
        small[2:],
        out_grad,
        small[1],
        gate_up_grad,
        down_grad,
    )


def solution(mesh):
    in_specs = (
        P(("dp", "tensor"), None),
        P(),
        P(None, "dp", "tensor"),
        P(),
        P("tensor", "dp"),
        P(),
        P(None, "dp", "tensor"),
        P("tensor", "dp"),
        P(("dp", "tensor"), None),
        P(),
    )
    out_specs = (
        P(("dp", "tensor"), None),
        P(("dp", "tensor"), None),
        P(),
        P(None, "dp", "tensor"),
        P(),
        P("tensor", "dp"),
        P(),
        P(None, "dp", "tensor"),
        P("tensor", "dp"),
    )
    return jax.shard_map(shards, mesh=mesh, in_specs=in_specs, out_specs=out_specs, check_vma=False)
```

time: 490 us -> 261 us (0.53)
  waiting for transfers between devices: 297 us -> 112 us
  blocking collectives: 121 us -> 0 us
  starting transfers between devices: 3.16 us -> 84.7 us
  other arithmetic: 11.5 us -> 25.1 us
  between operations: 14.5 us -> 2.49 us
    reduce_scatter x8 -> x0, waiting for transfers between devices: 244 us -> none  [the longest x1 78.5 us: shards(): lax.psum_scatter(gate_up_part, 'dp', scatter_dimension=1, tiled=True)]
    ppermute x0 -> x74, waiting for transfers between devices: none -> 112 us  [swapped(): return lax.ppermute(block, axis, [(i, i ^ mask) for i in devices])]
    all_gather x5 -> x0, blocking collectives: 82.2 us -> none  [the longest x1 21.5 us: shards(): grad_rows = lax.all_gather(cotangent, 'tensor', axis=0, tiled=True)]
    ppermute x0 -> x74, starting transfers between devices: none -> 81.5 us  [swapped(): return lax.ppermute(block, axis, [(i, i ^ mask) for i in devices])]
    all_gather x3 -> x0, waiting for transfers between devices: 49.5 us -> none  [the longest x1 27.4 us: shards(): lax.all_gather(down_weight, 'dp', axis=1, tiled=True)]
    psum x1 -> x0, blocking collectives: 39.3 us -> none  [shards(): lax.psum((first_part, second_part, kernel_full), ('dp', 'tensor'))]
    concatenate x0 -> x25, other arithmetic: none -> 10.2 us  [the longest x4 4.53 us: gather_weight(): near = jnp.concatenate([shard, over_x, over_y, corner], axis=axis)]
    dot_general x8 -> x14, matrix products: 22.8 us -> 13.2 us  [dot(): return jnp.dot(left, right, preferred_element_type=jnp.float32)]
  transfers between devices with their start and end apart: 13 -> 76, of which waited for: 10 -> 39; matrix products, arithmetic and copies ran while one was open for 7% -> 14% of each run, Pallas kernels for 0% -> 0%
where the time goes in v1:
time: 261 us; the launch traced here: 260 us
  waiting for transfers between devices  112 us (43%)
  starting transfers between devices  84.7 us (32%)
  matrix products  30.2 us (12%)
  other arithmetic  25.1 us (10%)
  local copies, waits for them, and re-layouts  5.61 us (2%)
    ppermute x74, waiting for transfers between devices, swapped(): return lax.ppermute(block, axis, [(i, i ^ mask) for i in devices])  112 us
    ppermute x74, starting transfers between devices, swapped(): return lax.ppermute(block, axis, [(i, i ^ mask) for i in devices])  81.5 us
    dot_general x14, matrix products, dot(): return jnp.dot(left, right, preferred_element_type=jnp.float32)  13.2 us
    dot_general x14, matrix products, times_trans(): lax.dot_general(left, right, (((1,), (1,)), ((), ())), preferred_element_...  11.7 us
    add x4, other arithmetic, scatter_weight(): return own + wide(swapped(for_x, 'dp', 2)) + wide(swapped(for_y, 'dp', 4))  5.3 us
    dot_general x14, matrix products, trans_times(): lax.dot_general(left, right, (((0,), (0,)), ((), ())), preferred_element_...  5.29 us
  transfers between devices with their start and end apart: 76, of which 39 were waited for; matrix products, arithmetic and copies ran while one was open for 14% of the time, Pallas kernels for 0%

profile of v1, /device:TPU:0, one launch (start us, length us, event | category | flops | bytes accessed | tf_op | source)
XLA Modules:
  0.0 260.3 jit_solution(15579662177786973815)
XLA Ops:
  5.0 5.1 %collective-permute-start = (bf16[64,1024]{1,0:T(8,128)(2,1)S(1)}, bf16[64,1024]{1,0:T(8,128)(2,1)S(1)}, u32[]{:S(2)}, u32[]{:S(2)}) collective-permute-start(bf16[64,1024]{1,0:T(8,128)(2,1)S(1)} %fusion.32), channel_id=1, source_target_pairs={{0,3},{1,2},{2,1},{3,0},{4,7},{5,6},{6,5},{7,4},{8,11},{9,10},{10,... | collective-permute-start | bytes 393224 | tf_op jit(solution)/shard_map/ppermute | solution.py:41
  10.8 1.7 collective-permute-start.10
  21.1 1.7 collective-permute-start.3
  23.2 1.5 collective-permute-start.25
  25.5 2.1 collective-permute-done.4
  29.0 1.5 collective-permute-start.5
  30.6 3.8 %collective-permute-done.6 = bf16[3,128,128]{2,1,0:T(8,128)(2,1)S(1)} collective-permute-done((bf16[3,128,128]{2,1,0:T(8,128)(2,1)S(1)}, bf16[3,128,128]{2,1,0:T(8,128)(2,1)S(1)}, u32[]{:S(2)}, u32[]{:S(2)}) %collective-permute-start.6) | collective-permute-done | bytes 98336 | tf_op jit(solution)/shard_map/ppermute | solution.py:41
  34.4 1.7 collective-permute-start.20
  36.1 9.6 %collective-permute-done.5 = bf16[3,128,128]{2,1,0:T(8,128)(2,1)S(1)} collective-permute-done((bf16[3,128,128]{2,1,0:T(8,128)(2,1)S(1)}, bf16[3,128,128]{2,1,0:T(8,128)(2,1)S(1)}, u32[]{:S(2)}, u32[]{:S(2)}) %collective-permute-start.5) | collective-permute-done | bytes 98336 | tf_op jit(solution)/shard_map/ppermute | solution.py:41
  48.8 3.9 %collective-permute-done.28 = bf16[576,128]{1,0:T(8,128)(2,1)S(1)} collective-permute-done((bf16[576,128]{1,0:T(8,128)(2,1)S(1)}, bf16[576,128]{1,0:T(8,128)(2,1)S(1)}, u32[]{:S(2)}, u32[]{:S(2)}) %collective-permute-start.28) | collective-permute-done | bytes 147488 | tf_op jit(solution)/shard_map/ppermute | solution.py:41
  56.9 1.7 collective-permute-start.8
  58.6 4.6 %collective-permute-done.23 = bf16[1,128,1152]{2,1,0:T(8,128)(2,1)S(1)} collective-permute-done((bf16[1,128,1152]{2,1,0:T(8,128)(2,1)S(1)}, bf16[1,128,1152]{2,1,0:T(8,128)(2,1)S(1)}, u32[]{:S(2)}, u32[]{:S(2)}) %collective-permute-start.23) | collective-permute-done | bytes 294944 | tf_op jit(solution)/shard_map/ppermute | solution.py:41
  64.1 4.3 %maximum_maximum_fusion = bf16[2,512,1152]{2,1,0:T(8,128)(2,1)} fusion(bf16[1,128,1152]{2,1,0:T(8,128)(2,1)S(1)} %collective-permute-done.23, bf16[1,128,1152]{2,1,0:T(8,128)(2,1)S(1)} %collective-permute-done.22, bf16[2,128,1152]{2,1,0:T(8,128)(2,1)S(1)} %collective-permute-done.21, bf16[2,128,1152]{2,1,0:T(8,128)(2,1)S(1)} %collective-permute-done.20, ...), kind=kLoop, calls=%fused_computation.16 | loop fusion | flops 11796480 | bytes 4718592 | tf_op jit(solution)/shard_map/concatenate | solution.py:82
  70.5 3.5 %collective-permute-start.16 = (bf16[64,1024]{1,0:T(8,128)(2,1)S(1)}, bf16[64,1024]{1,0:T(8,128)(2,1)S(1)}, u32[]{:S(2)}, u32[]{:S(2)}) collective-permute-start(bf16[64,1024]{1,0:T(8,128)(2,1)S(1)} %get-tuple-element.156), channel_id=1, source_target_pairs={{0,3},{1,2},{2,1},{3,0},{4,7},{5,6},{6,5},{7,4},{8,11},{9,10},{10,... | collective-permute-start | bytes 393224 | tf_op jit(solution)/shard_map/ppermute | solution.py:41
  74.9 3.8 %collective-permute-done.16 = bf16[64,1024]{1,0:T(8,128)(2,1)S(1)} collective-permute-done((bf16[64,1024]{1,0:T(8,128)(2,1)S(1)}, bf16[64,1024]{1,0:T(8,128)(2,1)S(1)}, u32[]{:S(2)}, u32[]{:S(2)}) %collective-permute-start.16) | collective-permute-done | bytes 131104 | tf_op jit(solution)/shard_map/ppermute | solution.py:41
  78.7 3.5 %collective-permute-start.35 = (bf16[64,1024]{1,0:T(8,128)(2,1)S(1)}, bf16[64,1024]{1,0:T(8,128)(2,1)}, u32[]{:S(2)}, u32[]{:S(2)}) collective-permute-start(bf16[64,1024]{1,0:T(8,128)(2,1)S(1)} %constant_dynamic-update-slice_fusion.18), channel_id=1, source_target_pairs={{0,3},{1,2},{2,1},{3,0},{4,7},{5,6},{6,5},{7,4},{8,11},{9,10},{10,... | collective-permute-start | bytes 393224 | tf_op jit(solution)/shard_map/ppermute | solution.py:41
  82.2 6.4 %collective-permute-done.15 = bf16[64,1024]{1,0:T(8,128)(2,1)S(1)} collective-permute-done((bf16[64,1024]{1,0:T(8,128)(2,1)S(1)}, bf16[64,1024]{1,0:T(8,128)(2,1)S(1)}, u32[]{:S(2)}, u32[]{:S(2)}) %collective-permute-start.15) | collective-permute-done | bytes 131104 | tf_op jit(solution)/shard_map/ppermute | solution.py:41
  88.6 3.2 %collective-permute-start.33 = (bf16[64,1024]{1,0:T(8,128)(2,1)S(1)}, bf16[64,1024]{1,0:T(8,128)(2,1)}, u32[]{:S(2)}, u32[]{:S(2)}) collective-permute-start(bf16[64,1024]{1,0:T(8,128)(2,1)S(1)} %constant_dynamic-update-slice_fusion.18), channel_id=1, source_target_pairs={{0,1},{1,0},{2,3},{3,2},{4,5},{5,4},{6,7},{7,6},{8,9},{9,8},{10,11... | collective-permute-start | bytes 393224 | tf_op jit(solution)/shard_map/ppermute | solution.py:41
  93.9 6.2 %collective-permute-done.34 = bf16[64,1024]{1,0:T(8,128)(2,1)} collective-permute-done((bf16[64,1024]{1,0:T(8,128)(2,1)S(1)}, bf16[64,1024]{1,0:T(8,128)(2,1)}, u32[]{:S(2)}, u32[]{:S(2)}) %collective-permute-start.34) | collective-permute-done | bytes 131104 | tf_op jit(solution)/shard_map/ppermute | solution.py:41
  100.2 2.9 %collective-permute-start.17 = (bf16[64,1024]{1,0:T(8,128)(2,1)}, bf16[64,1024]{1,0:T(8,128)(2,1)}, u32[]{:S(2)}, u32[]{:S(2)}) collective-permute-start(bf16[64,1024]{1,0:T(8,128)(2,1)} %multiply_convert_fusion.7), channel_id=1, source_target_pairs={{0,1},{1,0},{2,3},{3,2},{4,5},{5,4},{6,7},{7,6},{8,9},{9,8},{10,11... | collective-permute-start | bytes 393224 | tf_op jit(solution)/shard_map/ppermute | solution.py:41
  104.2 4.3 %collective-permute-done.18 = bf16[64,1024]{1,0:T(8,128)(2,1)} collective-permute-done((bf16[64,1024]{1,0:T(8,128)(2,1)}, bf16[64,1024]{1,0:T(8,128)(2,1)}, u32[]{:S(2)}, u32[]{:S(2)}) %collective-permute-start.18) | collective-permute-done | bytes 131104 | tf_op jit(solution)/shard_map/ppermute | solution.py:41
  109.8 1.8 fusion.71
  112.2 1.8 fusion.21
  114.0 1.8 convolution_add_fusion.1
  115.8 1.8 fusion.18
  117.6 2.3 multiply_convert_fusion.1
  119.9 1.8 fusion.19
  124.4 1.8 convolution_add_fusion.4
  126.2 1.8 fusion.20
  128.0 1.8 convolution_add_fusion.3
  129.9 2.1 collective-permute-start.38
  132.0 2.3 collective-permute-start.36
  134.4 1.8 fusion.130
  136.3 2.1 collective-permute-start.32
  139.2 9.3 %collective-permute-done.37 = bf16[64,1024]{1,0:T(8,128)(2,1)S(1)} collective-permute-done((bf16[64,1024]{1,0:T(8,128)(2,1)S(1)}, bf16[64,1024]{1,0:T(8,128)(2,1)S(1)}, u32[]{:S(2)}, u32[]{:S(2)}) %collective-permute-start.37) | collective-permute-done | bytes 131104 | tf_op jit(solution)/shard_map/ppermute | solution.py:41
  148.9 2.4 collective-permute-start.39
  151.2 2.1 collective-permute-start.41
  153.5 3.7 %collective-permute-done.39 = bf16[64,1024]{1,0:T(8,128)(2,1)S(1)} collective-permute-done((bf16[64,1024]{1,0:T(8,128)(2,1)S(1)}, bf16[64,1024]{1,0:T(8,128)(2,1)S(1)}, u32[]{:S(2)}, u32[]{:S(2)}) %collective-permute-start.39) | collective-permute-done | bytes 131104 | tf_op jit(solution)/shard_map/ppermute | solution.py:41
  157.2 7.9 %collective-permute-done.40 = bf16[64,1024]{1,0:T(8,128)(2,1)S(1)} collective-permute-done((bf16[64,1024]{1,0:T(8,128)(2,1)S(1)}, bf16[64,1024]{1,0:T(8,128)(2,1)S(1)}, u32[]{:S(2)}, u32[]{:S(2)}) %collective-permute-start.40) | collective-permute-done | bytes 131104 | tf_op jit(solution)/shard_map/ppermute | solution.py:41
  166.6 1.5 collective-permute-start.42
  172.7 2.4 collective-permute-start.45
  175.1 2.1 collective-permute-start.43
  177.3 3.2 %collective-permute-done.45 = bf16[64,1024]{1,0:T(8,128)(2,1)S(1)} collective-permute-done((bf16[64,1024]{1,0:T(8,128)(2,1)S(1)}, bf16[64,1024]{1,0:T(8,128)(2,1)S(1)}, u32[]{:S(2)}, u32[]{:S(2)}) %collective-permute-start.45) | collective-permute-done | bytes 131104 | tf_op jit(solution)/shard_map/ppermute | solution.py:41
  180.4 6.2 %collective-permute-done.44 = bf16[64,1024]{1,0:T(8,128)(2,1)S(1)} collective-permute-done((bf16[64,1024]{1,0:T(8,128)(2,1)S(1)}, bf16[64,1024]{1,0:T(8,128)(2,1)S(1)}, u32[]{:S(2)}, u32[]{:S(2)}) %collective-permute-start.44) | collective-permute-done | bytes 131104 | tf_op jit(solution)/shard_map/ppermute | solution.py:41
  187.2 2.9 %collective-permute-start.47 = (f32[5,1024]{1,0:T(8,128)S(1)}, f32[5,1024]{1,0:T(8,128)S(1)}, u32[]{:S(2)}, u32[]{:S(2)}) collective-permute-start(f32[5,1024]{1,0:T(8,128)S(1)} %pad_maximum_fusion.18), channel_id=1, source_target_pairs={{0,2},{1,3},{2,0},{3,1},{4,6},{5,7},{6,4},{7,5},{8,10},{9,11},{10,... | collective-permute-start | bytes 61448 | tf_op jit(solution)/shard_map/ppermute | solution.py:41
  192.4 3.4 %collective-permute-done.46 = f32[5,1024]{1,0:T(8,128)S(1)} collective-permute-done((f32[5,1024]{1,0:T(8,128)S(1)}, f32[5,1024]{1,0:T(8,128)S(1)}, u32[]{:S(2)}, u32[]{:S(2)}) %collective-permute-start.46) | collective-permute-done | bytes 20512 | tf_op jit(solution)/shard_map/ppermute | solution.py:41
  195.9 1.7 collective-permute-start.54
  203.2 1.6 collective-permute-done.50
  205.7 2.3 collective-permute-start.62
  209.9 2.0 collective-permute-done.64
  212.1 1.6 collective-permute-start.63
  214.9 1.9 collective-permute-done.65
  218.9 2.8 %collective-permute-done.59 = bf16[3,128,128]{1,2,0:T(8,128)(2,1)S(1)} collective-permute-done((bf16[3,128,128]{1,2,0:T(8,128)(2,1)S(1)}, bf16[3,128,128]{1,2,0:T(8,128)(2,1)S(1)}, u32[]{:S(2)}, u32[]{:S(2)}) %collective-permute-start.59) | collective-permute-done | bytes 98336 | tf_op jit(solution)/shard_map/ppermute | solution.py:41
  222.5 1.6 collective-permute-start.74
  224.7 1.9 collective-permute-start.58
  226.6 2.2 collective-permute-done.72
  229.6 2.3 collective-permute-start.67
  234.8 5.1 %collective-permute-done.67 = bf16[1,128,1152]{2,1,0:T(8,128)(2,1)S(1)} collective-permute-done((bf16[1,128,1152]{2,1,0:T(8,128)(2,1)S(1)}, bf16[1,128,1152]{2,1,0:T(8,128)(2,1)S(1)}, u32[]{:S(2)}, u32[]{:S(2)}) %collective-permute-start.67) | collective-permute-done | bytes 294944 | tf_op jit(solution)/shard_map/ppermute | solution.py:41
  240.2 1.7 collective-permute-done.69
  246.3 3.8 %collective-permute-done.73 = bf16[1152,128]{1,0:T(8,128)(2,1)} collective-permute-done((bf16[1152,128]{1,0:T(8,128)(2,1)}, bf16[1152,128]{1,0:T(8,128)(2,1)}, u32[]{:S(2)}, u32[]{:S(2)}) %collective-permute-start.73) | collective-permute-done | bytes 294944 | tf_op jit(solution)/shard_map/ppermute | solution.py:41
  250.2 2.0 fusion.22
  252.1 2.8 %collective-permute-done.70 = bf16[2,128,1152]{2,1,0:T(8,128)(2,1)S(1)} collective-permute-done((bf16[2,128,1152]{2,1,0:T(8,128)(2,1)}, bf16[2,128,1152]{2,1,0:T(8,128)(2,1)S(1)}, u32[]{:S(2)}, u32[]{:S(2)}) %collective-permute-start.70) | collective-permute-done | bytes 589856 | tf_op jit(solution)/shard_map/ppermute | solution.py:41
  254.9 2.8 %collective-permute-done.68 = bf16[2,128,1152]{2,1,0:T(8,128)(2,1)} collective-permute-done((bf16[2,128,1152]{2,1,0:T(8,128)(2,1)}, bf16[2,128,1152]{2,1,0:T(8,128)(2,1)}, u32[]{:S(2)}, u32[]{:S(2)}) %collective-permute-start.68) | collective-permute-done | bytes 589856 | tf_op jit(solution)/shard_map/ppermute | solution.py:41
  257.7 2.6 fusion.8
  (398 shorter events, 66.1 us)
Async XLA Ops:
  5.0 17.9 %collective-permute-start = (bf16[64,1024]{1,0:T(8,128)(2,1)S(1)}, bf16[64,1024]{1,0:T(8,128)(2,1)S(1)}, u32[]{:S(2)}, u32[]{:S(2)}) collective-permute-start(bf16[64,1024]{1,0:T(8,128)(2,1)S(1)} %fusion.32), channel_id=1, source_target_pairs={{0,3},{1,2},{2,1},{3,0},{4,7},{5,6},{6,5},{7,4},{8,11},{9,10},{10,... | collective-permute-start | bytes 393224 | tf_op jit(solution)/shard_map/ppermute | solution.py:41
  10.2 13.1 %collective-permute-start.1 = (bf16[64,1024]{1,0:T(8,128)(2,1)S(1)}, bf16[64,1024]{1,0:T(8,128)(2,1)S(1)}, u32[]{:S(2)}, u32[]{:S(2)}) collective-permute-start(bf16[64,1024]{1,0:T(8,128)(2,1)S(1)} %fusion.32), channel_id=1, source_target_pairs={{0,2},{1,3},{2,0},{3,1},{4,6},{5,7},{6,4},{7,5},{8,10},{9,11},{10,... | collective-permute-start | bytes 393224 | tf_op jit(solution)/shard_map/ppermute | solution.py:41
  10.2 14.6 %collective-permute-start.2 = (bf16[64,1024]{1,0:T(8,128)(2,1)S(1)}, bf16[64,1024]{1,0:T(8,128)(2,1)S(1)}, u32[]{:S(2)}, u32[]{:S(2)}) collective-permute-start(bf16[64,1024]{1,0:T(8,128)(2,1)S(1)} %fusion.32), channel_id=1, source_target_pairs={{0,1},{1,0},{2,3},{3,2},{4,5},{5,4},{6,7},{7,6},{8,9},{9,8},{10,11... | collective-permute-start | bytes 393224 | tf_op jit(solution)/shard_map/ppermute | solution.py:41
  10.8 4.5 %collective-permute-start.10 = (bf16[256,128]{1,0:T(8,128)(2,1)S(1)}, bf16[256,128]{1,0:T(8,128)(2,1)S(1)}, u32[]{:S(2)}, u32[]{:S(2)}) collective-permute-start(bf16[256,128]{1,0:T(8,128)(2,1)S(1)} %copy-done.18), channel_id=1, source_target_pairs={{0,16},{4,20},{8,24},{12,28},{16,0},{20,4},{24,8},{28,12},{1,17},{... | collective-permute-start | bytes 196616 | tf_op jit(solution)/shard_map/ppermute | solution.py:41
  19.8 7.9 %collective-permute-start.4 = (bf16[3,128,256]{2,1,0:T(8,128)(2,1)S(1)}, bf16[3,128,256]{2,1,0:T(8,128)(2,1)S(1)}, u32[]{:S(2)}, u32[]{:S(2)}) collective-permute-start(bf16[3,128,256]{2,1,0:T(8,128)(2,1)S(1)} %copy-done.11), channel_id=1, source_target_pairs={{0,16},{4,20},{8,24},{12,28},{16,0},{20,4},{24,8},{28,12},{1,17},{... | collective-permute-start | bytes 589832 | tf_op jit(solution)/shard_map/ppermute | solution.py:41
  21.1 7.8 %collective-permute-start.3 = (bf16[3,128,256]{2,1,0:T(8,128)(2,1)S(1)}, bf16[3,128,256]{2,1,0:T(8,128)(2,1)S(1)}, u32[]{:S(2)}, u32[]{:S(2)}) collective-permute-start(bf16[3,128,256]{2,1,0:T(8,128)(2,1)S(1)} %copy-done.11), channel_id=1, source_target_pairs={{0,8},{4,12},{8,0},{12,4},{16,24},{20,28},{24,16},{28,20},{1,9},{5... | collective-permute-start | bytes 589832 | tf_op jit(solution)/shard_map/ppermute | solution.py:41
  22.9 23.5 %collective-permute-start.26 = (bf16[1152,128]{1,0:T(8,128)(2,1)S(1)}, bf16[1152,128]{1,0:T(8,128)(2,1)S(1)}, u32[]{:S(2)}, u32[]{:S(2)}) collective-permute-start(bf16[1152,128]{1,0:T(8,128)(2,1)S(1)} %copy-done.9), channel_id=1, source_target_pairs={{0,16},{4,20},{8,24},{12,28},{16,0},{20,4},{24,8},{28,12},{1,17},{... | collective-permute-start | bytes 884744 | tf_op jit(solution)/shard_map/ppermute | solution.py:41
  23.2 24.1 %collective-permute-start.25 = (bf16[1152,128]{1,0:T(8,128)(2,1)S(1)}, bf16[1152,128]{1,0:T(8,128)(2,1)S(1)}, u32[]{:S(2)}, u32[]{:S(2)}) collective-permute-start(bf16[1152,128]{1,0:T(8,128)(2,1)S(1)} %copy-done.9), channel_id=1, source_target_pairs={{0,8},{4,12},{8,0},{12,4},{16,24},{20,28},{24,16},{28,20},{1,9},{5... | collective-permute-start | bytes 884744 | tf_op jit(solution)/shard_map/ppermute | solution.py:41
  24.8 28.9 %collective-permute-start.21 = (bf16[2,128,1152]{2,1,0:T(8,128)(2,1)}, bf16[2,128,1152]{2,1,0:T(8,128)(2,1)S(1)}, u32[]{:S(2)}, u32[]{:S(2)}) collective-permute-start(bf16[2,128,1152]{2,1,0:T(8,128)(2,1)} %param.16), channel_id=1, source_target_pairs={{0,16},{4,20},{8,24},{12,28},{16,0},{20,4},{24,8},{28,12},{1,17},{... | collective-permute-start | bytes 1769480 | tf_op jit(solution)/shard_map/ppermute | solution.py:41
  27.7 6.7 %collective-permute-start.6 = (bf16[3,128,128]{2,1,0:T(8,128)(2,1)S(1)}, bf16[3,128,128]{2,1,0:T(8,128)(2,1)S(1)}, u32[]{:S(2)}, u32[]{:S(2)}) collective-permute-start(bf16[3,128,128]{2,1,0:T(8,128)(2,1)S(1)} %split.528), channel_id=1, source_target_pairs={{0,8},{4,12},{8,0},{12,4},{16,24},{20,28},{24,16},{28,20},{1,9},{5... | collective-permute-start | bytes 294920 | tf_op jit(solution)/shard_map/ppermute | solution.py:41
  29.0 16.8 %collective-permute-start.5 = (bf16[3,128,128]{2,1,0:T(8,128)(2,1)S(1)}, bf16[3,128,128]{2,1,0:T(8,128)(2,1)S(1)}, u32[]{:S(2)}, u32[]{:S(2)}) collective-permute-start(bf16[3,128,128]{2,1,0:T(8,128)(2,1)S(1)} %split.527), channel_id=1, source_target_pairs={{0,16},{4,20},{8,24},{12,28},{16,0},{20,4},{24,8},{28,12},{1,17},{... | collective-permute-start | bytes 294920 | tf_op jit(solution)/shard_map/ppermute | solution.py:41
  34.4 20.5 %collective-permute-start.20 = (bf16[2,128,1152]{2,1,0:T(8,128)(2,1)}, bf16[2,128,1152]{2,1,0:T(8,128)(2,1)S(1)}, u32[]{:S(2)}, u32[]{:S(2)}) collective-permute-start(bf16[2,128,1152]{2,1,0:T(8,128)(2,1)} %param.16), channel_id=1, source_target_pairs={{0,8},{4,12},{8,0},{12,4},{16,24},{20,28},{24,16},{28,20},{1,9},{5... | collective-permute-start | bytes 1769480 | tf_op jit(solution)/shard_map/ppermute | solution.py:41
  45.9 9.8 %collective-permute-start.7 = (bf16[3,512,256]{2,1,0:T(8,128)(2,1)S(1)}, bf16[3,512,256]{2,1,0:T(8,128)(2,1)S(1)}, u32[]{:S(2)}, u32[]{:S(2)}) collective-permute-start(bf16[3,512,256]{2,1,0:T(8,128)(2,1)S(1)} %maximum_maximum_fusion.2), channel_id=1, source_target_pairs={{0,4},{4,0},{8,12},{12,8},{16,20},{20,16},{24,28},{28,24},{1,5},{5... | collective-permute-start | bytes 2359304 | tf_op jit(solution)/shard_map/ppermute | solution.py:41
  46.4 6.3 %collective-permute-start.28 = (bf16[576,128]{1,0:T(8,128)(2,1)S(1)}, bf16[576,128]{1,0:T(8,128)(2,1)S(1)}, u32[]{:S(2)}, u32[]{:S(2)}) collective-permute-start(bf16[576,128]{1,0:T(8,128)(2,1)S(1)} %split.543), channel_id=1, source_target_pairs={{0,8},{4,12},{8,0},{12,4},{16,24},{20,28},{24,16},{28,20},{1,9},{5... | collective-permute-start | bytes 442376 | tf_op jit(solution)/shard_map/ppermute | solution.py:41
  47.4 6.0 %collective-permute-start.27 = (bf16[576,128]{1,0:T(8,128)(2,1)S(1)}, bf16[576,128]{1,0:T(8,128)(2,1)S(1)}, u32[]{:S(2)}, u32[]{:S(2)}) collective-permute-start(bf16[576,128]{1,0:T(8,128)(2,1)S(1)} %split.542), channel_id=1, source_target_pairs={{0,16},{4,20},{8,24},{12,28},{16,0},{20,4},{24,8},{28,12},{1,17},{... | collective-permute-start | bytes 442376 | tf_op jit(solution)/shard_map/ppermute | solution.py:41
  52.8 16.9 %collective-permute-start.13 = (bf16[256,512]{1,0:T(8,128)(2,1)S(1)}, bf16[256,512]{1,0:T(8,128)(2,1)S(1)}, u32[]{:S(2)}, u32[]{:S(2)}) collective-permute-start(bf16[256,512]{1,0:T(8,128)(2,1)S(1)} %maximum_maximum_fusion.3), channel_id=1, source_target_pairs={{0,4},{4,0},{8,12},{12,8},{16,20},{20,16},{24,28},{28,24},{1,5},{5... | collective-permute-start | bytes 786440 | tf_op jit(solution)/shard_map/ppermute | solution.py:41
  53.5 56.3 %collective-permute-start.29 = (bf16[1152,512]{1,0:T(8,128)(2,1)S(1)}, bf16[1152,512]{1,0:T(8,128)(2,1)}, u32[]{:S(2)}, u32[]{:S(2)}) collective-permute-start(bf16[1152,512]{1,0:T(8,128)(2,1)S(1)} %maximum_maximum_fusion.1), channel_id=1, source_target_pairs={{0,4},{4,0},{8,12},{12,8},{16,20},{20,16},{24,28},{28,24},{1,5},{5... | collective-permute-start | bytes 3538952 | tf_op jit(solution)/shard_map/ppermute | solution.py:41
  53.7 9.5 %collective-permute-start.23 = (bf16[1,128,1152]{2,1,0:T(8,128)(2,1)S(1)}, bf16[1,128,1152]{2,1,0:T(8,128)(2,1)S(1)}, u32[]{:S(2)}, u32[]{:S(2)}) collective-permute-start(bf16[1,128,1152]{2,1,0:T(8,128)(2,1)S(1)} %split.540), channel_id=1, source_target_pairs={{0,8},{4,12},{8,0},{12,4},{16,24},{20,28},{24,16},{28,20},{1,9},{5... | collective-permute-start | bytes 884744 | tf_op jit(solution)/shard_map/ppermute | solution.py:41
  55.0 9.2 %collective-permute-start.22 = (bf16[1,128,1152]{2,1,0:T(8,128)(2,1)S(1)}, bf16[1,128,1152]{2,1,0:T(8,128)(2,1)S(1)}, u32[]{:S(2)}, u32[]{:S(2)}) collective-permute-start(bf16[1,128,1152]{2,1,0:T(8,128)(2,1)S(1)} %split.539), channel_id=1, source_target_pairs={{0,16},{4,20},{8,24},{12,28},{16,0},{20,4},{24,8},{28,12},{1,17},{... | collective-permute-start | bytes 884744 | tf_op jit(solution)/shard_map/ppermute | solution.py:41
  56.9 11.5 %collective-permute-start.8 = (bf16[2,256]{1,0:T(2,128)(2,1)S(1)}, bf16[2,256]{1,0:T(2,128)(2,1)S(1)}, u32[]{:S(2)}, u32[]{:S(2)}) collective-permute-start(bf16[2,256]{1,0:T(2,128)(2,1)S(1)} %slice.181), channel_id=1, source_target_pairs={{0,4},{4,8},{8,12},{12,16},{16,20},{20,24},{24,28},{1,5},{5,9},{9,... | collective-permute-start | bytes 3080 | tf_op jit(solution)/shard_map/ppermute | solution.py:12
  68.4 43.8 %collective-permute-start.24 = (bf16[2,512,1152]{2,1,0:T(8,128)(2,1)}, bf16[2,512,1152]{2,1,0:T(8,128)(2,1)}, u32[]{:S(2)}, u32[]{:S(2)}) collective-permute-start(bf16[2,512,1152]{2,1,0:T(8,128)(2,1)} %maximum_maximum_fusion), channel_id=1, source_target_pairs={{0,4},{4,0},{8,12},{12,8},{16,20},{20,16},{24,28},{28,24},{1,5},{5... | collective-permute-start | bytes 7077896 | tf_op jit(solution)/shard_map/ppermute | solution.py:41
  70.5 8.3 %collective-permute-start.16 = (bf16[64,1024]{1,0:T(8,128)(2,1)S(1)}, bf16[64,1024]{1,0:T(8,128)(2,1)S(1)}, u32[]{:S(2)}, u32[]{:S(2)}) collective-permute-start(bf16[64,1024]{1,0:T(8,128)(2,1)S(1)} %get-tuple-element.156), channel_id=1, source_target_pairs={{0,3},{1,2},{2,1},{3,0},{4,7},{5,6},{6,5},{7,4},{8,11},{9,10},{10,... | collective-permute-start | bytes 393224 | tf_op jit(solution)/shard_map/ppermute | solution.py:41
  74.0 14.6 %collective-permute-start.15 = (bf16[64,1024]{1,0:T(8,128)(2,1)S(1)}, bf16[64,1024]{1,0:T(8,128)(2,1)S(1)}, u32[]{:S(2)}, u32[]{:S(2)}) collective-permute-start(bf16[64,1024]{1,0:T(8,128)(2,1)S(1)} %get-tuple-element.155), channel_id=1, source_target_pairs={{0,2},{1,3},{2,0},{3,1},{4,6},{5,7},{6,4},{7,5},{8,10},{9,11},{10,... | collective-permute-start | bytes 393224 | tf_op jit(solution)/shard_map/ppermute | solution.py:41
  74.0 14.6 %collective-permute-start.14 = (bf16[64,1024]{1,0:T(8,128)(2,1)S(1)}, bf16[64,1024]{1,0:T(8,128)(2,1)S(1)}, u32[]{:S(2)}, u32[]{:S(2)}) collective-permute-start(bf16[64,1024]{1,0:T(8,128)(2,1)S(1)} %get-tuple-element.105), channel_id=1, source_target_pairs={{0,1},{1,0},{2,3},{3,2},{4,5},{5,4},{6,7},{7,6},{8,9},{9,8},{10,11... | collective-permute-start | bytes 393224 | tf_op jit(solution)/shard_map/ppermute | solution.py:41
  78.7 14.1 %collective-permute-start.35 = (bf16[64,1024]{1,0:T(8,128)(2,1)S(1)}, bf16[64,1024]{1,0:T(8,128)(2,1)}, u32[]{:S(2)}, u32[]{:S(2)}) collective-permute-start(bf16[64,1024]{1,0:T(8,128)(2,1)S(1)} %constant_dynamic-update-slice_fusion.18), channel_id=1, source_target_pairs={{0,3},{1,2},{2,1},{3,0},{4,7},{5,6},{6,5},{7,4},{8,11},{9,10},{10,... | collective-permute-start | bytes 393224 | tf_op jit(solution)/shard_map/ppermute | solution.py:41
  88.6 11.5 %collective-permute-start.34 = (bf16[64,1024]{1,0:T(8,128)(2,1)S(1)}, bf16[64,1024]{1,0:T(8,128)(2,1)}, u32[]{:S(2)}, u32[]{:S(2)}) collective-permute-start(bf16[64,1024]{1,0:T(8,128)(2,1)S(1)} %constant_dynamic-update-slice_fusion.18), channel_id=1, source_target_pairs={{0,2},{1,3},{2,0},{3,1},{4,6},{5,7},{6,4},{7,5},{8,10},{9,11},{10,... | collective-permute-start | bytes 393224 | tf_op jit(solution)/shard_map/ppermute | solution.py:41
  88.6 11.6 %collective-permute-start.33 = (bf16[64,1024]{1,0:T(8,128)(2,1)S(1)}, bf16[64,1024]{1,0:T(8,128)(2,1)}, u32[]{:S(2)}, u32[]{:S(2)}) collective-permute-start(bf16[64,1024]{1,0:T(8,128)(2,1)S(1)} %constant_dynamic-update-slice_fusion.18), channel_id=1, source_target_pairs={{0,1},{1,0},{2,3},{3,2},{4,5},{5,4},{6,7},{7,6},{8,9},{9,8},{10,11... | collective-permute-start | bytes 393224 | tf_op jit(solution)/shard_map/ppermute | solution.py:41
  92.8 11.4 %collective-permute-start.19 = (bf16[64,1024]{1,0:T(8,128)(2,1)}, bf16[64,1024]{1,0:T(8,128)(2,1)}, u32[]{:S(2)}, u32[]{:S(2)}) collective-permute-start(bf16[64,1024]{1,0:T(8,128)(2,1)} %multiply_convert_fusion.7), channel_id=1, source_target_pairs={{0,3},{1,2},{2,1},{3,0},{4,7},{5,6},{6,5},{7,4},{8,11},{9,10},{10,... | collective-permute-start | bytes 393224 | tf_op jit(solution)/shard_map/ppermute | solution.py:41
  100.1 8.4 %collective-permute-start.18 = (bf16[64,1024]{1,0:T(8,128)(2,1)}, bf16[64,1024]{1,0:T(8,128)(2,1)}, u32[]{:S(2)}, u32[]{:S(2)}) collective-permute-start(bf16[64,1024]{1,0:T(8,128)(2,1)} %multiply_convert_fusion.7), channel_id=1, source_target_pairs={{0,2},{1,3},{2,0},{3,1},{4,6},{5,7},{6,4},{7,5},{8,10},{9,11},{10,... | collective-permute-start | bytes 393224 | tf_op jit(solution)/shard_map/ppermute | solution.py:41
  100.2 8.5 %collective-permute-start.17 = (bf16[64,1024]{1,0:T(8,128)(2,1)}, bf16[64,1024]{1,0:T(8,128)(2,1)}, u32[]{:S(2)}, u32[]{:S(2)}) collective-permute-start(bf16[64,1024]{1,0:T(8,128)(2,1)} %multiply_convert_fusion.7), channel_id=1, source_target_pairs={{0,1},{1,0},{2,3},{3,2},{4,5},{5,4},{6,7},{7,6},{8,9},{9,8},{10,11... | collective-permute-start | bytes 393224 | tf_op jit(solution)/shard_map/ppermute | solution.py:41
  129.9 9.3 %collective-permute-start.38 = (bf16[64,1024]{1,0:T(8,128)(2,1)S(1)}, bf16[64,1024]{1,0:T(8,128)(2,1)S(1)}, u32[]{:S(2)}, u32[]{:S(2)}) collective-permute-start(bf16[64,1024]{1,0:T(8,128)(2,1)S(1)} %get-tuple-element.168), channel_id=1, source_target_pairs={{0,3},{1,2},{2,1},{3,0},{4,7},{5,6},{6,5},{7,4},{8,11},{9,10},{10,... | collective-permute-start | bytes 393224 | tf_op jit(solution)/shard_map/ppermute | solution.py:41
  132.0 16.4 %collective-permute-start.37 = (bf16[64,1024]{1,0:T(8,128)(2,1)S(1)}, bf16[64,1024]{1,0:T(8,128)(2,1)S(1)}, u32[]{:S(2)}, u32[]{:S(2)}) collective-permute-start(bf16[64,1024]{1,0:T(8,128)(2,1)S(1)} %get-tuple-element.169), channel_id=1, source_target_pairs={{0,2},{1,3},{2,0},{3,1},{4,6},{5,7},{6,4},{7,5},{8,10},{9,11},{10,... | collective-permute-start | bytes 393224 | tf_op jit(solution)/shard_map/ppermute | solution.py:41
  132.0 16.4 %collective-permute-start.36 = (bf16[64,1024]{1,0:T(8,128)(2,1)S(1)}, bf16[64,1024]{1,0:T(8,128)(2,1)S(1)}, u32[]{:S(2)}, u32[]{:S(2)}) collective-permute-start(bf16[64,1024]{1,0:T(8,128)(2,1)S(1)} %get-tuple-element.167), channel_id=1, source_target_pairs={{0,1},{1,0},{2,3},{3,2},{4,5},{5,4},{6,7},{7,6},{8,9},{9,8},{10,11... | collective-permute-start | bytes 393224 | tf_op jit(solution)/shard_map/ppermute | solution.py:41
  136.3 51.0 %collective-permute-start.32 = (bf16[64,1024]{1,0:T(8,128)(2,1)S(1)}, bf16[64,1024]{1,0:T(8,128)(2,1)S(1)}, u32[]{:S(2)}, u32[]{:S(2)}) collective-permute-start(bf16[64,1024]{1,0:T(8,128)(2,1)S(1)} %get-tuple-element.171), channel_id=1, source_target_pairs={{0,3},{1,2},{2,1},{3,0},{4,7},{5,6},{6,5},{7,4},{8,11},{9,10},{10,... | collective-permute-start | bytes 393224 | tf_op jit(solution)/shard_map/ppermute | solution.py:41
  138.4 51.7 %collective-permute-start.31 = (bf16[64,1024]{1,0:T(8,128)(2,1)S(1)}, bf16[64,1024]{1,0:T(8,128)(2,1)S(1)}, u32[]{:S(2)}, u32[]{:S(2)}) collective-permute-start(bf16[64,1024]{1,0:T(8,128)(2,1)S(1)} %get-tuple-element.172), channel_id=1, source_target_pairs={{0,2},{1,3},{2,0},{3,1},{4,6},{5,7},{6,4},{7,5},{8,10},{9,11},{10,... | collective-permute-start | bytes 393224 | tf_op jit(solution)/shard_map/ppermute | solution.py:41
  148.9 8.3 %collective-permute-start.39 = (bf16[64,1024]{1,0:T(8,128)(2,1)S(1)}, bf16[64,1024]{1,0:T(8,128)(2,1)S(1)}, u32[]{:S(2)}, u32[]{:S(2)}) collective-permute-start(bf16[64,1024]{1,0:T(8,128)(2,1)S(1)} %fusion.104), channel_id=1, source_target_pairs={{0,3},{1,2},{2,1},{3,0},{4,7},{5,6},{6,5},{7,4},{8,11},{9,10},{10,... | collective-permute-start | bytes 393224 | tf_op jit(solution)/shard_map/ppermute | solution.py:41
  151.2 13.8 %collective-permute-start.40 = (bf16[64,1024]{1,0:T(8,128)(2,1)S(1)}, bf16[64,1024]{1,0:T(8,128)(2,1)S(1)}, u32[]{:S(2)}, u32[]{:S(2)}) collective-permute-start(bf16[64,1024]{1,0:T(8,128)(2,1)S(1)} %fusion.104), channel_id=1, source_target_pairs={{0,2},{1,3},{2,0},{3,1},{4,6},{5,7},{6,4},{7,5},{8,10},{9,11},{10,... | collective-permute-start | bytes 393224 | tf_op jit(solution)/shard_map/ppermute | solution.py:41
  151.2 13.8 %collective-permute-start.41 = (bf16[64,1024]{1,0:T(8,128)(2,1)S(1)}, bf16[64,1024]{1,0:T(8,128)(2,1)S(1)}, u32[]{:S(2)}, u32[]{:S(2)}) collective-permute-start(bf16[64,1024]{1,0:T(8,128)(2,1)S(1)} %fusion.104), channel_id=1, source_target_pairs={{0,1},{1,0},{2,3},{3,2},{4,5},{5,4},{6,7},{7,6},{8,9},{9,8},{10,11... | collective-permute-start | bytes 393224 | tf_op jit(solution)/shard_map/ppermute | solution.py:41
  172.7 7.7 %collective-permute-start.45 = (bf16[64,1024]{1,0:T(8,128)(2,1)S(1)}, bf16[64,1024]{1,0:T(8,128)(2,1)S(1)}, u32[]{:S(2)}, u32[]{:S(2)}) collective-permute-start(bf16[64,1024]{1,0:T(8,128)(2,1)S(1)} %get-tuple-element.154), channel_id=1, source_target_pairs={{0,3},{1,2},{2,1},{3,0},{4,7},{5,6},{6,5},{7,4},{8,11},{9,10},{10,... | collective-permute-start | bytes 393224 | tf_op jit(solution)/shard_map/ppermute | solution.py:41
  175.1 11.5 %collective-permute-start.44 = (bf16[64,1024]{1,0:T(8,128)(2,1)S(1)}, bf16[64,1024]{1,0:T(8,128)(2,1)S(1)}, u32[]{:S(2)}, u32[]{:S(2)}) collective-permute-start(bf16[64,1024]{1,0:T(8,128)(2,1)S(1)} %get-tuple-element.153), channel_id=1, source_target_pairs={{0,2},{1,3},{2,0},{3,1},{4,6},{5,7},{6,4},{7,5},{8,10},{9,11},{10,... | collective-permute-start | bytes 393224 | tf_op jit(solution)/shard_map/ppermute | solution.py:41
  175.1 11.6 %collective-permute-start.43 = (bf16[64,1024]{1,0:T(8,128)(2,1)S(1)}, bf16[64,1024]{1,0:T(8,128)(2,1)S(1)}, u32[]{:S(2)}, u32[]{:S(2)}) collective-permute-start(bf16[64,1024]{1,0:T(8,128)(2,1)S(1)} %get-tuple-element.65), channel_id=1, source_target_pairs={{0,1},{1,0},{2,3},{3,2},{4,5},{5,4},{6,7},{7,6},{8,9},{9,8},{10,11... | collective-permute-start | bytes 393224 | tf_op jit(solution)/shard_map/ppermute | solution.py:41
  180.4 11.2 %collective-permute-start.30 = (bf16[64,1024]{1,0:T(8,128)(2,1)S(1)}, bf16[64,1024]{1,0:T(8,128)(2,1)S(1)}, u32[]{:S(2)}, u32[]{:S(2)}) collective-permute-start(bf16[64,1024]{1,0:T(8,128)(2,1)S(1)} %get-tuple-element.170), channel_id=1, source_target_pairs={{0,1},{1,0},{2,3},{3,2},{4,5},{5,4},{6,7},{7,6},{8,9},{9,8},{10,11... | collective-permute-start | bytes 393224 | tf_op jit(solution)/shard_map/ppermute | solution.py:41
  186.6 18.8 %collective-permute-start.61 = (bf16[256,512]{1,0:T(8,128)(2,1)S(1)}, bf16[256,512]{1,0:T(8,128)(2,1)S(1)}, u32[]{:S(2)}, u32[]{:S(2)}) collective-permute-start(bf16[256,512]{1,0:T(8,128)(2,1)S(1)} %convolution_convert_fusion.6), channel_id=1, source_target_pairs={{0,4},{4,0},{8,12},{12,8},{16,20},{20,16},{24,28},{28,24},{1,5},{5... | collective-permute-start | bytes 786440 | tf_op jit(solution)/shard_map/ppermute | solution.py:41
  187.1 5.1 %collective-permute-start.48 = (f32[5,1024]{1,0:T(8,128)S(1)}, f32[5,1024]{1,0:T(8,128)S(1)}, u32[]{:S(2)}, u32[]{:S(2)}) collective-permute-start(f32[5,1024]{1,0:T(8,128)S(1)} %pad_maximum_fusion.18), channel_id=1, source_target_pairs={{0,1},{1,0},{2,3},{3,2},{4,5},{5,4},{6,7},{7,6},{8,9},{9,8},{10,11... | collective-permute-start | bytes 61448 | tf_op jit(solution)/shard_map/ppermute | solution.py:41
  187.2 5.2 %collective-permute-start.47 = (f32[5,1024]{1,0:T(8,128)S(1)}, f32[5,1024]{1,0:T(8,128)S(1)}, u32[]{:S(2)}, u32[]{:S(2)}) collective-permute-start(f32[5,1024]{1,0:T(8,128)S(1)} %pad_maximum_fusion.18), channel_id=1, source_target_pairs={{0,2},{1,3},{2,0},{3,1},{4,6},{5,7},{6,4},{7,5},{8,10},{9,11},{10,... | collective-permute-start | bytes 61448 | tf_op jit(solution)/shard_map/ppermute | solution.py:41
  190.1 5.7 %collective-permute-start.46 = (f32[5,1024]{1,0:T(8,128)S(1)}, f32[5,1024]{1,0:T(8,128)S(1)}, u32[]{:S(2)}, u32[]{:S(2)}) collective-permute-start(f32[5,1024]{1,0:T(8,128)S(1)} %pad_maximum_fusion.18), channel_id=1, source_target_pairs={{0,3},{1,2},{2,1},{3,0},{4,7},{5,6},{6,5},{7,4},{8,11},{9,10},{10,... | collective-permute-start | bytes 61448 | tf_op jit(solution)/shard_map/ppermute | solution.py:41
  199.9 4.8 %collective-permute-start.50 = (f32[5,1024]{1,0:T(8,128)S(1)}, f32[5,1024]{1,0:T(8,128)S(1)}, u32[]{:S(2)}, u32[]{:S(2)}) collective-permute-start(f32[5,1024]{1,0:T(8,128)S(1)} %select_add_fusion.1), channel_id=1, source_target_pairs={{0,24},{4,28},{8,16},{12,20},{16,8},{20,12},{24,0},{28,4},{1,25},{... | collective-permute-start | bytes 61448 | tf_op jit(solution)/shard_map/ppermute | solution.py:41
  202.3 26.6 %collective-permute-start.66 = (bf16[2,512,1152]{2,1,0:T(8,128)(2,1)S(1)}, bf16[2,512,1152]{2,1,0:T(8,128)(2,1)S(1)}, u32[]{:S(2)}, u32[]{:S(2)}) collective-permute-start(bf16[2,512,1152]{2,1,0:T(8,128)(2,1)S(1)} %pad_maximum_fusion), channel_id=1, source_target_pairs={{0,4},{4,0},{8,12},{12,8},{16,20},{20,16},{24,28},{28,24},{1,5},{5... | collective-permute-start | bytes 7077896 | tf_op jit(solution)/shard_map/ppermute | solution.py:41
  203.1 18.6 %collective-permute-start.71 = (bf16[1152,512]{1,0:T(8,128)(2,1)S(1)}, bf16[1152,512]{1,0:T(8,128)(2,1)S(1)}, u32[]{:S(2)}, u32[]{:S(2)}) collective-permute-start(bf16[1152,512]{1,0:T(8,128)(2,1)S(1)} %convolution_convert_fusion), channel_id=1, source_target_pairs={{0,4},{4,0},{8,12},{12,8},{16,20},{20,16},{24,28},{28,24},{1,5},{5... | collective-permute-start | bytes 3538952 | tf_op jit(solution)/shard_map/ppermute | solution.py:41
  204.7 9.0 %collective-permute-start.56 = (bf16[3,512,256]{1,2,0:T(8,128)(2,1)S(1)}, bf16[3,512,256]{1,2,0:T(8,128)(2,1)S(1)}, u32[]{:S(2)}, u32[]{:S(2)}) collective-permute-start(bf16[3,512,256]{1,2,0:T(8,128)(2,1)S(1)} %pad_maximum_fusion.3), channel_id=1, source_target_pairs={{0,4},{4,0},{8,12},{12,8},{16,20},{20,16},{24,28},{28,24},{1,5},{5... | collective-permute-start | bytes 2359304 | tf_op jit(solution)/shard_map/ppermute | solution.py:41
  212.0 4.8 %collective-permute-start.65 = (bf16[256,128]{1,0:T(8,128)(2,1)S(1)}, bf16[256,128]{1,0:T(8,128)(2,1)S(1)}, u32[]{:S(2)}, u32[]{:S(2)}) collective-permute-start(bf16[256,128]{1,0:T(8,128)(2,1)S(1)} %pad_maximum_fusion.17), channel_id=1, source_target_pairs={{0,16},{4,20},{8,24},{12,28},{16,0},{20,4},{24,8},{28,12},{1,17},{... | collective-permute-start | bytes 196616 | tf_op jit(solution)/shard_map/ppermute | solution.py:41
  212.1 5.1 %collective-permute-start.63 = (bf16[256,128]{1,0:T(8,128)(2,1)S(1)}, bf16[256,128]{1,0:T(8,128)(2,1)S(1)}, u32[]{:S(2)}, u32[]{:S(2)}) collective-permute-start(bf16[256,128]{1,0:T(8,128)(2,1)S(1)} %pad_maximum_fusion.16), channel_id=1, source_target_pairs={{0,8},{4,12},{8,0},{12,4},{16,24},{20,28},{24,16},{28,20},{1,9},{5... | collective-permute-start | bytes 196616 | tf_op jit(solution)/shard_map/ppermute | solution.py:41
  214.2 4.7 %collective-permute-start.57 = (bf16[3,128,128]{1,2,0:T(8,128)(2,1)S(1)}, bf16[3,128,128]{1,2,0:T(8,128)(2,1)S(1)}, u32[]{:S(2)}, u32[]{:S(2)}) collective-permute-start(bf16[3,128,128]{1,2,0:T(8,128)(2,1)S(1)} %get-tuple-element.160), channel_id=1, source_target_pairs={{0,16},{4,20},{8,24},{12,28},{16,0},{20,4},{24,8},{28,12},{1,17},{... | collective-permute-start | bytes 294920 | tf_op jit(solution)/shard_map/ppermute | solution.py:41
  216.8 4.9 %collective-permute-start.59 = (bf16[3,128,128]{1,2,0:T(8,128)(2,1)S(1)}, bf16[3,128,128]{1,2,0:T(8,128)(2,1)S(1)}, u32[]{:S(2)}, u32[]{:S(2)}) collective-permute-start(bf16[3,128,128]{1,2,0:T(8,128)(2,1)S(1)} %get-tuple-element.159), channel_id=1, source_target_pairs={{0,8},{4,12},{8,0},{12,4},{16,24},{20,28},{24,16},{28,20},{1,9},{5... | collective-permute-start | bytes 294920 | tf_op jit(solution)/shard_map/ppermute | solution.py:41
  222.3 6.5 %collective-permute-start.72 = (bf16[576,128]{1,0:T(8,128)(2,1)S(1)}, bf16[576,128]{1,0:T(8,128)(2,1)S(1)}, u32[]{:S(2)}, u32[]{:S(2)}) collective-permute-start(bf16[576,128]{1,0:T(8,128)(2,1)S(1)} %get-tuple-element.152), channel_id=1, source_target_pairs={{0,16},{4,20},{8,24},{12,28},{16,0},{20,4},{24,8},{28,12},{1,17},{... | collective-permute-start | bytes 442376 | tf_op jit(solution)/shard_map/ppermute | solution.py:41
  222.5 6.4 %collective-permute-start.74 = (bf16[576,128]{1,0:T(8,128)(2,1)S(1)}, bf16[576,128]{1,0:T(8,128)(2,1)S(1)}, u32[]{:S(2)}, u32[]{:S(2)}) collective-permute-start(bf16[576,128]{1,0:T(8,128)(2,1)S(1)} %get-tuple-element.151), channel_id=1, source_target_pairs={{0,8},{4,12},{8,0},{12,4},{16,24},{20,28},{24,16},{28,20},{1,9},{5... | collective-permute-start | bytes 442376 | tf_op jit(solution)/shard_map/ppermute | solution.py:41
  224.1 19.6 %collective-permute-start.60 = (bf16[3,128,256]{1,2,0:T(8,128)(2,1)S(1)}, bf16[3,128,256]{1,2,0:T(8,128)(2,1)S(1)}, u32[]{:S(2)}, u32[]{:S(2)}) collective-permute-start(bf16[3,128,256]{1,2,0:T(8,128)(2,1)S(1)} %pad_maximum_fusion.15), channel_id=1, source_target_pairs={{0,16},{4,20},{8,24},{12,28},{16,0},{20,4},{24,8},{28,12},{1,17},{... | collective-permute-start | bytes 589832 | tf_op jit(solution)/shard_map/ppermute | solution.py:41
  224.7 19.5 %collective-permute-start.58 = (bf16[3,128,256]{1,2,0:T(8,128)(2,1)S(1)}, bf16[3,128,256]{1,2,0:T(8,128)(2,1)S(1)}, u32[]{:S(2)}, u32[]{:S(2)}) collective-permute-start(bf16[3,128,256]{1,2,0:T(8,128)(2,1)S(1)} %pad_maximum_fusion.14), channel_id=1, source_target_pairs={{0,8},{4,12},{8,0},{12,4},{16,24},{20,28},{24,16},{28,20},{1,9},{5... | collective-permute-start | bytes 589832 | tf_op jit(solution)/shard_map/ppermute | solution.py:41
  229.6 10.3 %collective-permute-start.67 = (bf16[1,128,1152]{2,1,0:T(8,128)(2,1)S(1)}, bf16[1,128,1152]{2,1,0:T(8,128)(2,1)S(1)}, u32[]{:S(2)}, u32[]{:S(2)}) collective-permute-start(bf16[1,128,1152]{2,1,0:T(8,128)(2,1)S(1)} %get-tuple-element.141), channel_id=1, source_target_pairs={{0,16},{4,20},{8,24},{12,28},{16,0},{20,4},{24,8},{28,12},{1,17},{... | collective-permute-start | bytes 884744 | tf_op jit(solution)/shard_map/ppermute | solution.py:41
  232.0 9.9 %collective-permute-start.69 = (bf16[1,128,1152]{2,1,0:T(8,128)(2,1)S(1)}, bf16[1,128,1152]{2,1,0:T(8,128)(2,1)S(1)}, u32[]{:S(2)}, u32[]{:S(2)}) collective-permute-start(bf16[1,128,1152]{2,1,0:T(8,128)(2,1)S(1)} %get-tuple-element.140), channel_id=1, source_target_pairs={{0,8},{4,12},{8,0},{12,4},{16,24},{20,28},{24,16},{28,20},{1,9},{5... | collective-permute-start | bytes 884744 | tf_op jit(solution)/shard_map/ppermute | solution.py:41
  232.7 13.6 %collective-permute-start.75 = (bf16[1152,128]{1,0:T(8,128)(2,1)}, bf16[1152,128]{1,0:T(8,128)(2,1)}, u32[]{:S(2)}, u32[]{:S(2)}) collective-permute-start(bf16[1152,128]{1,0:T(8,128)(2,1)} %pad_maximum_fusion.11), channel_id=1, source_target_pairs={{0,16},{4,20},{8,24},{12,28},{16,0},{20,4},{24,8},{28,12},{1,17},{... | collective-permute-start | bytes 884744 | tf_op jit(solution)/shard_map/ppermute | solution.py:41
  239.9 10.3 %collective-permute-start.73 = (bf16[1152,128]{1,0:T(8,128)(2,1)}, bf16[1152,128]{1,0:T(8,128)(2,1)}, u32[]{:S(2)}, u32[]{:S(2)}) collective-permute-start(bf16[1152,128]{1,0:T(8,128)(2,1)} %pad_maximum_fusion.10), channel_id=1, source_target_pairs={{0,8},{4,12},{8,0},{12,4},{16,24},{20,28},{24,16},{28,20},{1,9},{5... | collective-permute-start | bytes 884744 | tf_op jit(solution)/shard_map/ppermute | solution.py:41
  242.8 12.1 %collective-permute-start.70 = (bf16[2,128,1152]{2,1,0:T(8,128)(2,1)}, bf16[2,128,1152]{2,1,0:T(8,128)(2,1)S(1)}, u32[]{:S(2)}, u32[]{:S(2)}) collective-permute-start(bf16[2,128,1152]{2,1,0:T(8,128)(2,1)} %pad_maximum_fusion.5), channel_id=1, source_target_pairs={{0,16},{4,20},{8,24},{12,28},{16,0},{20,4},{24,8},{28,12},{1,17},{... | collective-permute-start | bytes 1769480 | tf_op jit(solution)/shard_map/ppermute | solution.py:41
  243.7 13.9 %collective-permute-start.68 = (bf16[2,128,1152]{2,1,0:T(8,128)(2,1)}, bf16[2,128,1152]{2,1,0:T(8,128)(2,1)}, u32[]{:S(2)}, u32[]{:S(2)}) collective-permute-start(bf16[2,128,1152]{2,1,0:T(8,128)(2,1)} %pad_maximum_fusion.4), channel_id=1, source_target_pairs={{0,8},{4,12},{8,0},{12,4},{16,24},{20,28},{24,16},{28,20},{1,9},{5... | collective-permute-start | bytes 1769480 | tf_op jit(solution)/shard_map/ppermute | solution.py:41
  (71 other events, 473.3 us)

commit v2 on v1

--- a/solution.py
+++ b/solution.py
@@ -69,24 +69,48 @@
     return jnp.concatenate(xor_order(blocks, lax.axis_index("dp")), axis=-1)
 
 
-def gather_weight(shard, axis, cut):
+def gather_weight(shard):
     count = lax.axis_size("dp")
     if count == 8:
-        over_x = swapped(shard, "dp", 2)
-        over_y = swapped(shard, "dp", 4)
-        first, _ = jnp.split(over_x, 2, axis=cut)
-        _, second = jnp.split(over_y, 2, axis=cut)
-        corner = jnp.concatenate(
-            [swapped(first, "dp", 4), swapped(second, "dp", 2)], axis=cut
-        )
-        near = jnp.concatenate([shard, over_x, over_y, corner], axis=axis)
+        over_x, over_y = yield swapped(shard, "dp", 2), swapped(shard, "dp", 4)
+        first, _ = jnp.split(over_x, 2, axis=1)
+        _, second = jnp.split(over_y, 2, axis=1)
+        first, second = yield swapped(first, "dp", 4), swapped(second, "dp", 2)
+        near = jnp.concatenate([shard, over_x, over_y, first, second], axis=1)
     else:
         near = shard
         bit = 2
         while bit < count:
-            near = jnp.concatenate([near, swapped(near, "dp", bit)], axis=axis)
+            got = yield swapped(near, "dp", bit)
+            near = jnp.concatenate([near, got], axis=1)
             bit *= 2
-    return near, swapped(near, "dp", 1)
+    far = yield swapped(near, "dp", 1)
+    yield None, (near, far)
+
+
+def beside(values, *pending):
+    waited = [(steps, held) for steps, held in pending if not finished(held)]
+    values, got = lax.optimization_barrier((values, [held for _, held in waited]))
+    got = iter(got)
+    moved = [
+        (steps, held) if finished(held) else (steps, steps.send(next(got)))
+        for steps, held in pending
+    ]
+    return (values, *moved)
+
+
+def finished(held):
+    return isinstance(held, tuple) and held[0] is None
+
+
+def begin(steps):
+    return steps, next(steps)
+
+
+def finish(steps, held):
+    while not finished(held):
+        held = steps.send(held)
+    return held[1]
 
 
 def wide(values):
@@ -97,25 +121,28 @@
     return values.astype(jnp.bfloat16)
 
 
-def scatter_weight(near, far, axis, cut):
+def scatter_weight(near, far):
     count = lax.axis_size("dp")
-    total = wide(near) + wide(swapped(narrow(far), "dp", 1))
+    got = yield swapped(far, "dp", 1)
+    total = wide(near) + wide(got)
     if count == 8:
-        own, for_x, for_y, corner = jnp.split(total, 4, axis=axis)
-        first, second = jnp.split(narrow(corner), 2, axis=cut)
-        got_first = wide(swapped(first, "dp", 2))
-        got_second = wide(swapped(second, "dp", 4))
-        y_first, y_second = jnp.split(for_y, 2, axis=cut)
-        x_first, x_second = jnp.split(for_x, 2, axis=cut)
-        for_y = jnp.concatenate([narrow(y_first + got_first), narrow(y_second)], axis=cut)
-        for_x = jnp.concatenate([narrow(x_first), narrow(x_second + got_second)], axis=cut)
-        return own + wide(swapped(for_x, "dp", 2)) + wide(swapped(for_y, "dp", 4))
-    bit = count // 2
-    while bit > 1:
-        keep, send = jnp.split(total, 2, axis=axis)
-        total = keep + wide(swapped(narrow(send), "dp", bit))
-        bit //= 2
-    return total
+        own, for_x, for_y, corner = jnp.split(total, 4, axis=1)
+        first, second = jnp.split(narrow(corner), 2, axis=1)
+        first, second = yield swapped(first, "dp", 2), swapped(second, "dp", 4)
+        y_first, y_second = jnp.split(for_y, 2, axis=1)
+        x_first, x_second = jnp.split(for_x, 2, axis=1)
+        for_y = jnp.concatenate([narrow(y_first + wide(first)), narrow(y_second)], axis=1)
+        for_x = jnp.concatenate([narrow(x_first), narrow(x_second + wide(second))], axis=1)
+        from_x, from_y = yield swapped(for_x, "dp", 2), swapped(for_y, "dp", 4)
+        total = own + wide(from_x) + wide(from_y)
+    else:
+        bit = count // 2
+        while bit > 1:
+            keep, send = jnp.split(total, 2, axis=1)
+            got = yield swapped(narrow(send), "dp", bit)
+            total = keep + wide(got)
+            bit //= 2
+    yield None, total
 
 
 def gather_rows(rows):
@@ -196,15 +223,21 @@
     second_gain = to_relative(second_gain)
     cotangent = to_relative(cotangent)
 
-    normed = in_token_order(gather_rows(narrow(rms_norm(residual, first_gain))))
-    in_near, in_far = gather_weight(entry_projection_weight, 1, 2)
-    out_near, out_far = gather_weight(out_weight, 1, 0)
-    gate_up_near, gate_up_far = gather_weight(gate_up_weight, 1, 0)
-    down_near, down_far = gather_weight(down_weight, 1, 0)
-    grad_rows = jnp.concatenate(gather_rows(cotangent), axis=0)
+    mixer_weights = jnp.concatenate([entry_projection_weight, out_weight.T[None]], axis=0)
+    ffn_weights = jnp.concatenate([gate_up_weight, down_weight.T[None]], axis=0)
+    mixer_gather = begin(gather_weight(mixer_weights))
+    normed_parts = gather_rows(narrow(rms_norm(residual, first_gain)))
+    normed_parts, mixer_gather = beside(normed_parts, mixer_gather)
+    ffn_weights, mixer_gather = beside(ffn_weights, mixer_gather)
+    ffn_gather = begin(gather_weight(ffn_weights))
+    grad_parts = gather_rows(cotangent)
+    mixer_near, mixer_far = finish(*mixer_gather)
+    normed = in_token_order(normed_parts)
 
     normed_near, normed_far = halves(normed)
-    projected = [dot(normed_near, in_near[k]) + dot(normed_far, in_far[k]) for k in range(3)]
+    projected = [
+        dot(normed_near, mixer_near[k]) + dot(normed_far, mixer_far[k]) for k in range(3)
+    ]
     input_gate_value, c_value, v_value = projected
     product = narrow(input_gate_value * v_value)
     before = passed_along(product[-2:], "dp", 1)
@@ -215,48 +248,62 @@
         + kernel[0] * second_keep * extended[:-2]
     )
     gated = narrow(c_value * mixed)
-    mixer_part = jnp.concatenate([dot(gated, out_near), dot(gated, out_far)], axis=1)
+    gated, ffn_gather = beside(gated, ffn_gather)
+    mixer_part = jnp.concatenate(
+        [times_trans(gated, mixer_near[3]), times_trans(gated, mixer_far[3])], axis=1
+    )
     middle = residual + scatter_rows(for_owners(mixer_part))
+    (middle, grad_parts), ffn_gather = beside((middle, grad_parts), ffn_gather)
+    grad_rows = jnp.concatenate(grad_parts, axis=0)
     hidden_in = jnp.concatenate(
         gather_rows(narrow(rms_norm(middle, second_gain))), axis=0
     )
     hidden_near, hidden_far = halves(hidden_in)
-    gate_value = dot(hidden_near, gate_up_near[0]) + dot(hidden_far, gate_up_far[0])
-    up_value = dot(hidden_near, gate_up_near[1]) + dot(hidden_far, gate_up_far[1])
+    ffn_near, ffn_far = finish(*ffn_gather)
+    gate_value = dot(hidden_near, ffn_near[0]) + dot(hidden_far, ffn_far[0])
+    up_value = dot(hidden_near, ffn_near[1]) + dot(hidden_far, ffn_far[1])
     sigmoid = jax.nn.sigmoid(gate_value)
     swish = gate_value * sigmoid
     hidden = narrow(swish * up_value)
     grad_near, grad_far = halves(grad_rows)
-    down_part_far = narrow(trans_times(hidden, grad_far))
-    down_part_near = narrow(trans_times(hidden, grad_near))
-    grad_hidden = times_trans(grad_near, down_near) + times_trans(grad_far, down_far)
+    grad_hidden = dot(grad_near, ffn_near[2]) + dot(grad_far, ffn_far[2])
     grad_gate = narrow(grad_hidden * up_value * sigmoid * (1.0 + gate_value * (1.0 - sigmoid)))
     grad_up = narrow(grad_hidden * swish)
     hidden_back = jnp.concatenate(
         [
             times_trans(grad_gate, half[0]) + times_trans(grad_up, half[1])
-            for half in (gate_up_near, gate_up_far)
+            for half in (ffn_near, ffn_far)
         ],
         axis=1,
     )
+    ffn_scatter = begin(
+        scatter_weight(
+            *[
+                jnp.stack(
+                    [
+                        narrow(trans_times(rows, grad_gate)),
+                        narrow(trans_times(rows, grad_up)),
+                        narrow(trans_times(outer, hidden)),
+                    ]
+                )
+                for rows, outer in ((hidden_near, grad_near), (hidden_far, grad_far))
+            ]
+        )
+    )
     grad_hin = scatter_rows(jnp.split(hidden_back, lax.axis_size("tensor"), axis=0))
-    gate_up_part_far = jnp.stack(
-        [narrow(trans_times(hidden_far, grad)) for grad in (grad_gate, grad_up)]
-    )
-    gate_up_part_near = jnp.stack(
-        [narrow(trans_times(hidden_near, grad)) for grad in (grad_gate, grad_up)]
-    )
-    ffn_part = jnp.concatenate([dot(hidden, down_near), dot(hidden, down_far)], axis=1)
-    output = narrow(
-        middle + scatter_rows(jnp.split(ffn_part, lax.axis_size("tensor"), axis=0))
-    )
+    grad_hin, ffn_scatter = beside(grad_hin, ffn_scatter)
     second_back, second_part = rms_back(middle, second_gain, grad_hin)
     grad_middle = wide(cotangent) + second_back
     branch_rows = in_token_order(gather_rows(narrow(grad_middle)))
+    (branch_rows, hidden), ffn_scatter = beside((branch_rows, hidden), ffn_scatter)
+    ffn_part = jnp.concatenate(
+        [times_trans(hidden, ffn_near[2]), times_trans(hidden, ffn_far[2])], axis=1
+    )
+    output = narrow(
+        middle + scatter_rows(jnp.split(ffn_part, lax.axis_size("tensor"), axis=0))
+    )
     branch_near, branch_far = halves(branch_rows)
-    grad_gated = times_trans(branch_near, out_near) + times_trans(branch_far, out_far)
-    out_part_far = narrow(trans_times(gated, branch_far))
-    out_part_near = narrow(trans_times(gated, branch_near))
+    grad_gated = dot(branch_near, mixer_near[3]) + dot(branch_far, mixer_far[3])
     output_gate_gradient = narrow(grad_gated * mixed)
     grad_mixed = narrow(grad_gated * c_value)
     after = passed_along(grad_mixed[:2], "dp", -1)
@@ -280,22 +327,32 @@
     input_gate_gradient = narrow(elementwise_product_gradient * v_value)
     value_branch_gradient = narrow(elementwise_product_gradient * input_gate_value)
     grads = [input_gate_gradient, output_gate_gradient, value_branch_gradient]
-    in_part_far = jnp.stack([narrow(trans_times(normed_far, grad)) for grad in grads])
-    in_part_near = jnp.stack([narrow(trans_times(normed_near, grad)) for grad in grads])
+    mixer_scatter = begin(
+        scatter_weight(
+            *[
+                jnp.stack(
+                    [narrow(trans_times(rows, grad)) for grad in grads]
+                    + [narrow(trans_times(outer, gated))]
+                )
+                for rows, outer in ((normed_near, branch_near), (normed_far, branch_far))
+            ]
+        )
+    )
     normed_back = jnp.concatenate(
         [
             sum(times_trans(grads[k], half[k]) for k in range(3))
-            for half in (in_near, in_far)
+            for half in (mixer_near, mixer_far)
         ],
         axis=1,
     )
     grad_normed = scatter_rows(for_owners(normed_back))
+    (grad_normed, output), ffn_scatter, mixer_scatter = beside(
+        (grad_normed, output), ffn_scatter, mixer_scatter
+    )
     first_back, first_part = rms_back(residual, first_gain, grad_normed)
     input_grad = grad_middle + first_back
-    down_grad = scatter_weight(down_part_near, down_part_far, 1, 0)
-    gate_up_grad = scatter_weight(gate_up_part_near, gate_up_part_far, 1, 0)
-    out_grad = scatter_weight(out_part_near, out_part_far, 1, 0)
-    in_grad = scatter_weight(in_part_near, in_part_far, 1, 2)
+    ffn_grad = finish(*ffn_scatter)
+    mixer_grad = finish(*mixer_scatter)
     small = jnp.concatenate(
         [to_absolute(first_part)[None], to_absolute(second_part)[None], kernel_full], axis=0
     )
@@ -304,12 +361,12 @@
         to_absolute(output),
         to_absolute(input_grad),
         small[0],
-        in_grad,
+        mixer_grad[:3],
         small[2:],
-        out_grad,
+        mixer_grad[3].T,
         small[1],
-        gate_up_grad,
-        down_grad,
+        ffn_grad[:2],
+        ffn_grad[2].T,
     )
 
 

time: 261 us -> 229 us (0.88)
  waiting for transfers between devices: 112 us -> 83.7 us
  starting transfers between devices: 84.7 us -> 68.7 us
  local copies, waits for them, and re-layouts: 5.61 us -> 19.3 us
  other arithmetic: 25.1 us -> 19.7 us
  matrix products: 30.2 us -> 33.6 us
    ppermute x74 -> x54, waiting for transfers between devices: 112 us -> 83.1 us  [swapped(): return lax.ppermute(block, axis, [(i, i ^ mask) for i in devices])]
    ppermute x74 -> x54, starting transfers between devices: 81.5 us -> 65.4 us  [swapped(): return lax.ppermute(block, axis, [(i, i ^ mask) for i in devices])]
    unnamed x119 -> x128, local copies, waits for them, and re-layouts: 1.8 us -> 9.58 us
    concatenate x13 -> x6, other arithmetic: 8.89 us -> 1.93 us  [the longest x1 1.67 us: shards(): jnp.concatenate([entry_projection_weight, out_weight.T[None]], axis=0)]
    another operation x6 -> x5, other arithmetic: 1.29 us -> 4.05 us  [the longest x1 2.28 us: shards(): jnp.stack([narrow(trans_times(rows, grad_gate)), narrow(trans_times(rows,...]
    add x4 -> x6, other arithmetic: 5.3 us -> 3.14 us  [the longest x1 2.49 us: scatter_weight(): total = wide(near) + wide(got)]
  transfers between devices with their start and end apart: 76 -> 56, of which waited for: 39 -> 23; matrix products, arithmetic and copies ran while one was open for 14% -> 20% of each run, Pallas kernels for 0% -> 0%
where the time goes in v2:
time: 229 us; the launch traced here: 228 us
  waiting for transfers between devices  83.7 us (37%)
  starting transfers between devices  68.7 us (30%)
  matrix products  33.6 us (15%)
  other arithmetic  19.7 us (9%)
  local copies, waits for them, and re-layouts  19.3 us (8%)
  between operations  2.55 us (1%)
    ppermute x54, waiting for transfers between devices, swapped(): return lax.ppermute(block, axis, [(i, i ^ mask) for i in devices])  83.1 us
    ppermute x54, starting transfers between devices, swapped(): return lax.ppermute(block, axis, [(i, i ^ mask) for i in devices])  65.4 us
    dot_general x14, matrix products, dot(): return jnp.dot(left, right, preferred_element_type=jnp.float32)  14.6 us
    dot_general x14, matrix products, times_trans(): lax.dot_general(left, right, (((1,), (1,)), ((), ())), preferred_element_...  12.9 us
    unnamed x128, local copies, waits for them, and re-layouts  9.58 us
    dot_general x14, matrix products, trans_times(): lax.dot_general(left, right, (((0,), (0,)), ((), ())), preferred_element_...  6.11 us
    unnamed x60, other arithmetic  4.62 us
  transfers between devices with their start and end apart: 56, of which 23 were waited for; matrix products, arithmetic and copies ran while one was open for 20% of the time, Pallas kernels for 0%

profile of v2, /device:TPU:0, one launch (start us, length us, event | category | flops | bytes accessed | tf_op | source)
XLA Modules:
  0.0 227.6 jit_solution(3138432225218584861)
XLA Ops:
  5.0 3.1 %collective-permute-start = (bf16[64,1024]{1,0:T(8,128)(2,1)S(1)}, bf16[64,1024]{1,0:T(8,128)(2,1)S(1)}, u32[]{:S(2)}, u32[]{:S(2)}) collective-permute-start(bf16[64,1024]{1,0:T(8,128)(2,1)S(1)} %fusion.33), channel_id=1, source_target_pairs={{0,1},{1,0},{2,3},{3,2},{4,5},{5,4},{6,7},{7,6},{8,9},{9,8},{10,11... | collective-permute-start | bytes 393224 | tf_op jit(solution)/shard_map/ppermute | solution.py:41
  8.1 2.6 %collective-permute-start.1 = (bf16[64,1024]{1,0:T(8,128)(2,1)S(1)}, bf16[64,1024]{1,0:T(8,128)(2,1)}, u32[]{:S(2)}, u32[]{:S(2)}) collective-permute-start(bf16[64,1024]{1,0:T(8,128)(2,1)S(1)} %fusion.33), channel_id=1, source_target_pairs={{0,2},{1,3},{2,0},{3,1},{4,6},{5,7},{6,4},{7,5},{8,10},{9,11},{10,... | collective-permute-start | bytes 393224 | tf_op jit(solution)/shard_map/ppermute | solution.py:41
  11.7 1.7 pad_maximum_fusion.12
  13.3 1.7 collective-permute-start.3
  15.1 1.5 collective-permute-start.4
  19.0 2.2 collective-permute-done.1
  21.2 1.2 collective-permute-done.4
  23.3 1.6 collective-permute-start.5
  28.3 2.5 %collective-permute-done.6 = bf16[4,64,256]{2,1,0:T(8,128)(2,1)S(1)} collective-permute-done((bf16[4,64,256]{2,1,0:T(8,128)(2,1)S(1)}, bf16[4,64,256]{2,1,0:T(8,128)(2,1)S(1)}, u32[]{:S(2)}, u32[]{:S(2)}) %collective-permute-start.6) | collective-permute-done | bytes 131104 | tf_op jit(solution)/shard_map/ppermute | solution.py:41
  30.9 1.0 broadcast_select_fusion.23
  35.8 1.8 collective-permute-start.8
  38.5 1.0 multiply_convert_fusion.8
  39.5 14.6 %collective-permute-done.10 = bf16[3,128,1152]{2,1,0:T(8,128)(2,1)S(1)} collective-permute-done((bf16[3,128,1152]{2,1,0:T(8,128)(2,1)S(1)}, bf16[3,128,1152]{2,1,0:T(8,128)(2,1)S(1)}, u32[]{:S(2)}, u32[]{:S(2)}) %collective-permute-start.10) | collective-permute-done | bytes 884768 | tf_op jit(solution)/shard_map/ppermute | solution.py:41
  55.1 1.9 collective-permute-start.12
  56.9 1.8 collective-permute-start.13
  59.3 2.3 %collective-permute-start.17 = (bf16[3,64,1152]{2,1,0:T(8,128)(2,1)S(1)}, bf16[3,64,1152]{2,1,0:T(8,128)(2,1)S(1)}, u32[]{:S(2)}, u32[]{:S(2)}) collective-permute-start(bf16[3,64,1152]{2,1,0:T(8,128)(2,1)S(1)} %split.368), channel_id=1, source_target_pairs={{0,16},{4,20},{8,24},{12,28},{16,0},{20,4},{24,8},{28,12},{1,17},{... | collective-permute-start | bytes 1327112 | tf_op jit(solution)/shard_map/ppermute | solution.py:41
  64.3 3.3 %collective-permute-done.12 = bf16[64,1024]{1,0:T(8,128)(2,1)S(1)} collective-permute-done((bf16[64,1024]{1,0:T(8,128)(2,1)S(1)}, bf16[64,1024]{1,0:T(8,128)(2,1)S(1)}, u32[]{:S(2)}, u32[]{:S(2)}) %collective-permute-start.12) | collective-permute-done | bytes 131104 | tf_op jit(solution)/shard_map/ppermute | solution.py:41
  67.6 4.0 %collective-permute-start.15 = (bf16[64,1024]{1,0:T(8,128)(2,1)S(1)}, bf16[64,1024]{1,0:T(8,128)(2,1)S(1)}, u32[]{:S(2)}, u32[]{:S(2)}) collective-permute-start(bf16[64,1024]{1,0:T(8,128)(2,1)S(1)} %constant_dynamic-update-slice_fusion), channel_id=1, source_target_pairs={{0,2},{1,3},{2,0},{3,1},{4,6},{5,7},{6,4},{7,5},{8,10},{9,11},{10,... | collective-permute-start | bytes 393224 | tf_op jit(solution)/shard_map/ppermute | solution.py:41
  72.8 8.4 %collective-permute-done.15 = bf16[64,1024]{1,0:T(8,128)(2,1)S(1)} collective-permute-done((bf16[64,1024]{1,0:T(8,128)(2,1)S(1)}, bf16[64,1024]{1,0:T(8,128)(2,1)S(1)}, u32[]{:S(2)}, u32[]{:S(2)}) %collective-permute-start.15) | collective-permute-done | bytes 131104 | tf_op jit(solution)/shard_map/ppermute | solution.py:41
  83.3 3.0 %collective-permute-start.20 = (bf16[64,1024]{1,0:T(8,128)(2,1)S(1)}, bf16[64,1024]{1,0:T(8,128)(2,1)S(1)}, u32[]{:S(2)}, u32[]{:S(2)}) collective-permute-start(bf16[64,1024]{1,0:T(8,128)(2,1)S(1)} %multiply_convert_fusion.7), channel_id=1, source_target_pairs={{0,1},{1,0},{2,3},{3,2},{4,5},{5,4},{6,7},{7,6},{8,9},{9,8},{10,11... | collective-permute-start | bytes 393224 | tf_op jit(solution)/shard_map/ppermute | solution.py:41
  86.4 2.4 %collective-permute-start.22 = (bf16[64,1024]{1,0:T(8,128)(2,1)S(1)}, bf16[64,1024]{1,0:T(8,128)(2,1)S(1)}, u32[]{:S(2)}, u32[]{:S(2)}) collective-permute-start(bf16[64,1024]{1,0:T(8,128)(2,1)S(1)} %multiply_convert_fusion.7), channel_id=1, source_target_pairs={{0,3},{1,2},{2,1},{3,0},{4,7},{5,6},{6,5},{7,4},{8,11},{9,10},{10,... | collective-permute-start | bytes 393224 | tf_op jit(solution)/shard_map/ppermute | solution.py:41
  90.7 2.0 fusion.20
  92.7 6.4 %collective-permute-done.21 = bf16[64,1024]{1,0:T(8,128)(2,1)S(1)} collective-permute-done((bf16[64,1024]{1,0:T(8,128)(2,1)S(1)}, bf16[64,1024]{1,0:T(8,128)(2,1)S(1)}, u32[]{:S(2)}, u32[]{:S(2)}) %collective-permute-start.21) | collective-permute-done | bytes 131104 | tf_op jit(solution)/shard_map/ppermute | solution.py:41
  99.1 1.8 fusion.25
  100.9 1.8 convolution_add_fusion
  102.7 1.8 fusion.23
  104.5 1.8 convolution_add_fusion.2
  106.3 2.2 multiply_convert_fusion
  110.2 2.3 %pad_maximum_fusion = bf16[3,512,1152]{2,1,0:T(8,128)(2,1)} fusion(bf16[1,512,1152]{2,1,0:T(8,128)(2,1)S(1)} %fusion.2, bf16[1,512,1152]{2,1,0:T(8,128)(2,1)S(1)} %fusion.1, bf16[1,512,1152]{2,1,0:T(8,128)(2,1)S(1)} %fusion), kind=kLoop, calls=%fused_computation.1 | loop fusion | flops 3538944 | bytes 7077888 | tf_op jit(solution)/shard_map/stack | solution.py:282
  112.4 1.8 fusion.24
  114.3 1.8 fusion.22
  116.1 1.8 convolution_add_fusion.4
  117.9 1.8 convolution_add_fusion.3
  119.8 2.8 %collective-permute-start.23 = (bf16[64,1024]{1,0:T(8,128)(2,1)S(1)}, bf16[64,1024]{1,0:T(8,128)(2,1)S(1)}, u32[]{:S(2)}, u32[]{:S(2)}) collective-permute-start(bf16[64,1024]{1,0:T(8,128)(2,1)S(1)} %get-tuple-element.218), channel_id=1, source_target_pairs={{0,1},{1,0},{2,3},{3,2},{4,5},{5,4},{6,7},{7,6},{8,9},{9,8},{10,11... | collective-permute-start | bytes 393224 | tf_op jit(solution)/shard_map/ppermute | solution.py:41
  122.6 2.4 %collective-permute-start.25 = (bf16[64,1024]{1,0:T(8,128)(2,1)S(1)}, bf16[64,1024]{1,0:T(8,128)(2,1)S(1)}, u32[]{:S(2)}, u32[]{:S(2)}) collective-permute-start(bf16[64,1024]{1,0:T(8,128)(2,1)S(1)} %get-tuple-element.219), channel_id=1, source_target_pairs={{0,3},{1,2},{2,1},{3,0},{4,7},{5,6},{6,5},{7,4},{8,11},{9,10},{10,... | collective-permute-start | bytes 393224 | tf_op jit(solution)/shard_map/ppermute | solution.py:41
  126.7 1.2 collective-permute-done.23
  127.9 7.5 %collective-permute-done.24 = bf16[64,1024]{1,0:T(8,128)(2,1)S(1)} collective-permute-done((bf16[64,1024]{1,0:T(8,128)(2,1)S(1)}, bf16[64,1024]{1,0:T(8,128)(2,1)S(1)}, u32[]{:S(2)}, u32[]{:S(2)}) %collective-permute-start.24) | collective-permute-done | bytes 131104 | tf_op jit(solution)/shard_map/ppermute | solution.py:41
  137.4 3.2 %collective-permute-start.28 = (bf16[64,1024]{1,0:T(8,128)(2,1)S(1)}, bf16[64,1024]{1,0:T(8,128)(2,1)S(1)}, u32[]{:S(2)}, u32[]{:S(2)}) collective-permute-start(bf16[64,1024]{1,0:T(8,128)(2,1)S(1)} %fusion.101), channel_id=1, source_target_pairs={{0,2},{1,3},{2,0},{3,1},{4,6},{5,7},{6,4},{7,5},{8,10},{9,11},{10,... | collective-permute-start | bytes 393224 | tf_op jit(solution)/shard_map/ppermute | solution.py:41
  140.8 2.5 %convert_add_fusion = (f32[3,512,1152]{2,1,0:T(8,128)S(1)}, bf16[3,512,1152]{2,1,0:T(8,128)(2,1)S(1)}) fusion(bf16[3,512,1152]{2,1,0:T(8,128)(2,1)} %collective-permute-done.26, bf16[1,512,1152]{2,1,0:T(8,128)(2,1)S(1)} %fusion.5, bf16[1,512,1152]{2,1,0:T(8,128)(2,1)S(1)} %fusion.4, bf16[1,512,1152]{2,1,0:T(8,128)(2,1)S(1)} %fusion.3), kind=kLoop, calls=%fused_computation | loop fusion | flops 10616832 | bytes 17694720 | tf_op jit(solution)/shard_map/add | solution.py:127
  143.5 1.1 collective-permute-start.30
  144.6 1.2 collective-permute-start.31
  146.0 4.8 %collective-permute-done.28 = bf16[64,1024]{1,0:T(8,128)(2,1)S(1)} collective-permute-done((bf16[64,1024]{1,0:T(8,128)(2,1)S(1)}, bf16[64,1024]{1,0:T(8,128)(2,1)S(1)}, u32[]{:S(2)}, u32[]{:S(2)}) %collective-permute-start.28) | collective-permute-done | bytes 131104 | tf_op jit(solution)/shard_map/ppermute | solution.py:41
  151.0 3.4 %collective-permute-done.30 = bf16[3,64,1152]{2,1,0:T(8,128)(2,1)S(1)} collective-permute-done((bf16[3,64,1152]{2,1,0:T(8,128)(2,1)S(1)}, bf16[3,64,1152]{2,1,0:T(8,128)(2,1)S(1)}, u32[]{:S(2)}, u32[]{:S(2)}) %collective-permute-start.30) | collective-permute-done | bytes 442400 | tf_op jit(solution)/shard_map/ppermute | solution.py:41
  156.5 1.5 collective-permute-start.32
  158.3 1.9 collective-permute-start.40
  160.3 1.3 collective-permute-start.39
  161.6 1.8 fusion.19
  163.4 1.8 fusion.21
  165.4 1.8 collective-permute-start.36
  171.7 2.9 %collective-permute-start.38 = (bf16[64,1024]{1,0:T(8,128)(2,1)S(1)}, bf16[64,1024]{1,0:T(8,128)(2,1)S(1)}, u32[]{:S(2)}, u32[]{:S(2)}) collective-permute-start(bf16[64,1024]{1,0:T(8,128)(2,1)S(1)} %get-tuple-element.212), channel_id=1, source_target_pairs={{0,3},{1,2},{2,1},{3,0},{4,7},{5,6},{6,5},{7,4},{8,11},{9,10},{10,... | collective-permute-start | bytes 393224 | tf_op jit(solution)/shard_map/ppermute | solution.py:41
  174.5 7.5 %collective-permute-done.37 = bf16[64,1024]{1,0:T(8,128)(2,1)S(1)} collective-permute-done((bf16[64,1024]{1,0:T(8,128)(2,1)S(1)}, bf16[64,1024]{1,0:T(8,128)(2,1)S(1)}, u32[]{:S(2)}, u32[]{:S(2)}) %collective-permute-start.37) | collective-permute-done | bytes 131104 | tf_op jit(solution)/shard_map/ppermute | solution.py:41
  183.0 7.5 %collective-permute-done.34 = bf16[64,1024]{1,0:T(8,128)(2,1)S(1)} collective-permute-done((bf16[64,1024]{1,0:T(8,128)(2,1)S(1)}, bf16[64,1024]{1,0:T(8,128)(2,1)S(1)}, u32[]{:S(2)}, u32[]{:S(2)}) %collective-permute-start.34) | collective-permute-done | bytes 131104 | tf_op jit(solution)/shard_map/ppermute | solution.py:41
  190.6 4.9 %collective-permute-done.33 = bf16[64,1024]{1,0:T(8,128)(2,1)S(1)} collective-permute-done((bf16[64,1024]{1,0:T(8,128)(2,1)S(1)}, bf16[64,1024]{1,0:T(8,128)(2,1)S(1)}, u32[]{:S(2)}, u32[]{:S(2)}) %collective-permute-start.33) | collective-permute-done | bytes 131104 | tf_op jit(solution)/shard_map/ppermute | solution.py:41
  196.0 1.1 slice.226
  198.6 2.0 collective-permute-start.42
  200.6 2.4 %collective-permute-start.44 = (f32[5,1024]{1,0:T(8,128)}, f32[5,1024]{1,0:T(8,128)}, u32[]{:S(2)}, u32[]{:S(2)}) collective-permute-start(f32[5,1024]{1,0:T(8,128)} %pad_maximum_fusion.15), channel_id=1, source_target_pairs={{0,1},{1,0},{2,3},{3,2},{4,5},{5,4},{6,7},{7,6},{8,9},{9,8},{10,11... | collective-permute-start | bytes 61448 | tf_op jit(solution)/shard_map/ppermute | solution.py:41
  203.0 1.0 copy.26
  204.1 1.5 fusion.102
  206.3 2.7 %collective-permute-start.54 = (bf16[4,64,256]{2,1,0:T(8,128)(2,1)S(1)}, bf16[4,64,256]{2,1,0:T(8,128)(2,1)S(1)}, u32[]{:S(2)}, u32[]{:S(2)}) collective-permute-start(bf16[4,64,256]{2,1,0:T(8,128)(2,1)S(1)} %get-tuple-element.205), channel_id=1, source_target_pairs={{0,8},{4,12},{8,0},{12,4},{16,24},{20,28},{24,16},{28,20},{1,9},{5... | collective-permute-start | bytes 393224 | tf_op jit(solution)/shard_map/ppermute | solution.py:41
  211.0 2.1 collective-permute-start.47
  213.2 1.9 collective-permute-start.48
  215.8 1.4 collective-permute-start.51
  217.7 1.4 collective-permute-start.55
  220.5 5.0 %collective-permute-done.53 = bf16[4,128,256]{2,1,0:T(8,128)(2,1)S(1)} collective-permute-done((bf16[4,128,256]{2,1,0:T(8,128)(2,1)S(1)}, bf16[4,128,256]{2,1,0:T(8,128)(2,1)S(1)}, u32[]{:S(2)}, u32[]{:S(2)}) %collective-permute-start.53) | collective-permute-done | bytes 262176 | tf_op jit(solution)/shard_map/ppermute | solution.py:41
  (363 shorter events, 48.4 us)
Async XLA Ops:
  4.8 67.5 %copy-start.2 = (bf16[64,1024]{1,0:T(8,128)(2,1)}, bf16[64,1024]{1,0:T(8,128)(2,1)S(1)}, u32[]{:S(2)}) copy-start(bf16[64,1024]{1,0:T(8,128)(2,1)S(1)} %constant_dynamic-update-slice_fusion.8) | copy-start | bytes 393220
  5.0 13.9 %collective-permute-start = (bf16[64,1024]{1,0:T(8,128)(2,1)S(1)}, bf16[64,1024]{1,0:T(8,128)(2,1)S(1)}, u32[]{:S(2)}, u32[]{:S(2)}) collective-permute-start(bf16[64,1024]{1,0:T(8,128)(2,1)S(1)} %fusion.33), channel_id=1, source_target_pairs={{0,1},{1,0},{2,3},{3,2},{4,5},{5,4},{6,7},{7,6},{8,9},{9,8},{10,11... | collective-permute-start | bytes 393224 | tf_op jit(solution)/shard_map/ppermute | solution.py:41
  8.1 13.0 %collective-permute-start.1 = (bf16[64,1024]{1,0:T(8,128)(2,1)S(1)}, bf16[64,1024]{1,0:T(8,128)(2,1)}, u32[]{:S(2)}, u32[]{:S(2)}) collective-permute-start(bf16[64,1024]{1,0:T(8,128)(2,1)S(1)} %fusion.33), channel_id=1, source_target_pairs={{0,2},{1,3},{2,0},{3,1},{4,6},{5,7},{6,4},{7,5},{8,10},{9,11},{10,... | collective-permute-start | bytes 393224 | tf_op jit(solution)/shard_map/ppermute | solution.py:41
  10.7 10.4 %collective-permute-start.2 = (bf16[64,1024]{1,0:T(8,128)(2,1)S(1)}, bf16[64,1024]{1,0:T(8,128)(2,1)}, u32[]{:S(2)}, u32[]{:S(2)}) collective-permute-start(bf16[64,1024]{1,0:T(8,128)(2,1)S(1)} %fusion.33), channel_id=1, source_target_pairs={{0,3},{1,2},{2,1},{3,0},{4,7},{5,6},{6,5},{7,4},{8,11},{9,10},{10,... | collective-permute-start | bytes 393224 | tf_op jit(solution)/shard_map/ppermute | solution.py:41
  13.3 7.8 %collective-permute-start.3 = (bf16[4,128,256]{2,1,0:T(8,128)(2,1)}, bf16[4,128,256]{2,1,0:T(8,128)(2,1)}, u32[]{:S(2)}, u32[]{:S(2)}) collective-permute-start(bf16[4,128,256]{2,1,0:T(8,128)(2,1)} %get-tuple-element.229), channel_id=1, source_target_pairs={{0,8},{4,12},{8,0},{12,4},{16,24},{20,28},{24,16},{28,20},{1,9},{5... | collective-permute-start | bytes 786440 | tf_op jit(solution)/shard_map/ppermute | solution.py:41
  15.1 7.3 %collective-permute-start.4 = (bf16[4,128,256]{2,1,0:T(8,128)(2,1)}, bf16[4,128,256]{2,1,0:T(8,128)(2,1)}, u32[]{:S(2)}, u32[]{:S(2)}) collective-permute-start(bf16[4,128,256]{2,1,0:T(8,128)(2,1)} %get-tuple-element.229), channel_id=1, source_target_pairs={{0,16},{4,20},{8,24},{12,28},{16,0},{20,4},{24,8},{28,12},{1,17},{... | collective-permute-start | bytes 786440 | tf_op jit(solution)/shard_map/ppermute | solution.py:41
  16.8 72.0 %copy-start.14 = (bf16[64,1024]{1,0:T(8,128)(2,1)}, bf16[64,1024]{1,0:T(8,128)(2,1)S(1)}, u32[]{:S(2)}) copy-start(bf16[64,1024]{1,0:T(8,128)(2,1)S(1)} %constant_dynamic-update-slice_fusion) | copy-start | bytes 393220
  18.1 20.4 %copy-start.47 = (f32[256]{0:T(256)}, f32[256]{0:T(256)S(1)}, u32[]{:S(2)}) copy-start(f32[256]{0:T(256)S(1)} %get-tuple-element.239) | copy-start | bytes 3076
  18.1 20.4 %copy-start.49 = (f32[256]{0:T(256)}, f32[256]{0:T(256)S(1)}, u32[]{:S(2)}) copy-start(f32[256]{0:T(256)S(1)} %get-tuple-element.245) | copy-start | bytes 3076
  19.0 19.5 %copy-start.44 = (f32[1,256]{1,0:T(1,128)}, f32[1,256]{1,0:T(1,128)S(1)}, u32[]{:S(2)}) copy-start(f32[1,256]{1,0:T(1,128)S(1)} %get-tuple-element.235) | copy-start | bytes 3076
  23.3 5.0 %collective-permute-start.5 = (bf16[4,64,256]{2,1,0:T(8,128)(2,1)S(1)}, bf16[4,64,256]{2,1,0:T(8,128)(2,1)S(1)}, u32[]{:S(2)}, u32[]{:S(2)}) collective-permute-start(bf16[4,64,256]{2,1,0:T(8,128)(2,1)S(1)} %split.361), channel_id=1, source_target_pairs={{0,16},{4,20},{8,24},{12,28},{16,0},{20,4},{24,8},{28,12},{1,17},{... | collective-permute-start | bytes 393224 | tf_op jit(solution)/shard_map/ppermute | solution.py:41
  25.8 5.0 %collective-permute-start.6 = (bf16[4,64,256]{2,1,0:T(8,128)(2,1)S(1)}, bf16[4,64,256]{2,1,0:T(8,128)(2,1)S(1)}, u32[]{:S(2)}, u32[]{:S(2)}) collective-permute-start(bf16[4,64,256]{2,1,0:T(8,128)(2,1)S(1)} %split.362), channel_id=1, source_target_pairs={{0,8},{4,12},{8,0},{12,4},{16,24},{20,28},{24,16},{28,20},{1,9},{5... | collective-permute-start | bytes 393224 | tf_op jit(solution)/shard_map/ppermute | solution.py:41
  30.8 3.7 %collective-permute-start.7 = (bf16[4,512,256]{2,1,0:T(8,128)(2,1)S(1)}, bf16[4,512,256]{2,1,0:T(8,128)(2,1)S(1)}, u32[]{:S(2)}, u32[]{:S(2)}) collective-permute-start(bf16[4,512,256]{2,1,0:T(8,128)(2,1)S(1)} %constant_dynamic-update-slice_fusion.17), channel_id=1, source_target_pairs={{0,4},{4,0},{8,12},{12,8},{16,20},{20,16},{24,28},{28,24},{1,5},{5... | collective-permute-start | bytes 3145736 | tf_op jit(solution)/shard_map/ppermute | solution.py:41
  32.0 22.1 %collective-permute-start.10 = (bf16[3,128,1152]{2,1,0:T(8,128)(2,1)S(1)}, bf16[3,128,1152]{2,1,0:T(8,128)(2,1)S(1)}, u32[]{:S(2)}, u32[]{:S(2)}) collective-permute-start(bf16[3,128,1152]{2,1,0:T(8,128)(2,1)S(1)} %pad_maximum_fusion.4), channel_id=1, source_target_pairs={{0,16},{4,20},{8,24},{12,28},{16,0},{20,4},{24,8},{28,12},{1,17},{... | collective-permute-start | bytes 2654216 | tf_op jit(solution)/shard_map/ppermute | solution.py:41
  32.6 21.8 %collective-permute-start.9 = (bf16[3,128,1152]{2,1,0:T(8,128)(2,1)S(1)}, bf16[3,128,1152]{2,1,0:T(8,128)(2,1)S(1)}, u32[]{:S(2)}, u32[]{:S(2)}) collective-permute-start(bf16[3,128,1152]{2,1,0:T(8,128)(2,1)S(1)} %pad_maximum_fusion.4), channel_id=1, source_target_pairs={{0,8},{4,12},{8,0},{12,4},{16,24},{20,28},{24,16},{28,20},{1,9},{5... | collective-permute-start | bytes 2654216 | tf_op jit(solution)/shard_map/ppermute | solution.py:41
  34.6 20.0 %copy-start.4 = (bf16[4,512,256]{2,1,0:T(8,128)(2,1)}, bf16[4,512,256]{2,1,0:T(8,128)(2,1)S(1)}, u32[]{:S(2)}) copy-start(bf16[4,512,256]{2,1,0:T(8,128)(2,1)S(1)} %collective-permute-done.7) | copy-start | bytes 3145732
  35.8 2.6 %collective-permute-start.8 = (bf16[2,256]{1,0:T(2,128)(2,1)S(1)}, bf16[2,256]{1,0:T(2,128)(2,1)S(1)}, u32[]{:S(2)}, u32[]{:S(2)}) collective-permute-start(bf16[2,256]{1,0:T(2,128)(2,1)S(1)} %slice.205), channel_id=1, source_target_pairs={{0,4},{4,8},{8,12},{12,16},{16,20},{20,24},{24,28},{1,5},{5,9},{9,... | collective-permute-start | bytes 3080 | tf_op jit(solution)/shard_map/ppermute | solution.py:12
  55.1 12.5 %collective-permute-start.12 = (bf16[64,1024]{1,0:T(8,128)(2,1)S(1)}, bf16[64,1024]{1,0:T(8,128)(2,1)S(1)}, u32[]{:S(2)}, u32[]{:S(2)}) collective-permute-start(bf16[64,1024]{1,0:T(8,128)(2,1)S(1)} %get-tuple-element.209), channel_id=1, source_target_pairs={{0,2},{1,3},{2,0},{3,1},{4,6},{5,7},{6,4},{7,5},{8,10},{9,11},{10,... | collective-permute-start | bytes 393224 | tf_op jit(solution)/shard_map/ppermute | solution.py:41
  56.9 10.7 %collective-permute-start.13 = (bf16[64,1024]{1,0:T(8,128)(2,1)S(1)}, bf16[64,1024]{1,0:T(8,128)(2,1)S(1)}, u32[]{:S(2)}, u32[]{:S(2)}) collective-permute-start(bf16[64,1024]{1,0:T(8,128)(2,1)S(1)} %get-tuple-element.210), channel_id=1, source_target_pairs={{0,3},{1,2},{2,1},{3,0},{4,7},{5,6},{6,5},{7,4},{8,11},{9,10},{10,... | collective-permute-start | bytes 393224 | tf_op jit(solution)/shard_map/ppermute | solution.py:41
  58.8 12.8 %collective-permute-start.11 = (bf16[64,1024]{1,0:T(8,128)(2,1)S(1)}, bf16[64,1024]{1,0:T(8,128)(2,1)S(1)}, u32[]{:S(2)}, u32[]{:S(2)}) collective-permute-start(bf16[64,1024]{1,0:T(8,128)(2,1)S(1)} %get-tuple-element.161), channel_id=1, source_target_pairs={{0,1},{1,0},{2,3},{3,2},{4,5},{5,4},{6,7},{7,6},{8,9},{9,8},{10,11... | collective-permute-start | bytes 393224 | tf_op jit(solution)/shard_map/ppermute | solution.py:41
  59.3 22.0 %collective-permute-start.17 = (bf16[3,64,1152]{2,1,0:T(8,128)(2,1)S(1)}, bf16[3,64,1152]{2,1,0:T(8,128)(2,1)S(1)}, u32[]{:S(2)}, u32[]{:S(2)}) collective-permute-start(bf16[3,64,1152]{2,1,0:T(8,128)(2,1)S(1)} %split.368), channel_id=1, source_target_pairs={{0,16},{4,20},{8,24},{12,28},{16,0},{20,4},{24,8},{28,12},{1,17},{... | collective-permute-start | bytes 1327112 | tf_op jit(solution)/shard_map/ppermute | solution.py:41
  61.6 19.6 %collective-permute-start.18 = (bf16[3,64,1152]{2,1,0:T(8,128)(2,1)S(1)}, bf16[3,64,1152]{2,1,0:T(8,128)(2,1)S(1)}, u32[]{:S(2)}, u32[]{:S(2)}) collective-permute-start(bf16[3,64,1152]{2,1,0:T(8,128)(2,1)S(1)} %split.369), channel_id=1, source_target_pairs={{0,8},{4,12},{8,0},{12,4},{16,24},{20,28},{24,16},{28,20},{1,9},{5... | collective-permute-start | bytes 1327112 | tf_op jit(solution)/shard_map/ppermute | solution.py:41
  67.6 5.2 %collective-permute-start.14 = (bf16[64,1024]{1,0:T(8,128)(2,1)S(1)}, bf16[64,1024]{1,0:T(8,128)(2,1)S(1)}, u32[]{:S(2)}, u32[]{:S(2)}) collective-permute-start(bf16[64,1024]{1,0:T(8,128)(2,1)S(1)} %constant_dynamic-update-slice_fusion), channel_id=1, source_target_pairs={{0,1},{1,0},{2,3},{3,2},{4,5},{5,4},{6,7},{7,6},{8,9},{9,8},{10,11... | collective-permute-start | bytes 393224 | tf_op jit(solution)/shard_map/ppermute | solution.py:41
  67.6 13.6 %collective-permute-start.15 = (bf16[64,1024]{1,0:T(8,128)(2,1)S(1)}, bf16[64,1024]{1,0:T(8,128)(2,1)S(1)}, u32[]{:S(2)}, u32[]{:S(2)}) collective-permute-start(bf16[64,1024]{1,0:T(8,128)(2,1)S(1)} %constant_dynamic-update-slice_fusion), channel_id=1, source_target_pairs={{0,2},{1,3},{2,0},{3,1},{4,6},{5,7},{6,4},{7,5},{8,10},{9,11},{10,... | collective-permute-start | bytes 393224 | tf_op jit(solution)/shard_map/ppermute | solution.py:41
  71.6 9.7 %collective-permute-start.16 = (bf16[64,1024]{1,0:T(8,128)(2,1)S(1)}, bf16[64,1024]{1,0:T(8,128)(2,1)S(1)}, u32[]{:S(2)}, u32[]{:S(2)}) collective-permute-start(bf16[64,1024]{1,0:T(8,128)(2,1)S(1)} %constant_dynamic-update-slice_fusion), channel_id=1, source_target_pairs={{0,3},{1,2},{2,1},{3,0},{4,7},{5,6},{6,5},{7,4},{8,11},{9,10},{10,... | collective-permute-start | bytes 393224 | tf_op jit(solution)/shard_map/ppermute | solution.py:41
  82.9 16.2 %collective-permute-start.19 = (bf16[3,512,1152]{2,1,0:T(8,128)(2,1)}, bf16[3,512,1152]{2,1,0:T(8,128)(2,1)}, u32[]{:S(2)}, u32[]{:S(2)}) collective-permute-start(bf16[3,512,1152]{2,1,0:T(8,128)(2,1)} %constant_dynamic-update-slice_fusion.27), channel_id=1, source_target_pairs={{0,4},{4,0},{8,12},{12,8},{16,20},{20,16},{24,28},{28,24},{1,5},{5... | collective-permute-start | bytes 10616840 | tf_op jit(solution)/shard_map/ppermute | solution.py:41
  83.1 52.6 %copy-start.25 = (f32[1024]{0:T(1024)}, f32[1024]{0:T(1024)S(1)}, u32[]{:S(2)}) copy-start(f32[1024]{0:T(1024)S(1)} %constant_dynamic-update-slice_fusion.63) | copy-start | bytes 12292
  83.2 52.5 %copy-start.37 = (f32[64]{0:T(128)}, f32[64]{0:T(128)S(1)}, u32[]{:S(2)}) copy-start(f32[64]{0:T(128)S(1)} %add_rsqrt_fusion) | copy-start | bytes 772
  83.3 9.4 %collective-permute-start.20 = (bf16[64,1024]{1,0:T(8,128)(2,1)S(1)}, bf16[64,1024]{1,0:T(8,128)(2,1)S(1)}, u32[]{:S(2)}, u32[]{:S(2)}) collective-permute-start(bf16[64,1024]{1,0:T(8,128)(2,1)S(1)} %multiply_convert_fusion.7), channel_id=1, source_target_pairs={{0,1},{1,0},{2,3},{3,2},{4,5},{5,4},{6,7},{7,6},{8,9},{9,8},{10,11... | collective-permute-start | bytes 393224 | tf_op jit(solution)/shard_map/ppermute | solution.py:41
  86.4 12.7 %collective-permute-start.21 = (bf16[64,1024]{1,0:T(8,128)(2,1)S(1)}, bf16[64,1024]{1,0:T(8,128)(2,1)S(1)}, u32[]{:S(2)}, u32[]{:S(2)}) collective-permute-start(bf16[64,1024]{1,0:T(8,128)(2,1)S(1)} %multiply_convert_fusion.7), channel_id=1, source_target_pairs={{0,2},{1,3},{2,0},{3,1},{4,6},{5,7},{6,4},{7,5},{8,10},{9,11},{10,... | collective-permute-start | bytes 393224 | tf_op jit(solution)/shard_map/ppermute | solution.py:41
  86.4 12.7 %collective-permute-start.22 = (bf16[64,1024]{1,0:T(8,128)(2,1)S(1)}, bf16[64,1024]{1,0:T(8,128)(2,1)S(1)}, u32[]{:S(2)}, u32[]{:S(2)}) collective-permute-start(bf16[64,1024]{1,0:T(8,128)(2,1)S(1)} %multiply_convert_fusion.7), channel_id=1, source_target_pairs={{0,3},{1,2},{2,1},{3,0},{4,7},{5,6},{6,5},{7,4},{8,11},{9,10},{10,... | collective-permute-start | bytes 393224 | tf_op jit(solution)/shard_map/ppermute | solution.py:41
  112.4 23.0 %collective-permute-start.26 = (bf16[3,512,1152]{2,1,0:T(8,128)(2,1)}, bf16[3,512,1152]{2,1,0:T(8,128)(2,1)}, u32[]{:S(2)}, u32[]{:S(2)}) collective-permute-start(bf16[3,512,1152]{2,1,0:T(8,128)(2,1)} %pad_maximum_fusion), channel_id=1, source_target_pairs={{0,4},{4,0},{8,12},{12,8},{16,20},{20,16},{24,28},{28,24},{1,5},{5... | collective-permute-start | bytes 10616840 | tf_op jit(solution)/shard_map/ppermute | solution.py:41
  119.8 8.1 %collective-permute-start.23 = (bf16[64,1024]{1,0:T(8,128)(2,1)S(1)}, bf16[64,1024]{1,0:T(8,128)(2,1)S(1)}, u32[]{:S(2)}, u32[]{:S(2)}) collective-permute-start(bf16[64,1024]{1,0:T(8,128)(2,1)S(1)} %get-tuple-element.218), channel_id=1, source_target_pairs={{0,1},{1,0},{2,3},{3,2},{4,5},{5,4},{6,7},{7,6},{8,9},{9,8},{10,11... | collective-permute-start | bytes 393224 | tf_op jit(solution)/shard_map/ppermute | solution.py:41
  122.6 12.8 %collective-permute-start.24 = (bf16[64,1024]{1,0:T(8,128)(2,1)S(1)}, bf16[64,1024]{1,0:T(8,128)(2,1)S(1)}, u32[]{:S(2)}, u32[]{:S(2)}) collective-permute-start(bf16[64,1024]{1,0:T(8,128)(2,1)S(1)} %get-tuple-element.220), channel_id=1, source_target_pairs={{0,2},{1,3},{2,0},{3,1},{4,6},{5,7},{6,4},{7,5},{8,10},{9,11},{10,... | collective-permute-start | bytes 393224 | tf_op jit(solution)/shard_map/ppermute | solution.py:41
  122.6 12.8 %collective-permute-start.25 = (bf16[64,1024]{1,0:T(8,128)(2,1)S(1)}, bf16[64,1024]{1,0:T(8,128)(2,1)S(1)}, u32[]{:S(2)}, u32[]{:S(2)}) collective-permute-start(bf16[64,1024]{1,0:T(8,128)(2,1)S(1)} %get-tuple-element.219), channel_id=1, source_target_pairs={{0,3},{1,2},{2,1},{3,0},{4,7},{5,6},{6,5},{7,4},{8,11},{9,10},{10,... | collective-permute-start | bytes 393224 | tf_op jit(solution)/shard_map/ppermute | solution.py:41
  136.4 9.7 %collective-permute-start.27 = (bf16[64,1024]{1,0:T(8,128)(2,1)S(1)}, bf16[64,1024]{1,0:T(8,128)(2,1)S(1)}, u32[]{:S(2)}, u32[]{:S(2)}) collective-permute-start(bf16[64,1024]{1,0:T(8,128)(2,1)S(1)} %fusion.101), channel_id=1, source_target_pairs={{0,3},{1,2},{2,1},{3,0},{4,7},{5,6},{6,5},{7,4},{8,11},{9,10},{10,... | collective-permute-start | bytes 393224 | tf_op jit(solution)/shard_map/ppermute | solution.py:41
  137.4 13.5 %collective-permute-start.28 = (bf16[64,1024]{1,0:T(8,128)(2,1)S(1)}, bf16[64,1024]{1,0:T(8,128)(2,1)S(1)}, u32[]{:S(2)}, u32[]{:S(2)}) collective-permute-start(bf16[64,1024]{1,0:T(8,128)(2,1)S(1)} %fusion.101), channel_id=1, source_target_pairs={{0,2},{1,3},{2,0},{3,1},{4,6},{5,7},{6,4},{7,5},{8,10},{9,11},{10,... | collective-permute-start | bytes 393224 | tf_op jit(solution)/shard_map/ppermute | solution.py:41
  140.6 10.3 %collective-permute-start.29 = (bf16[64,1024]{1,0:T(8,128)(2,1)S(1)}, bf16[64,1024]{1,0:T(8,128)(2,1)S(1)}, u32[]{:S(2)}, u32[]{:S(2)}) collective-permute-start(bf16[64,1024]{1,0:T(8,128)(2,1)S(1)} %fusion.101), channel_id=1, source_target_pairs={{0,1},{1,0},{2,3},{3,2},{4,5},{5,4},{6,7},{7,6},{8,9},{9,8},{10,11... | collective-permute-start | bytes 393224 | tf_op jit(solution)/shard_map/ppermute | solution.py:41
  143.5 10.8 %collective-permute-start.30 = (bf16[3,64,1152]{2,1,0:T(8,128)(2,1)S(1)}, bf16[3,64,1152]{2,1,0:T(8,128)(2,1)S(1)}, u32[]{:S(2)}, u32[]{:S(2)}) collective-permute-start(bf16[3,64,1152]{2,1,0:T(8,128)(2,1)S(1)} %get-tuple-element.195), channel_id=1, source_target_pairs={{0,8},{4,12},{8,0},{12,4},{16,24},{20,28},{24,16},{28,20},{1,9},{5... | collective-permute-start | bytes 1327112 | tf_op jit(solution)/shard_map/ppermute | solution.py:41
  144.6 10.5 %collective-permute-start.31 = (bf16[3,64,1152]{2,1,0:T(8,128)(2,1)S(1)}, bf16[3,64,1152]{2,1,0:T(8,128)(2,1)S(1)}, u32[]{:S(2)}, u32[]{:S(2)}) collective-permute-start(bf16[3,64,1152]{2,1,0:T(8,128)(2,1)S(1)} %get-tuple-element.194), channel_id=1, source_target_pairs={{0,16},{4,20},{8,24},{12,28},{16,0},{20,4},{24,8},{28,12},{1,17},{... | collective-permute-start | bytes 1327112 | tf_op jit(solution)/shard_map/ppermute | solution.py:41
  156.5 11.6 %collective-permute-start.32 = (bf16[2,256]{1,0:T(2,128)(2,1)S(1)}, bf16[2,256]{1,0:T(2,128)(2,1)S(1)}, u32[]{:S(2)}, u32[]{:S(2)}) collective-permute-start(bf16[2,256]{1,0:T(2,128)(2,1)S(1)} %slice.217), channel_id=1, source_target_pairs={{4,0},{8,4},{12,8},{16,12},{20,16},{24,20},{28,24},{5,1},{9,5},{13... | collective-permute-start | bytes 3080 | tf_op jit(solution)/shard_map/ppermute | solution.py:12
  158.3 37.3 %collective-permute-start.40 = (bf16[3,128,1152]{2,1,0:T(8,128)(2,1)S(1)}, bf16[3,128,1152]{2,1,0:T(8,128)(2,1)S(1)}, u32[]{:S(2)}, u32[]{:S(2)}) collective-permute-start(bf16[3,128,1152]{2,1,0:T(8,128)(2,1)S(1)} %pad_maximum_fusion.6), channel_id=1, source_target_pairs={{0,16},{4,20},{8,24},{12,28},{16,0},{20,4},{24,8},{28,12},{1,17},{... | collective-permute-start | bytes 2654216 | tf_op jit(solution)/shard_map/ppermute | solution.py:41
  160.3 35.3 %collective-permute-start.39 = (bf16[3,128,1152]{2,1,0:T(8,128)(2,1)S(1)}, bf16[3,128,1152]{2,1,0:T(8,128)(2,1)S(1)}, u32[]{:S(2)}, u32[]{:S(2)}) collective-permute-start(bf16[3,128,1152]{2,1,0:T(8,128)(2,1)S(1)} %pad_maximum_fusion.5), channel_id=1, source_target_pairs={{0,8},{4,12},{8,0},{12,4},{16,24},{20,28},{24,16},{28,20},{1,9},{5... | collective-permute-start | bytes 2654216 | tf_op jit(solution)/shard_map/ppermute | solution.py:41
  165.4 6.2 %collective-permute-start.36 = (bf16[64,1024]{1,0:T(8,128)(2,1)S(1)}, bf16[64,1024]{1,0:T(8,128)(2,1)S(1)}, u32[]{:S(2)}, u32[]{:S(2)}) collective-permute-start(bf16[64,1024]{1,0:T(8,128)(2,1)S(1)} %get-tuple-element.211), channel_id=1, source_target_pairs={{0,1},{1,0},{2,3},{3,2},{4,5},{5,4},{6,7},{7,6},{8,9},{9,8},{10,11... | collective-permute-start | bytes 393224 | tf_op jit(solution)/shard_map/ppermute | solution.py:41
  167.2 14.8 %collective-permute-start.37 = (bf16[64,1024]{1,0:T(8,128)(2,1)S(1)}, bf16[64,1024]{1,0:T(8,128)(2,1)S(1)}, u32[]{:S(2)}, u32[]{:S(2)}) collective-permute-start(bf16[64,1024]{1,0:T(8,128)(2,1)S(1)} %get-tuple-element.213), channel_id=1, source_target_pairs={{0,2},{1,3},{2,0},{3,1},{4,6},{5,7},{6,4},{7,5},{8,10},{9,11},{10,... | collective-permute-start | bytes 393224 | tf_op jit(solution)/shard_map/ppermute | solution.py:41
  169.7 25.9 %collective-permute-start.41 = (bf16[4,512,256]{2,1,0:T(8,128)(2,1)S(1)}, bf16[4,512,256]{2,1,0:T(8,128)(2,1)}, u32[]{:S(2)}, u32[]{:S(2)}) collective-permute-start(bf16[4,512,256]{2,1,0:T(8,128)(2,1)S(1)} %pad_maximum_fusion.3), channel_id=1, source_target_pairs={{0,4},{4,0},{8,12},{12,8},{16,20},{20,16},{24,28},{28,24},{1,5},{5... | collective-permute-start | bytes 3145736 | tf_op jit(solution)/shard_map/ppermute | solution.py:41
  171.7 11.4 %collective-permute-start.38 = (bf16[64,1024]{1,0:T(8,128)(2,1)S(1)}, bf16[64,1024]{1,0:T(8,128)(2,1)S(1)}, u32[]{:S(2)}, u32[]{:S(2)}) collective-permute-start(bf16[64,1024]{1,0:T(8,128)(2,1)S(1)} %get-tuple-element.212), channel_id=1, source_target_pairs={{0,3},{1,2},{2,1},{3,0},{4,7},{5,6},{6,5},{7,4},{8,11},{9,10},{10,... | collective-permute-start | bytes 393224 | tf_op jit(solution)/shard_map/ppermute | solution.py:41
  182.0 8.5 %collective-permute-start.34 = (bf16[64,1024]{1,0:T(8,128)(2,1)S(1)}, bf16[64,1024]{1,0:T(8,128)(2,1)S(1)}, u32[]{:S(2)}, u32[]{:S(2)}) collective-permute-start(bf16[64,1024]{1,0:T(8,128)(2,1)S(1)} %get-tuple-element.207), channel_id=1, source_target_pairs={{0,2},{1,3},{2,0},{3,1},{4,6},{5,7},{6,4},{7,5},{8,10},{9,11},{10,... | collective-permute-start | bytes 393224 | tf_op jit(solution)/shard_map/ppermute | solution.py:41
  183.0 7.6 %collective-permute-start.35 = (bf16[64,1024]{1,0:T(8,128)(2,1)S(1)}, bf16[64,1024]{1,0:T(8,128)(2,1)S(1)}, u32[]{:S(2)}, u32[]{:S(2)}) collective-permute-start(bf16[64,1024]{1,0:T(8,128)(2,1)S(1)} %get-tuple-element.208), channel_id=1, source_target_pairs={{0,3},{1,2},{2,1},{3,0},{4,7},{5,6},{6,5},{7,4},{8,11},{9,10},{10,... | collective-permute-start | bytes 393224 | tf_op jit(solution)/shard_map/ppermute | solution.py:41
  190.5 5.0 %collective-permute-start.33 = (bf16[64,1024]{1,0:T(8,128)(2,1)S(1)}, bf16[64,1024]{1,0:T(8,128)(2,1)S(1)}, u32[]{:S(2)}, u32[]{:S(2)}) collective-permute-start(bf16[64,1024]{1,0:T(8,128)(2,1)S(1)} %get-tuple-element.134), channel_id=1, source_target_pairs={{0,1},{1,0},{2,3},{3,2},{4,5},{5,4},{6,7},{7,6},{8,9},{9,8},{10,11... | collective-permute-start | bytes 393224 | tf_op jit(solution)/shard_map/ppermute | solution.py:41
  198.6 11.1 %collective-permute-start.42 = (f32[5,1024]{1,0:T(8,128)}, f32[5,1024]{1,0:T(8,128)}, u32[]{:S(2)}, u32[]{:S(2)}) collective-permute-start(f32[5,1024]{1,0:T(8,128)} %pad_maximum_fusion.15), channel_id=1, source_target_pairs={{0,3},{1,2},{2,1},{3,0},{4,7},{5,6},{6,5},{7,4},{8,11},{9,10},{10,... | collective-permute-start | bytes 61448 | tf_op jit(solution)/shard_map/ppermute | solution.py:41
  200.6 9.2 %collective-permute-start.43 = (f32[5,1024]{1,0:T(8,128)}, f32[5,1024]{1,0:T(8,128)}, u32[]{:S(2)}, u32[]{:S(2)}) collective-permute-start(f32[5,1024]{1,0:T(8,128)} %pad_maximum_fusion.15), channel_id=1, source_target_pairs={{0,2},{1,3},{2,0},{3,1},{4,6},{5,7},{6,4},{7,5},{8,10},{9,11},{10,... | collective-permute-start | bytes 61448 | tf_op jit(solution)/shard_map/ppermute | solution.py:41
  200.6 9.2 %collective-permute-start.44 = (f32[5,1024]{1,0:T(8,128)}, f32[5,1024]{1,0:T(8,128)}, u32[]{:S(2)}, u32[]{:S(2)}) collective-permute-start(f32[5,1024]{1,0:T(8,128)} %pad_maximum_fusion.15), channel_id=1, source_target_pairs={{0,1},{1,0},{2,3},{3,2},{4,5},{5,4},{6,7},{7,6},{8,9},{9,8},{10,11... | collective-permute-start | bytes 61448 | tf_op jit(solution)/shard_map/ppermute | solution.py:41
  205.7 7.5 %collective-permute-start.52 = (bf16[4,64,256]{2,1,0:T(8,128)(2,1)S(1)}, bf16[4,64,256]{2,1,0:T(8,128)(2,1)S(1)}, u32[]{:S(2)}, u32[]{:S(2)}) collective-permute-start(bf16[4,64,256]{2,1,0:T(8,128)(2,1)S(1)} %get-tuple-element.206), channel_id=1, source_target_pairs={{0,16},{4,20},{8,24},{12,28},{16,0},{20,4},{24,8},{28,12},{1,17},{... | collective-permute-start | bytes 393224 | tf_op jit(solution)/shard_map/ppermute | solution.py:41
  206.3 8.9 %collective-permute-start.54 = (bf16[4,64,256]{2,1,0:T(8,128)(2,1)S(1)}, bf16[4,64,256]{2,1,0:T(8,128)(2,1)S(1)}, u32[]{:S(2)}, u32[]{:S(2)}) collective-permute-start(bf16[4,64,256]{2,1,0:T(8,128)(2,1)S(1)} %get-tuple-element.205), channel_id=1, source_target_pairs={{0,8},{4,12},{8,0},{12,4},{16,24},{20,28},{24,16},{28,20},{1,9},{5... | collective-permute-start | bytes 393224 | tf_op jit(solution)/shard_map/ppermute | solution.py:41
  210.7 4.6 %collective-permute-start.45 = (f32[5,1024]{1,0:T(8,128)S(1)}, f32[5,1024]{1,0:T(8,128)S(1)}, u32[]{:S(2)}, u32[]{:S(2)}) collective-permute-start(f32[5,1024]{1,0:T(8,128)S(1)} %select_add_fusion.1), channel_id=1, source_target_pairs={{0,28},{4,24},{8,20},{12,16},{16,12},{20,8},{24,4},{28,0},{1,29},{... | collective-permute-start | bytes 61448 | tf_op jit(solution)/shard_map/ppermute | solution.py:41
  210.8 5.0 %collective-permute-start.46 = (f32[5,1024]{1,0:T(8,128)S(1)}, f32[5,1024]{1,0:T(8,128)S(1)}, u32[]{:S(2)}, u32[]{:S(2)}) collective-permute-start(f32[5,1024]{1,0:T(8,128)S(1)} %select_add_fusion.1), channel_id=1, source_target_pairs={{0,24},{4,28},{8,16},{12,20},{16,8},{20,12},{24,0},{28,4},{1,25},{... | collective-permute-start | bytes 61448 | tf_op jit(solution)/shard_map/ppermute | solution.py:41
  211.0 6.2 %collective-permute-start.47 = (f32[5,1024]{1,0:T(8,128)S(1)}, f32[5,1024]{1,0:T(8,128)S(1)}, u32[]{:S(2)}, u32[]{:S(2)}) collective-permute-start(f32[5,1024]{1,0:T(8,128)S(1)} %select_add_fusion.1), channel_id=1, source_target_pairs={{0,20},{4,16},{8,28},{12,24},{16,4},{20,0},{24,12},{28,8},{1,21},{... | collective-permute-start | bytes 61448 | tf_op jit(solution)/shard_map/ppermute | solution.py:41
  213.2 4.5 %collective-permute-start.48 = (f32[5,1024]{1,0:T(8,128)S(1)}, f32[5,1024]{1,0:T(8,128)S(1)}, u32[]{:S(2)}, u32[]{:S(2)}) collective-permute-start(f32[5,1024]{1,0:T(8,128)S(1)} %select_add_fusion.1), channel_id=1, source_target_pairs={{0,16},{4,20},{8,24},{12,28},{16,0},{20,4},{24,8},{28,12},{1,17},{... | collective-permute-start | bytes 61448 | tf_op jit(solution)/shard_map/ppermute | solution.py:41
  215.1 3.9 %collective-permute-start.49 = (f32[5,1024]{1,0:T(8,128)S(1)}, f32[5,1024]{1,0:T(8,128)S(1)}, u32[]{:S(2)}, u32[]{:S(2)}) collective-permute-start(f32[5,1024]{1,0:T(8,128)S(1)} %select_add_fusion.1), channel_id=1, source_target_pairs={{0,12},{4,8},{8,4},{12,0},{16,28},{20,24},{24,20},{28,16},{1,13},{... | collective-permute-start | bytes 61448 | tf_op jit(solution)/shard_map/ppermute | solution.py:41
  215.3 4.0 %collective-permute-start.50 = (f32[5,1024]{1,0:T(8,128)S(1)}, f32[5,1024]{1,0:T(8,128)S(1)}, u32[]{:S(2)}, u32[]{:S(2)}) collective-permute-start(f32[5,1024]{1,0:T(8,128)S(1)} %select_add_fusion.1), channel_id=1, source_target_pairs={{0,8},{4,12},{8,0},{12,4},{16,24},{20,28},{24,16},{28,20},{1,9},{5... | collective-permute-start | bytes 61448 | tf_op jit(solution)/shard_map/ppermute | solution.py:41
  215.8 3.5 %collective-permute-start.51 = (f32[5,1024]{1,0:T(8,128)S(1)}, f32[5,1024]{1,0:T(8,128)S(1)}, u32[]{:S(2)}, u32[]{:S(2)}) collective-permute-start(f32[5,1024]{1,0:T(8,128)S(1)} %select_add_fusion.1), channel_id=1, source_target_pairs={{0,4},{4,0},{8,12},{12,8},{16,20},{20,16},{24,28},{28,24},{1,5},{5... | collective-permute-start | bytes 61448 | tf_op jit(solution)/shard_map/ppermute | solution.py:41
  217.2 8.3 %collective-permute-start.53 = (bf16[4,128,256]{2,1,0:T(8,128)(2,1)S(1)}, bf16[4,128,256]{2,1,0:T(8,128)(2,1)S(1)}, u32[]{:S(2)}, u32[]{:S(2)}) collective-permute-start(bf16[4,128,256]{2,1,0:T(8,128)(2,1)S(1)} %pad_maximum_fusion.13), channel_id=1, source_target_pairs={{0,8},{4,12},{8,0},{12,4},{16,24},{20,28},{24,16},{28,20},{1,9},{5... | collective-permute-start | bytes 786440 | tf_op jit(solution)/shard_map/ppermute | solution.py:41
  217.7 8.2 %collective-permute-start.55 = (bf16[4,128,256]{2,1,0:T(8,128)(2,1)S(1)}, bf16[4,128,256]{2,1,0:T(8,128)(2,1)S(1)}, u32[]{:S(2)}, u32[]{:S(2)}) collective-permute-start(bf16[4,128,256]{2,1,0:T(8,128)(2,1)S(1)} %pad_maximum_fusion.14), channel_id=1, source_target_pairs={{0,16},{4,20},{8,24},{12,28},{16,0},{20,4},{24,8},{28,12},{1,17},{... | collective-permute-start | bytes 786440 | tf_op jit(solution)/shard_map/ppermute | solution.py:41
  (50 other events, 349.7 us)

commit v3 on v2

--- a/solution.py
+++ b/solution.py
@@ -218,21 +218,22 @@
     first_keep = first_all[:group_rows]
     second_keep = second_all[:group_rows]
     kernel = lax.dynamic_slice_in_dim(conv_weight, column, channels, 1)
-    residual = wide(to_relative(inputs))
-    first_gain = to_relative(first_gain)
-    second_gain = to_relative(second_gain)
-    cotangent = to_relative(cotangent)
-
     mixer_weights = jnp.concatenate([entry_projection_weight, out_weight.T[None]], axis=0)
+    mixer_weights, inputs, cotangent = lax.optimization_barrier(
+        (mixer_weights, inputs, cotangent)
+    )
+    mixer_gather = begin(gather_weight(mixer_weights))
     ffn_weights = jnp.concatenate([gate_up_weight, down_weight.T[None]], axis=0)
-    mixer_gather = begin(gather_weight(mixer_weights))
+    ffn_gather = begin(gather_weight(ffn_weights))
+    both = to_relative(jnp.concatenate([inputs, cotangent], axis=0))
+    residual, cotangent = wide(both[:own_rows]), both[own_rows:]
+    first_gain, second_gain = to_relative(jnp.stack([first_gain, second_gain]))
     normed_parts = gather_rows(narrow(rms_norm(residual, first_gain)))
     normed_parts, mixer_gather = beside(normed_parts, mixer_gather)
-    ffn_weights, mixer_gather = beside(ffn_weights, mixer_gather)
-    ffn_gather = begin(gather_weight(ffn_weights))
     grad_parts = gather_rows(cotangent)
     mixer_near, mixer_far = finish(*mixer_gather)
     normed = in_token_order(normed_parts)
+    normed, grad_parts = lax.optimization_barrier((normed, grad_parts))
 
     normed_near, normed_far = halves(normed)
     projected = [
@@ -253,7 +254,7 @@
         [times_trans(gated, mixer_near[3]), times_trans(gated, mixer_far[3])], axis=1
     )
     middle = residual + scatter_rows(for_owners(mixer_part))
-    (middle, grad_parts), ffn_gather = beside((middle, grad_parts), ffn_gather)
+    middle, ffn_gather = beside(middle, ffn_gather)
     grad_rows = jnp.concatenate(grad_parts, axis=0)
     hidden_in = jnp.concatenate(
         gather_rows(narrow(rms_norm(middle, second_gain))), axis=0
@@ -266,6 +267,12 @@
     swish = gate_value * sigmoid
     hidden = narrow(swish * up_value)
     grad_near, grad_far = halves(grad_rows)
+    ffn_part = jnp.concatenate(
+        [times_trans(hidden, ffn_near[2]), times_trans(hidden, ffn_far[2])], axis=1
+    )
+    output = narrow(
+        middle + scatter_rows(jnp.split(ffn_part, lax.axis_size("tensor"), axis=0))
+    )
     grad_hidden = dot(grad_near, ffn_near[2]) + dot(grad_far, ffn_far[2])
     grad_gate = narrow(grad_hidden * up_value * sigmoid * (1.0 + gate_value * (1.0 - sigmoid)))
     grad_up = narrow(grad_hidden * swish)
@@ -290,18 +297,13 @@
             ]
         )
     )
+    hidden_back, output = lax.optimization_barrier((hidden_back, output))
     grad_hin = scatter_rows(jnp.split(hidden_back, lax.axis_size("tensor"), axis=0))
     grad_hin, ffn_scatter = beside(grad_hin, ffn_scatter)
     second_back, second_part = rms_back(middle, second_gain, grad_hin)
     grad_middle = wide(cotangent) + second_back
     branch_rows = in_token_order(gather_rows(narrow(grad_middle)))
-    (branch_rows, hidden), ffn_scatter = beside((branch_rows, hidden), ffn_scatter)
-    ffn_part = jnp.concatenate(
-        [times_trans(hidden, ffn_near[2]), times_trans(hidden, ffn_far[2])], axis=1
-    )
-    output = narrow(
-        middle + scatter_rows(jnp.split(ffn_part, lax.axis_size("tensor"), axis=0))
-    )
+    branch_rows, ffn_scatter = beside(branch_rows, ffn_scatter)
     branch_near, branch_far = halves(branch_rows)
     grad_gated = dot(branch_near, mixer_near[3]) + dot(branch_far, mixer_far[3])
     output_gate_gradient = narrow(grad_gated * mixed)
@@ -346,17 +348,17 @@
         axis=1,
     )
     grad_normed = scatter_rows(for_owners(normed_back))
-    (grad_normed, output), ffn_scatter, mixer_scatter = beside(
-        (grad_normed, output), ffn_scatter, mixer_scatter
-    )
+    grad_normed, ffn_scatter, mixer_scatter = beside(grad_normed, ffn_scatter, mixer_scatter)
     first_back, first_part = rms_back(residual, first_gain, grad_normed)
     input_grad = grad_middle + first_back
+    small = jnp.concatenate(
+        [to_absolute(first_part)[None], to_absolute(second_part)[None], kernel_full], axis=0
+    )
+    small = summed_over(small, "tensor")
+    small, mixer_scatter = beside(small, mixer_scatter)
+    small = summed_over(small, "dp")
     ffn_grad = finish(*ffn_scatter)
     mixer_grad = finish(*mixer_scatter)
-    small = jnp.concatenate(
-        [to_absolute(first_part)[None], to_absolute(second_part)[None], kernel_full], axis=0
-    )
-    small = summed_over(summed_over(small, "tensor"), "dp")
     return (
         to_absolute(output),
         to_absolute(input_grad),

time: 229 us -> 223 us (0.974)
  starting transfers between devices: 68.7 us -> 78.2 us
  other arithmetic: 19.7 us -> 12.3 us
  waiting for transfers between devices: 83.7 us -> 78.3 us
    ppermute x54, starting transfers between devices: 65.4 us -> 74.7 us  [swapped(): return lax.ppermute(block, axis, [(i, i ^ mask) for i in devices])]
    ppermute x54, waiting for transfers between devices: 83.1 us -> 77.9 us  [swapped(): return lax.ppermute(block, axis, [(i, i ^ mask) for i in devices])]
    unnamed x60 -> x44, other arithmetic: 4.62 us -> 1.69 us
    unnamed x128 -> x77, local copies, waits for them, and re-layouts: 9.58 us -> 8.79 us
  transfers between devices with their start and end apart: 56 -> 56, of which waited for: 23 -> 26; matrix products, arithmetic and copies ran while one was open for 20% -> 14% of each run, Pallas kernels for 0% -> 0%
where the time goes in v3:
time: 223 us; the launch traced here: 222 us
  waiting for transfers between devices  78.3 us (35%)
  starting transfers between devices  78.2 us (35%)
  matrix products  32.8 us (15%)
  local copies, waits for them, and re-layouts  18.3 us (8%)
  other arithmetic  12.3 us (6%)
    ppermute x54, waiting for transfers between devices, swapped(): return lax.ppermute(block, axis, [(i, i ^ mask) for i in devices])  77.9 us
    ppermute x54, starting transfers between devices, swapped(): return lax.ppermute(block, axis, [(i, i ^ mask) for i in devices])  74.7 us
    dot_general x14, matrix products, dot(): return jnp.dot(left, right, preferred_element_type=jnp.float32)  14.5 us
    dot_general x14, matrix products, times_trans(): lax.dot_general(left, right, (((1,), (1,)), ((), ())), preferred_element_...  12.9 us
    unnamed x77, local copies, waits for them, and re-layouts  8.79 us
    dot_general x14, matrix products, trans_times(): lax.dot_general(left, right, (((0,), (0,)), ((), ())), preferred_element_...  5.45 us
  transfers between devices with their start and end apart: 56, of which 26 were waited for; matrix products, arithmetic and copies ran while one was open for 14% of the time, Pallas kernels for 0%

profile of v3, /device:TPU:0, one launch (start us, length us, event | category | flops | bytes accessed | tf_op | source)
XLA Modules:
  0.0 222.0 jit_solution(4890632110873785085)
XLA Ops:
  6.1 3.1 %collective-permute-start = (bf16[64,1024]{1,0:T(8,128)(2,1)S(1)}, bf16[64,1024]{1,0:T(8,128)(2,1)S(1)}, u32[]{:S(2)}, u32[]{:S(2)}) collective-permute-start(bf16[64,1024]{1,0:T(8,128)(2,1)S(1)} %fusion.33), channel_id=1, source_target_pairs={{0,1},{1,0},{2,3},{3,2},{4,5},{5,4},{6,7},{7,6},{8,9},{9,8},{10,11... | collective-permute-start | bytes 393224 | tf_op jit(solution)/shard_map/ppermute | solution.py:41
  9.2 2.6 %collective-permute-start.1 = (bf16[64,1024]{1,0:T(8,128)(2,1)S(1)}, bf16[64,1024]{1,0:T(8,128)(2,1)S(1)}, u32[]{:S(2)}, u32[]{:S(2)}) collective-permute-start(bf16[64,1024]{1,0:T(8,128)(2,1)S(1)} %fusion.33), channel_id=1, source_target_pairs={{0,2},{1,3},{2,0},{3,1},{4,6},{5,7},{6,4},{7,5},{8,10},{9,11},{10,... | collective-permute-start | bytes 393224 | tf_op jit(solution)/shard_map/ppermute | solution.py:41
  11.8 1.7 collective-permute-start.3
  13.5 1.5 collective-permute-start.4
  15.2 1.4 pad_maximum_fusion.4
  16.7 1.5 fusion.127
  19.0 3.1 %collective-permute-done.1 = bf16[64,1024]{1,0:T(8,128)(2,1)S(1)} collective-permute-done((bf16[64,1024]{1,0:T(8,128)(2,1)S(1)}, bf16[64,1024]{1,0:T(8,128)(2,1)S(1)}, u32[]{:S(2)}, u32[]{:S(2)}) %collective-permute-start.1) | collective-permute-done | bytes 131104 | tf_op jit(solution)/shard_map/ppermute | solution.py:41
  22.5 1.9 collective-permute-start.7
  24.4 2.0 collective-permute-start.8
  26.4 1.9 collective-permute-start.9
  29.5 1.8 collective-permute-start.12
  31.3 1.6 collective-permute-done.9
  37.4 2.2 collective-permute-start.11
  41.3 7.6 %collective-permute-done.12 = bf16[3,128,1152]{2,1,0:T(8,128)(2,1)S(1)} collective-permute-done((bf16[3,128,1152]{2,1,0:T(8,128)(2,1)}, bf16[3,128,1152]{2,1,0:T(8,128)(2,1)S(1)}, u32[]{:S(2)}, u32[]{:S(2)}) %collective-permute-start.12) | collective-permute-done | bytes 884768 | tf_op jit(solution)/shard_map/ppermute | solution.py:41
  48.9 8.3 %collective-permute-done.13 = bf16[3,128,1152]{2,1,0:T(8,128)(2,1)S(1)} collective-permute-done((bf16[3,128,1152]{2,1,0:T(8,128)(2,1)}, bf16[3,128,1152]{2,1,0:T(8,128)(2,1)S(1)}, u32[]{:S(2)}, u32[]{:S(2)}) %collective-permute-start.13) | collective-permute-done | bytes 884768 | tf_op jit(solution)/shard_map/ppermute | solution.py:41
  60.2 8.2 %collective-permute-start.15 = (bf16[64,1024]{1,0:T(8,128)(2,1)S(1)}, bf16[64,1024]{1,0:T(8,128)(2,1)S(1)}, u32[]{:S(2)}, u32[]{:S(2)}) collective-permute-start(bf16[64,1024]{1,0:T(8,128)(2,1)S(1)} %get-tuple-element.205), channel_id=1, source_target_pairs={{0,2},{1,3},{2,0},{3,1},{4,6},{5,7},{6,4},{7,5},{8,10},{9,11},{10,... | collective-permute-start | bytes 393224 | tf_op jit(solution)/shard_map/ppermute | solution.py:41
  68.7 1.8 collective-permute-start.18
  71.5 5.6 %collective-permute-done.15 = bf16[64,1024]{1,0:T(8,128)(2,1)S(1)} collective-permute-done((bf16[64,1024]{1,0:T(8,128)(2,1)S(1)}, bf16[64,1024]{1,0:T(8,128)(2,1)S(1)}, u32[]{:S(2)}, u32[]{:S(2)}) %collective-permute-start.15) | collective-permute-done | bytes 131104 | tf_op jit(solution)/shard_map/ppermute | solution.py:41
  77.2 2.4 %collective-permute-done.17 = bf16[3,64,1152]{2,1,0:T(8,128)(2,1)S(1)} collective-permute-done((bf16[3,64,1152]{2,1,0:T(8,128)(2,1)S(1)}, bf16[3,64,1152]{2,1,0:T(8,128)(2,1)S(1)}, u32[]{:S(2)}, u32[]{:S(2)}) %collective-permute-start.17) | collective-permute-done | bytes 442400 | tf_op jit(solution)/shard_map/ppermute | solution.py:41
  85.4 1.6 collective-permute-start.22
  87.1 1.6 collective-permute-start.21
  89.9 1.8 fusion.20
  91.7 2.0 collective-permute-done.22
  93.7 7.3 %collective-permute-done.21 = bf16[64,1024]{1,0:T(8,128)(2,1)S(1)} collective-permute-done((bf16[64,1024]{1,0:T(8,128)(2,1)S(1)}, bf16[64,1024]{1,0:T(8,128)(2,1)S(1)}, u32[]{:S(2)}, u32[]{:S(2)}) %collective-permute-start.21) | collective-permute-done | bytes 131104 | tf_op jit(solution)/shard_map/ppermute | solution.py:41
  101.1 1.8 fusion.25
  102.8 1.8 convolution_add_fusion
  104.6 1.8 fusion.23
  106.4 1.8 convolution_add_fusion.2
  108.2 2.2 multiply_convert_fusion
  110.4 1.8 fusion.19
  112.8 1.8 fusion.24
  117.4 1.8 fusion.21
  119.3 1.6 collective-permute-start.25
  121.0 2.8 %collective-permute-start.23 = (bf16[64,1024]{1,0:T(8,128)(2,1)S(1)}, bf16[64,1024]{1,0:T(8,128)(2,1)S(1)}, u32[]{:S(2)}, u32[]{:S(2)}) collective-permute-start(bf16[64,1024]{1,0:T(8,128)(2,1)S(1)} %get-tuple-element.216), channel_id=1, source_target_pairs={{0,1},{1,0},{2,3},{3,2},{4,5},{5,4},{6,7},{7,6},{8,9},{9,8},{10,11... | collective-permute-start | bytes 393224 | tf_op jit(solution)/shard_map/ppermute | solution.py:41
  124.4 1.8 fusion.22
  126.2 1.8 convolution_add_fusion.4
  128.0 1.8 convolution_add_fusion.3
  129.9 2.0 collective-permute-done.24
  132.1 1.6 collective-permute-start.28
  133.8 2.8 %collective-permute-start.26 = (bf16[64,1024]{1,0:T(8,128)(2,1)S(1)}, bf16[64,1024]{1,0:T(8,128)(2,1)S(1)}, u32[]{:S(2)}, u32[]{:S(2)}) collective-permute-start(bf16[64,1024]{1,0:T(8,128)(2,1)S(1)} %get-tuple-element.213), channel_id=1, source_target_pairs={{0,1},{1,0},{2,3},{3,2},{4,5},{5,4},{6,7},{7,6},{8,9},{9,8},{10,11... | collective-permute-start | bytes 393224 | tf_op jit(solution)/shard_map/ppermute | solution.py:41
  136.8 3.6 %collective-permute-done.28 = bf16[64,1024]{1,0:T(8,128)(2,1)S(1)} collective-permute-done((bf16[64,1024]{1,0:T(8,128)(2,1)S(1)}, bf16[64,1024]{1,0:T(8,128)(2,1)S(1)}, u32[]{:S(2)}, u32[]{:S(2)}) %collective-permute-start.28) | collective-permute-done | bytes 131104 | tf_op jit(solution)/shard_map/ppermute | solution.py:41
  140.5 4.6 %collective-permute-done.27 = bf16[64,1024]{1,0:T(8,128)(2,1)S(1)} collective-permute-done((bf16[64,1024]{1,0:T(8,128)(2,1)S(1)}, bf16[64,1024]{1,0:T(8,128)(2,1)S(1)}, u32[]{:S(2)}, u32[]{:S(2)}) %collective-permute-start.27) | collective-permute-done | bytes 131104 | tf_op jit(solution)/shard_map/ppermute | solution.py:41
  145.5 2.1 collective-permute-start.30
  147.6 2.3 %collective-permute-start.32 = (bf16[64,1024]{1,0:T(8,128)(2,1)S(1)}, bf16[64,1024]{1,0:T(8,128)(2,1)S(1)}, u32[]{:S(2)}, u32[]{:S(2)}) collective-permute-start(bf16[64,1024]{1,0:T(8,128)(2,1)S(1)} %fusion.105), channel_id=1, source_target_pairs={{0,1},{1,0},{2,3},{3,2},{4,5},{5,4},{6,7},{7,6},{8,9},{9,8},{10,11... | collective-permute-start | bytes 393224 | tf_op jit(solution)/shard_map/ppermute | solution.py:41
  151.1 1.6 collective-permute-start.33
  152.7 1.5 collective-permute-start.34
  154.3 4.1 %collective-permute-done.31 = bf16[64,1024]{1,0:T(8,128)(2,1)S(1)} collective-permute-done((bf16[64,1024]{1,0:T(8,128)(2,1)S(1)}, bf16[64,1024]{1,0:T(8,128)(2,1)S(1)}, u32[]{:S(2)}, u32[]{:S(2)}) %collective-permute-start.31) | collective-permute-done | bytes 131104 | tf_op jit(solution)/shard_map/ppermute | solution.py:41
  158.6 3.8 %collective-permute-done.33 = bf16[3,64,1152]{2,1,0:T(8,128)(2,1)S(1)} collective-permute-done((bf16[3,64,1152]{2,1,0:T(8,128)(2,1)S(1)}, bf16[3,64,1152]{2,1,0:T(8,128)(2,1)S(1)}, u32[]{:S(2)}, u32[]{:S(2)}) %collective-permute-start.33) | collective-permute-done | bytes 442400 | tf_op jit(solution)/shard_map/ppermute | solution.py:41
  168.1 1.6 collective-permute-start.40
  173.1 1.9 collective-permute-start.38
  175.2 6.1 %collective-permute-done.38 = bf16[64,1024]{1,0:T(8,128)(2,1)S(1)} collective-permute-done((bf16[64,1024]{1,0:T(8,128)(2,1)S(1)}, bf16[64,1024]{1,0:T(8,128)(2,1)S(1)}, u32[]{:S(2)}, u32[]{:S(2)}) %collective-permute-start.38) | collective-permute-done | bytes 131104 | tf_op jit(solution)/shard_map/ppermute | solution.py:41
  181.3 4.0 %collective-permute-start.36 = (bf16[64,1024]{1,0:T(8,128)(2,1)S(1)}, bf16[64,1024]{1,0:T(8,128)(2,1)S(1)}, u32[]{:S(2)}, u32[]{:S(2)}) collective-permute-start(bf16[64,1024]{1,0:T(8,128)(2,1)S(1)} %get-tuple-element.132), channel_id=1, source_target_pairs={{0,1},{1,0},{2,3},{3,2},{4,5},{5,4},{6,7},{7,6},{8,9},{9,8},{10,11... | collective-permute-start | bytes 393224 | tf_op jit(solution)/shard_map/ppermute | solution.py:41
  185.6 1.7 collective-permute-done.37
  187.3 2.7 %collective-permute-done.36 = bf16[64,1024]{1,0:T(8,128)(2,1)S(1)} collective-permute-done((bf16[64,1024]{1,0:T(8,128)(2,1)S(1)}, bf16[64,1024]{1,0:T(8,128)(2,1)S(1)}, u32[]{:S(2)}, u32[]{:S(2)}) %collective-permute-start.36) | collective-permute-done | bytes 131104 | tf_op jit(solution)/shard_map/ppermute | solution.py:41
  191.4 2.1 collective-permute-start.43
  193.5 2.0 collective-permute-start.42
  197.8 1.5 collective-permute-start.45
  199.3 1.4 collective-permute-start.46
  202.7 1.5 collective-permute-done.46
  206.1 1.4 collective-permute-start.50
  207.8 1.4 collective-permute-start.48
  209.3 1.4 collective-permute-start.47
  210.7 1.5 collective-permute-start.55
  214.8 4.8 %collective-permute-done.55 = bf16[4,128,256]{2,1,0:T(8,128)(2,1)S(1)} collective-permute-done((bf16[4,128,256]{2,1,0:T(8,128)(2,1)S(1)}, bf16[4,128,256]{2,1,0:T(8,128)(2,1)S(1)}, u32[]{:S(2)}, u32[]{:S(2)}) %collective-permute-start.55) | collective-permute-done | bytes 262176 | tf_op jit(solution)/shard_map/ppermute | solution.py:41
  (298 shorter events, 53.7 us)
Async XLA Ops:
  0.7 14.4 %copy-start.5 = (bf16[1152,128]{1,0:T(8,128)(2,1)S(1)}, bf16[1152,128]{1,0:T(8,128)(2,1)}, u32[]{:S(2)}) copy-start(bf16[1152,128]{1,0:T(8,128)(2,1)} %param.17) | copy-start | bytes 884740
  6.1 12.2 %collective-permute-start = (bf16[64,1024]{1,0:T(8,128)(2,1)S(1)}, bf16[64,1024]{1,0:T(8,128)(2,1)S(1)}, u32[]{:S(2)}, u32[]{:S(2)}) collective-permute-start(bf16[64,1024]{1,0:T(8,128)(2,1)S(1)} %fusion.33), channel_id=1, source_target_pairs={{0,1},{1,0},{2,3},{3,2},{4,5},{5,4},{6,7},{7,6},{8,9},{9,8},{10,11... | collective-permute-start | bytes 393224 | tf_op jit(solution)/shard_map/ppermute | solution.py:41
  9.2 12.9 %collective-permute-start.1 = (bf16[64,1024]{1,0:T(8,128)(2,1)S(1)}, bf16[64,1024]{1,0:T(8,128)(2,1)S(1)}, u32[]{:S(2)}, u32[]{:S(2)}) collective-permute-start(bf16[64,1024]{1,0:T(8,128)(2,1)S(1)} %fusion.33), channel_id=1, source_target_pairs={{0,2},{1,3},{2,0},{3,1},{4,6},{5,7},{6,4},{7,5},{8,10},{9,11},{10,... | collective-permute-start | bytes 393224 | tf_op jit(solution)/shard_map/ppermute | solution.py:41
  11.8 10.8 %collective-permute-start.2 = (bf16[64,1024]{1,0:T(8,128)(2,1)S(1)}, bf16[64,1024]{1,0:T(8,128)(2,1)}, u32[]{:S(2)}, u32[]{:S(2)}) collective-permute-start(bf16[64,1024]{1,0:T(8,128)(2,1)S(1)} %fusion.33), channel_id=1, source_target_pairs={{0,3},{1,2},{2,1},{3,0},{4,7},{5,6},{6,5},{7,4},{8,11},{9,10},{10,... | collective-permute-start | bytes 393224 | tf_op jit(solution)/shard_map/ppermute | solution.py:41
  11.8 12.6 %collective-permute-start.3 = (bf16[4,128,256]{2,1,0:T(8,128)(2,1)S(1)}, bf16[4,128,256]{2,1,0:T(8,128)(2,1)S(1)}, u32[]{:S(2)}, u32[]{:S(2)}) collective-permute-start(bf16[4,128,256]{2,1,0:T(8,128)(2,1)S(1)} %pad_maximum_fusion.12), channel_id=1, source_target_pairs={{0,8},{4,12},{8,0},{12,4},{16,24},{20,28},{24,16},{28,20},{1,9},{5... | collective-permute-start | bytes 786440 | tf_op jit(solution)/shard_map/ppermute | solution.py:41
  13.5 10.9 %collective-permute-start.4 = (bf16[4,128,256]{2,1,0:T(8,128)(2,1)S(1)}, bf16[4,128,256]{2,1,0:T(8,128)(2,1)S(1)}, u32[]{:S(2)}, u32[]{:S(2)}) collective-permute-start(bf16[4,128,256]{2,1,0:T(8,128)(2,1)S(1)} %pad_maximum_fusion.12), channel_id=1, source_target_pairs={{0,16},{4,20},{8,24},{12,28},{16,0},{20,4},{24,8},{28,12},{1,17},{... | collective-permute-start | bytes 786440 | tf_op jit(solution)/shard_map/ppermute | solution.py:41
  18.2 21.6 %copy-start.4 = (bf16[64,1024]{1,0:T(8,128)(2,1)}, bf16[64,1024]{1,0:T(8,128)(2,1)S(1)}, u32[]{:S(2)}) copy-start(bf16[64,1024]{1,0:T(8,128)(2,1)S(1)} %slice.208) | copy-start | bytes 393220
  18.3 16.6 %collective-permute-start.5 = (bf16[64,1024]{1,0:T(8,128)(2,1)S(1)}, bf16[64,1024]{1,0:T(8,128)(2,1)S(1)}, u32[]{:S(2)}, u32[]{:S(2)}) collective-permute-start(bf16[64,1024]{1,0:T(8,128)(2,1)S(1)} %slice.208), channel_id=1, source_target_pairs={{0,1},{1,0},{2,3},{3,2},{4,5},{5,4},{6,7},{7,6},{8,9},{9,8},{10,11... | collective-permute-start | bytes 393224 | tf_op jit(solution)/shard_map/ppermute | solution.py:41
  22.1 13.1 %collective-permute-start.6 = (bf16[64,1024]{1,0:T(8,128)(2,1)S(1)}, bf16[64,1024]{1,0:T(8,128)(2,1)S(1)}, u32[]{:S(2)}, u32[]{:S(2)}) collective-permute-start(bf16[64,1024]{1,0:T(8,128)(2,1)S(1)} %slice.208), channel_id=1, source_target_pairs={{0,2},{1,3},{2,0},{3,1},{4,6},{5,7},{6,4},{7,5},{8,10},{9,11},{10,... | collective-permute-start | bytes 393224 | tf_op jit(solution)/shard_map/ppermute | solution.py:41
  22.5 12.7 %collective-permute-start.7 = (bf16[64,1024]{1,0:T(8,128)(2,1)S(1)}, bf16[64,1024]{1,0:T(8,128)(2,1)S(1)}, u32[]{:S(2)}, u32[]{:S(2)}) collective-permute-start(bf16[64,1024]{1,0:T(8,128)(2,1)S(1)} %slice.208), channel_id=1, source_target_pairs={{0,3},{1,2},{2,1},{3,0},{4,7},{5,6},{6,5},{7,4},{8,11},{9,10},{10,... | collective-permute-start | bytes 393224 | tf_op jit(solution)/shard_map/ppermute | solution.py:41
  24.4 5.0 %collective-permute-start.8 = (bf16[4,64,256]{2,1,0:T(8,128)(2,1)S(1)}, bf16[4,64,256]{2,1,0:T(8,128)(2,1)S(1)}, u32[]{:S(2)}, u32[]{:S(2)}) collective-permute-start(bf16[4,64,256]{2,1,0:T(8,128)(2,1)S(1)} %split.306), channel_id=1, source_target_pairs={{0,16},{4,20},{8,24},{12,28},{16,0},{20,4},{24,8},{28,12},{1,17},{... | collective-permute-start | bytes 393224 | tf_op jit(solution)/shard_map/ppermute | solution.py:41
  26.4 6.5 %collective-permute-start.9 = (bf16[4,64,256]{2,1,0:T(8,128)(2,1)S(1)}, bf16[4,64,256]{2,1,0:T(8,128)(2,1)S(1)}, u32[]{:S(2)}, u32[]{:S(2)}) collective-permute-start(bf16[4,64,256]{2,1,0:T(8,128)(2,1)S(1)} %split.307), channel_id=1, source_target_pairs={{0,8},{4,12},{8,0},{12,4},{16,24},{20,28},{24,16},{28,20},{1,9},{5... | collective-permute-start | bytes 393224 | tf_op jit(solution)/shard_map/ppermute | solution.py:41
  29.5 19.4 %collective-permute-start.12 = (bf16[3,128,1152]{2,1,0:T(8,128)(2,1)}, bf16[3,128,1152]{2,1,0:T(8,128)(2,1)S(1)}, u32[]{:S(2)}, u32[]{:S(2)}) collective-permute-start(bf16[3,128,1152]{2,1,0:T(8,128)(2,1)} %get-tuple-element.207), channel_id=1, source_target_pairs={{0,8},{4,12},{8,0},{12,4},{16,24},{20,28},{24,16},{28,20},{1,9},{5... | collective-permute-start | bytes 2654216 | tf_op jit(solution)/shard_map/ppermute | solution.py:41
  33.0 2.7 %collective-permute-start.10 = (bf16[4,512,256]{2,1,0:T(8,128)(2,1)S(1)}, bf16[4,512,256]{2,1,0:T(8,128)(2,1)S(1)}, u32[]{:S(2)}, u32[]{:S(2)}) collective-permute-start(bf16[4,512,256]{2,1,0:T(8,128)(2,1)S(1)} %constant_dynamic-update-slice_fusion.22), channel_id=1, source_target_pairs={{0,4},{4,0},{8,12},{12,8},{16,20},{20,16},{24,28},{28,24},{1,5},{5... | collective-permute-start | bytes 3145736 | tf_op jit(solution)/shard_map/ppermute | solution.py:41
  34.9 22.3 %copy-start.8 = (bf16[64,1024]{1,0:T(8,128)(2,1)}, bf16[64,1024]{1,0:T(8,128)(2,1)S(1)}, u32[]{:S(2)}) copy-start(bf16[64,1024]{1,0:T(8,128)(2,1)S(1)} %collective-permute-done.5) | copy-start | bytes 393220
  34.9 22.3 %collective-permute-start.13 = (bf16[3,128,1152]{2,1,0:T(8,128)(2,1)}, bf16[3,128,1152]{2,1,0:T(8,128)(2,1)S(1)}, u32[]{:S(2)}, u32[]{:S(2)}) collective-permute-start(bf16[3,128,1152]{2,1,0:T(8,128)(2,1)} %get-tuple-element.207), channel_id=1, source_target_pairs={{0,16},{4,20},{8,24},{12,28},{16,0},{20,4},{24,8},{28,12},{1,17},{... | collective-permute-start | bytes 2654216 | tf_op jit(solution)/shard_map/ppermute | solution.py:41
  35.2 22.0 %copy-start.9 = (bf16[64,1024]{1,0:T(8,128)(2,1)}, bf16[64,1024]{1,0:T(8,128)(2,1)S(1)}, u32[]{:S(2)}) copy-start(bf16[64,1024]{1,0:T(8,128)(2,1)S(1)} %collective-permute-done.6) | copy-start | bytes 393220
  35.2 22.1 %copy-start.10 = (bf16[64,1024]{1,0:T(8,128)(2,1)}, bf16[64,1024]{1,0:T(8,128)(2,1)S(1)}, u32[]{:S(2)}) copy-start(bf16[64,1024]{1,0:T(8,128)(2,1)S(1)} %collective-permute-done.7) | copy-start | bytes 393220
  37.4 2.8 %collective-permute-start.11 = (bf16[2,256]{1,0:T(2,128)(2,1)S(1)}, bf16[2,256]{1,0:T(2,128)(2,1)S(1)}, u32[]{:S(2)}, u32[]{:S(2)}) collective-permute-start(bf16[2,256]{1,0:T(2,128)(2,1)S(1)} %slice.215), channel_id=1, source_target_pairs={{0,4},{4,8},{8,12},{12,16},{16,20},{20,24},{24,28},{1,5},{5,9},{9,... | collective-permute-start | bytes 3080 | tf_op jit(solution)/shard_map/ppermute | solution.py:12
  59.0 12.5 %collective-permute-start.16 = (bf16[64,1024]{1,0:T(8,128)(2,1)S(1)}, bf16[64,1024]{1,0:T(8,128)(2,1)S(1)}, u32[]{:S(2)}, u32[]{:S(2)}) collective-permute-start(bf16[64,1024]{1,0:T(8,128)(2,1)S(1)} %get-tuple-element.206), channel_id=1, source_target_pairs={{0,3},{1,2},{2,1},{3,0},{4,7},{5,6},{6,5},{7,4},{8,11},{9,10},{10,... | collective-permute-start | bytes 393224 | tf_op jit(solution)/shard_map/ppermute | solution.py:41
  60.2 16.9 %collective-permute-start.15 = (bf16[64,1024]{1,0:T(8,128)(2,1)S(1)}, bf16[64,1024]{1,0:T(8,128)(2,1)S(1)}, u32[]{:S(2)}, u32[]{:S(2)}) collective-permute-start(bf16[64,1024]{1,0:T(8,128)(2,1)S(1)} %get-tuple-element.205), channel_id=1, source_target_pairs={{0,2},{1,3},{2,0},{3,1},{4,6},{5,7},{6,4},{7,5},{8,10},{9,11},{10,... | collective-permute-start | bytes 393224 | tf_op jit(solution)/shard_map/ppermute | solution.py:41
  68.4 8.7 %collective-permute-start.14 = (bf16[64,1024]{1,0:T(8,128)(2,1)S(1)}, bf16[64,1024]{1,0:T(8,128)(2,1)S(1)}, u32[]{:S(2)}, u32[]{:S(2)}) collective-permute-start(bf16[64,1024]{1,0:T(8,128)(2,1)S(1)} %get-tuple-element.149), channel_id=1, source_target_pairs={{0,1},{1,0},{2,3},{3,2},{4,5},{5,4},{6,7},{7,6},{8,9},{9,8},{10,11... | collective-permute-start | bytes 393224 | tf_op jit(solution)/shard_map/ppermute | solution.py:41
  68.4 11.2 %collective-permute-start.17 = (bf16[3,64,1152]{2,1,0:T(8,128)(2,1)S(1)}, bf16[3,64,1152]{2,1,0:T(8,128)(2,1)S(1)}, u32[]{:S(2)}, u32[]{:S(2)}) collective-permute-start(bf16[3,64,1152]{2,1,0:T(8,128)(2,1)S(1)} %split.313), channel_id=1, source_target_pairs={{0,16},{4,20},{8,24},{12,28},{16,0},{20,4},{24,8},{28,12},{1,17},{... | collective-permute-start | bytes 1327112 | tf_op jit(solution)/shard_map/ppermute | solution.py:41
  68.7 11.2 %collective-permute-start.18 = (bf16[3,64,1152]{2,1,0:T(8,128)(2,1)S(1)}, bf16[3,64,1152]{2,1,0:T(8,128)(2,1)S(1)}, u32[]{:S(2)}, u32[]{:S(2)}) collective-permute-start(bf16[3,64,1152]{2,1,0:T(8,128)(2,1)S(1)} %split.314), channel_id=1, source_target_pairs={{0,8},{4,12},{8,0},{12,4},{16,24},{20,28},{24,16},{28,20},{1,9},{5... | collective-permute-start | bytes 1327112 | tf_op jit(solution)/shard_map/ppermute | solution.py:41
  81.5 19.5 %collective-permute-start.19 = (bf16[3,512,1152]{2,1,0:T(8,128)(2,1)}, bf16[3,512,1152]{2,1,0:T(8,128)(2,1)}, u32[]{:S(2)}, u32[]{:S(2)}) collective-permute-start(bf16[3,512,1152]{2,1,0:T(8,128)(2,1)} %constant_dynamic-update-slice_fusion.27), channel_id=1, source_target_pairs={{0,4},{4,0},{8,12},{12,8},{16,20},{20,16},{24,28},{28,24},{1,5},{5... | collective-permute-start | bytes 10616840 | tf_op jit(solution)/shard_map/ppermute | solution.py:41
  85.4 8.3 %collective-permute-start.22 = (bf16[64,1024]{1,0:T(8,128)(2,1)S(1)}, bf16[64,1024]{1,0:T(8,128)(2,1)S(1)}, u32[]{:S(2)}, u32[]{:S(2)}) collective-permute-start(bf16[64,1024]{1,0:T(8,128)(2,1)S(1)} %multiply_convert_fusion.7), channel_id=1, source_target_pairs={{0,3},{1,2},{2,1},{3,0},{4,7},{5,6},{6,5},{7,4},{8,11},{9,10},{10,... | collective-permute-start | bytes 393224 | tf_op jit(solution)/shard_map/ppermute | solution.py:41
  87.1 13.9 %collective-permute-start.21 = (bf16[64,1024]{1,0:T(8,128)(2,1)S(1)}, bf16[64,1024]{1,0:T(8,128)(2,1)S(1)}, u32[]{:S(2)}, u32[]{:S(2)}) collective-permute-start(bf16[64,1024]{1,0:T(8,128)(2,1)S(1)} %multiply_convert_fusion.7), channel_id=1, source_target_pairs={{0,2},{1,3},{2,0},{3,1},{4,6},{5,7},{6,4},{7,5},{8,10},{9,11},{10,... | collective-permute-start | bytes 393224 | tf_op jit(solution)/shard_map/ppermute | solution.py:41
  88.7 12.3 %collective-permute-start.20 = (bf16[64,1024]{1,0:T(8,128)(2,1)S(1)}, bf16[64,1024]{1,0:T(8,128)(2,1)S(1)}, u32[]{:S(2)}, u32[]{:S(2)}) collective-permute-start(bf16[64,1024]{1,0:T(8,128)(2,1)S(1)} %multiply_convert_fusion.7), channel_id=1, source_target_pairs={{0,1},{1,0},{2,3},{3,2},{4,5},{5,4},{6,7},{7,6},{8,9},{9,8},{10,11... | collective-permute-start | bytes 393224 | tf_op jit(solution)/shard_map/ppermute | solution.py:41
  119.3 10.6 %collective-permute-start.25 = (bf16[64,1024]{1,0:T(8,128)(2,1)S(1)}, bf16[64,1024]{1,0:T(8,128)(2,1)S(1)}, u32[]{:S(2)}, u32[]{:S(2)}) collective-permute-start(bf16[64,1024]{1,0:T(8,128)(2,1)S(1)} %get-tuple-element.217), channel_id=1, source_target_pairs={{0,3},{1,2},{2,1},{3,0},{4,7},{5,6},{6,5},{7,4},{8,11},{9,10},{10,... | collective-permute-start | bytes 393224 | tf_op jit(solution)/shard_map/ppermute | solution.py:41
  121.0 11.0 %collective-permute-start.24 = (bf16[64,1024]{1,0:T(8,128)(2,1)S(1)}, bf16[64,1024]{1,0:T(8,128)(2,1)S(1)}, u32[]{:S(2)}, u32[]{:S(2)}) collective-permute-start(bf16[64,1024]{1,0:T(8,128)(2,1)S(1)} %get-tuple-element.218), channel_id=1, source_target_pairs={{0,2},{1,3},{2,0},{3,1},{4,6},{5,7},{6,4},{7,5},{8,10},{9,11},{10,... | collective-permute-start | bytes 393224 | tf_op jit(solution)/shard_map/ppermute | solution.py:41
  121.0 11.0 %collective-permute-start.23 = (bf16[64,1024]{1,0:T(8,128)(2,1)S(1)}, bf16[64,1024]{1,0:T(8,128)(2,1)S(1)}, u32[]{:S(2)}, u32[]{:S(2)}) collective-permute-start(bf16[64,1024]{1,0:T(8,128)(2,1)S(1)} %get-tuple-element.216), channel_id=1, source_target_pairs={{0,1},{1,0},{2,3},{3,2},{4,5},{5,4},{6,7},{7,6},{8,9},{9,8},{10,11... | collective-permute-start | bytes 393224 | tf_op jit(solution)/shard_map/ppermute | solution.py:41
  124.3 20.9 %collective-permute-start.29 = (bf16[3,512,1152]{2,1,0:T(8,128)(2,1)S(1)}, bf16[3,512,1152]{2,1,0:T(8,128)(2,1)S(1)}, u32[]{:S(2)}, u32[]{:S(2)}) collective-permute-start(bf16[3,512,1152]{2,1,0:T(8,128)(2,1)S(1)} %pad_maximum_fusion), channel_id=1, source_target_pairs={{0,4},{4,0},{8,12},{12,8},{16,20},{20,16},{24,28},{28,24},{1,5},{5... | collective-permute-start | bytes 10616840 | tf_op jit(solution)/shard_map/ppermute | solution.py:41
  132.1 8.3 %collective-permute-start.28 = (bf16[64,1024]{1,0:T(8,128)(2,1)S(1)}, bf16[64,1024]{1,0:T(8,128)(2,1)S(1)}, u32[]{:S(2)}, u32[]{:S(2)}) collective-permute-start(bf16[64,1024]{1,0:T(8,128)(2,1)S(1)} %get-tuple-element.214), channel_id=1, source_target_pairs={{0,3},{1,2},{2,1},{3,0},{4,7},{5,6},{6,5},{7,4},{8,11},{9,10},{10,... | collective-permute-start | bytes 393224 | tf_op jit(solution)/shard_map/ppermute | solution.py:41
  133.8 11.3 %collective-permute-start.27 = (bf16[64,1024]{1,0:T(8,128)(2,1)S(1)}, bf16[64,1024]{1,0:T(8,128)(2,1)S(1)}, u32[]{:S(2)}, u32[]{:S(2)}) collective-permute-start(bf16[64,1024]{1,0:T(8,128)(2,1)S(1)} %get-tuple-element.215), channel_id=1, source_target_pairs={{0,2},{1,3},{2,0},{3,1},{4,6},{5,7},{6,4},{7,5},{8,10},{9,11},{10,... | collective-permute-start | bytes 393224 | tf_op jit(solution)/shard_map/ppermute | solution.py:41
  133.8 11.3 %collective-permute-start.26 = (bf16[64,1024]{1,0:T(8,128)(2,1)S(1)}, bf16[64,1024]{1,0:T(8,128)(2,1)S(1)}, u32[]{:S(2)}, u32[]{:S(2)}) collective-permute-start(bf16[64,1024]{1,0:T(8,128)(2,1)S(1)} %get-tuple-element.213), channel_id=1, source_target_pairs={{0,1},{1,0},{2,3},{3,2},{4,5},{5,4},{6,7},{7,6},{8,9},{9,8},{10,11... | collective-permute-start | bytes 393224 | tf_op jit(solution)/shard_map/ppermute | solution.py:41
  145.5 8.8 %collective-permute-start.30 = (bf16[64,1024]{1,0:T(8,128)(2,1)S(1)}, bf16[64,1024]{1,0:T(8,128)(2,1)S(1)}, u32[]{:S(2)}, u32[]{:S(2)}) collective-permute-start(bf16[64,1024]{1,0:T(8,128)(2,1)S(1)} %fusion.105), channel_id=1, source_target_pairs={{0,3},{1,2},{2,1},{3,0},{4,7},{5,6},{6,5},{7,4},{8,11},{9,10},{10,... | collective-permute-start | bytes 393224 | tf_op jit(solution)/shard_map/ppermute | solution.py:41
  147.6 10.8 %collective-permute-start.31 = (bf16[64,1024]{1,0:T(8,128)(2,1)S(1)}, bf16[64,1024]{1,0:T(8,128)(2,1)S(1)}, u32[]{:S(2)}, u32[]{:S(2)}) collective-permute-start(bf16[64,1024]{1,0:T(8,128)(2,1)S(1)} %fusion.105), channel_id=1, source_target_pairs={{0,2},{1,3},{2,0},{3,1},{4,6},{5,7},{6,4},{7,5},{8,10},{9,11},{10,... | collective-permute-start | bytes 393224 | tf_op jit(solution)/shard_map/ppermute | solution.py:41
  147.6 10.8 %collective-permute-start.32 = (bf16[64,1024]{1,0:T(8,128)(2,1)S(1)}, bf16[64,1024]{1,0:T(8,128)(2,1)S(1)}, u32[]{:S(2)}, u32[]{:S(2)}) collective-permute-start(bf16[64,1024]{1,0:T(8,128)(2,1)S(1)} %fusion.105), channel_id=1, source_target_pairs={{0,1},{1,0},{2,3},{3,2},{4,5},{5,4},{6,7},{7,6},{8,9},{9,8},{10,11... | collective-permute-start | bytes 393224 | tf_op jit(solution)/shard_map/ppermute | solution.py:41
  151.1 11.3 %collective-permute-start.33 = (bf16[3,64,1152]{2,1,0:T(8,128)(2,1)S(1)}, bf16[3,64,1152]{2,1,0:T(8,128)(2,1)S(1)}, u32[]{:S(2)}, u32[]{:S(2)}) collective-permute-start(bf16[3,64,1152]{2,1,0:T(8,128)(2,1)S(1)} %get-tuple-element.191), channel_id=1, source_target_pairs={{0,8},{4,12},{8,0},{12,4},{16,24},{20,28},{24,16},{28,20},{1,9},{5... | collective-permute-start | bytes 1327112 | tf_op jit(solution)/shard_map/ppermute | solution.py:41
  152.7 11.0 %collective-permute-start.34 = (bf16[3,64,1152]{2,1,0:T(8,128)(2,1)S(1)}, bf16[3,64,1152]{2,1,0:T(8,128)(2,1)S(1)}, u32[]{:S(2)}, u32[]{:S(2)}) collective-permute-start(bf16[3,64,1152]{2,1,0:T(8,128)(2,1)S(1)} %get-tuple-element.190), channel_id=1, source_target_pairs={{0,16},{4,20},{8,24},{12,28},{16,0},{20,4},{24,8},{28,12},{1,17},{... | collective-permute-start | bytes 1327112 | tf_op jit(solution)/shard_map/ppermute | solution.py:41
  154.3 36.2 %copy-start.13 = (f32[1024]{0:T(1024)}, f32[1024]{0:T(1024)S(1)}, u32[]{:S(2)}) copy-start(f32[1024]{0:T(1024)S(1)} %constant_dynamic-update-slice_fusion.57) | copy-start | bytes 12292
  165.2 5.1 %collective-permute-start.35 = (bf16[2,256]{1,0:T(2,128)(2,1)S(1)}, bf16[2,256]{1,0:T(2,128)(2,1)S(1)}, u32[]{:S(2)}, u32[]{:S(2)}) collective-permute-start(bf16[2,256]{1,0:T(2,128)(2,1)S(1)} %slice.227), channel_id=1, source_target_pairs={{4,0},{8,4},{12,8},{16,12},{20,16},{24,20},{28,24},{5,1},{9,5},{13... | collective-permute-start | bytes 3080 | tf_op jit(solution)/shard_map/ppermute | solution.py:12
  166.8 23.3 %collective-permute-start.39 = (bf16[3,128,1152]{2,1,0:T(8,128)(2,1)S(1)}, bf16[3,128,1152]{2,1,0:T(8,128)(2,1)S(1)}, u32[]{:S(2)}, u32[]{:S(2)}) collective-permute-start(bf16[3,128,1152]{2,1,0:T(8,128)(2,1)S(1)} %pad_maximum_fusion.5), channel_id=1, source_target_pairs={{0,8},{4,12},{8,0},{12,4},{16,24},{20,28},{24,16},{28,20},{1,9},{5... | collective-permute-start | bytes 2654216 | tf_op jit(solution)/shard_map/ppermute | solution.py:41
  168.1 22.0 %collective-permute-start.40 = (bf16[3,128,1152]{2,1,0:T(8,128)(2,1)S(1)}, bf16[3,128,1152]{2,1,0:T(8,128)(2,1)S(1)}, u32[]{:S(2)}, u32[]{:S(2)}) collective-permute-start(bf16[3,128,1152]{2,1,0:T(8,128)(2,1)S(1)} %pad_maximum_fusion.6), channel_id=1, source_target_pairs={{0,16},{4,20},{8,24},{12,28},{16,0},{20,4},{24,8},{28,12},{1,17},{... | collective-permute-start | bytes 2654216 | tf_op jit(solution)/shard_map/ppermute | solution.py:41
  172.0 18.1 %collective-permute-start.41 = (bf16[4,512,256]{2,1,0:T(8,128)(2,1)S(1)}, bf16[4,512,256]{2,1,0:T(8,128)(2,1)S(1)}, u32[]{:S(2)}, u32[]{:S(2)}) collective-permute-start(bf16[4,512,256]{2,1,0:T(8,128)(2,1)S(1)} %pad_maximum_fusion.3), channel_id=1, source_target_pairs={{0,4},{4,0},{8,12},{12,8},{16,20},{20,16},{24,28},{28,24},{1,5},{5... | collective-permute-start | bytes 3145736 | tf_op jit(solution)/shard_map/ppermute | solution.py:41
  173.0 17.1 %copy-start.16 = (f32[64]{0:T(128)S(1)}, f32[64]{0:T(128)}, u32[]{:S(2)}) copy-start(f32[64]{0:T(128)} %copy-done.15) | copy-start | bytes 772
  173.1 17.3 %copy-start.11 = (f32[1024]{0:T(1024)S(1)}, f32[1024]{0:T(1024)}, u32[]{:S(2)}) copy-start(f32[1024]{0:T(1024)} %custom-call.1) | copy-start | bytes 12292
  173.1 8.3 %collective-permute-start.38 = (bf16[64,1024]{1,0:T(8,128)(2,1)S(1)}, bf16[64,1024]{1,0:T(8,128)(2,1)S(1)}, u32[]{:S(2)}, u32[]{:S(2)}) collective-permute-start(bf16[64,1024]{1,0:T(8,128)(2,1)S(1)} %get-tuple-element.204), channel_id=1, source_target_pairs={{0,3},{1,2},{2,1},{3,0},{4,7},{5,6},{6,5},{7,4},{8,11},{9,10},{10,... | collective-permute-start | bytes 393224 | tf_op jit(solution)/shard_map/ppermute | solution.py:41
  175.0 12.3 %collective-permute-start.37 = (bf16[64,1024]{1,0:T(8,128)(2,1)S(1)}, bf16[64,1024]{1,0:T(8,128)(2,1)S(1)}, u32[]{:S(2)}, u32[]{:S(2)}) collective-permute-start(bf16[64,1024]{1,0:T(8,128)(2,1)S(1)} %get-tuple-element.203), channel_id=1, source_target_pairs={{0,2},{1,3},{2,0},{3,1},{4,6},{5,7},{6,4},{7,5},{8,10},{9,11},{10,... | collective-permute-start | bytes 393224 | tf_op jit(solution)/shard_map/ppermute | solution.py:41
  181.3 8.7 %collective-permute-start.36 = (bf16[64,1024]{1,0:T(8,128)(2,1)S(1)}, bf16[64,1024]{1,0:T(8,128)(2,1)S(1)}, u32[]{:S(2)}, u32[]{:S(2)}) collective-permute-start(bf16[64,1024]{1,0:T(8,128)(2,1)S(1)} %get-tuple-element.132), channel_id=1, source_target_pairs={{0,1},{1,0},{2,3},{3,2},{4,5},{5,4},{6,7},{7,6},{8,9},{9,8},{10,11... | collective-permute-start | bytes 393224 | tf_op jit(solution)/shard_map/ppermute | solution.py:41
  191.1 10.6 %collective-permute-start.44 = (f32[5,1024]{1,0:T(8,128)}, f32[5,1024]{1,0:T(8,128)S(1)}, u32[]{:S(2)}, u32[]{:S(2)}) collective-permute-start(f32[5,1024]{1,0:T(8,128)} %pad_maximum_fusion.15), channel_id=1, source_target_pairs={{0,1},{1,0},{2,3},{3,2},{4,5},{5,4},{6,7},{7,6},{8,9},{9,8},{10,11... | collective-permute-start | bytes 61448 | tf_op jit(solution)/shard_map/ppermute | solution.py:41
  191.4 10.3 %collective-permute-start.43 = (f32[5,1024]{1,0:T(8,128)}, f32[5,1024]{1,0:T(8,128)}, u32[]{:S(2)}, u32[]{:S(2)}) collective-permute-start(f32[5,1024]{1,0:T(8,128)} %pad_maximum_fusion.15), channel_id=1, source_target_pairs={{0,2},{1,3},{2,0},{3,1},{4,6},{5,7},{6,4},{7,5},{8,10},{9,11},{10,... | collective-permute-start | bytes 61448 | tf_op jit(solution)/shard_map/ppermute | solution.py:41
  193.5 8.2 %collective-permute-start.42 = (f32[5,1024]{1,0:T(8,128)}, f32[5,1024]{1,0:T(8,128)}, u32[]{:S(2)}, u32[]{:S(2)}) collective-permute-start(f32[5,1024]{1,0:T(8,128)} %pad_maximum_fusion.15), channel_id=1, source_target_pairs={{0,3},{1,2},{2,1},{3,0},{4,7},{5,6},{6,5},{7,4},{8,11},{9,10},{10,... | collective-permute-start | bytes 61448 | tf_op jit(solution)/shard_map/ppermute | solution.py:41
  197.8 5.0 %collective-permute-start.45 = (bf16[4,64,256]{2,1,0:T(8,128)(2,1)S(1)}, bf16[4,64,256]{2,1,0:T(8,128)(2,1)S(1)}, u32[]{:S(2)}, u32[]{:S(2)}) collective-permute-start(bf16[4,64,256]{2,1,0:T(8,128)(2,1)S(1)} %get-tuple-element.202), channel_id=1, source_target_pairs={{0,8},{4,12},{8,0},{12,4},{16,24},{20,28},{24,16},{28,20},{1,9},{5... | collective-permute-start | bytes 393224 | tf_op jit(solution)/shard_map/ppermute | solution.py:41
  199.3 5.0 %collective-permute-start.46 = (bf16[4,64,256]{2,1,0:T(8,128)(2,1)S(1)}, bf16[4,64,256]{2,1,0:T(8,128)(2,1)S(1)}, u32[]{:S(2)}, u32[]{:S(2)}) collective-permute-start(bf16[4,64,256]{2,1,0:T(8,128)(2,1)S(1)} %get-tuple-element.201), channel_id=1, source_target_pairs={{0,16},{4,20},{8,24},{12,28},{16,0},{20,4},{24,8},{28,12},{1,17},{... | collective-permute-start | bytes 393224 | tf_op jit(solution)/shard_map/ppermute | solution.py:41
  204.2 3.6 %collective-permute-start.53 = (f32[5,1024]{1,0:T(8,128)S(1)}, f32[5,1024]{1,0:T(8,128)S(1)}, u32[]{:S(2)}, u32[]{:S(2)}) collective-permute-start(f32[5,1024]{1,0:T(8,128)S(1)} %select_add_fusion.1), channel_id=1, source_target_pairs={{0,4},{4,0},{8,12},{12,8},{16,20},{20,16},{24,28},{28,24},{1,5},{5... | collective-permute-start | bytes 61448 | tf_op jit(solution)/shard_map/ppermute | solution.py:41
  204.2 5.0 %collective-permute-start.52 = (f32[5,1024]{1,0:T(8,128)S(1)}, f32[5,1024]{1,0:T(8,128)S(1)}, u32[]{:S(2)}, u32[]{:S(2)}) collective-permute-start(f32[5,1024]{1,0:T(8,128)S(1)} %select_add_fusion.1), channel_id=1, source_target_pairs={{0,8},{4,12},{8,0},{12,4},{16,24},{20,28},{24,16},{28,20},{1,9},{5... | collective-permute-start | bytes 61448 | tf_op jit(solution)/shard_map/ppermute | solution.py:41
  204.8 5.9 %collective-permute-start.51 = (f32[5,1024]{1,0:T(8,128)S(1)}, f32[5,1024]{1,0:T(8,128)S(1)}, u32[]{:S(2)}, u32[]{:S(2)}) collective-permute-start(f32[5,1024]{1,0:T(8,128)S(1)} %select_add_fusion.1), channel_id=1, source_target_pairs={{0,12},{4,8},{8,4},{12,0},{16,28},{20,24},{24,20},{28,16},{1,13},{... | collective-permute-start | bytes 61448 | tf_op jit(solution)/shard_map/ppermute | solution.py:41
  206.1 6.1 %collective-permute-start.50 = (f32[5,1024]{1,0:T(8,128)S(1)}, f32[5,1024]{1,0:T(8,128)S(1)}, u32[]{:S(2)}, u32[]{:S(2)}) collective-permute-start(f32[5,1024]{1,0:T(8,128)S(1)} %select_add_fusion.1), channel_id=1, source_target_pairs={{0,16},{4,20},{8,24},{12,28},{16,0},{20,4},{24,8},{28,12},{1,17},{... | collective-permute-start | bytes 61448 | tf_op jit(solution)/shard_map/ppermute | solution.py:41
  207.5 5.2 %collective-permute-start.49 = (f32[5,1024]{1,0:T(8,128)S(1)}, f32[5,1024]{1,0:T(8,128)S(1)}, u32[]{:S(2)}, u32[]{:S(2)}) collective-permute-start(f32[5,1024]{1,0:T(8,128)S(1)} %select_add_fusion.1), channel_id=1, source_target_pairs={{0,20},{4,16},{8,28},{12,24},{16,4},{20,0},{24,12},{28,8},{1,21},{... | collective-permute-start | bytes 61448 | tf_op jit(solution)/shard_map/ppermute | solution.py:41
  207.8 4.9 %collective-permute-start.48 = (f32[5,1024]{1,0:T(8,128)S(1)}, f32[5,1024]{1,0:T(8,128)S(1)}, u32[]{:S(2)}, u32[]{:S(2)}) collective-permute-start(f32[5,1024]{1,0:T(8,128)S(1)} %select_add_fusion.1), channel_id=1, source_target_pairs={{0,24},{4,28},{8,16},{12,20},{16,8},{20,12},{24,0},{28,4},{1,25},{... | collective-permute-start | bytes 61448 | tf_op jit(solution)/shard_map/ppermute | solution.py:41
  209.3 4.2 %collective-permute-start.47 = (f32[5,1024]{1,0:T(8,128)S(1)}, f32[5,1024]{1,0:T(8,128)S(1)}, u32[]{:S(2)}, u32[]{:S(2)}) collective-permute-start(f32[5,1024]{1,0:T(8,128)S(1)} %select_add_fusion.1), channel_id=1, source_target_pairs={{0,28},{4,24},{8,20},{12,16},{16,12},{20,8},{24,4},{28,0},{1,29},{... | collective-permute-start | bytes 61448 | tf_op jit(solution)/shard_map/ppermute | solution.py:41
  210.7 8.8 %collective-permute-start.55 = (bf16[4,128,256]{2,1,0:T(8,128)(2,1)S(1)}, bf16[4,128,256]{2,1,0:T(8,128)(2,1)S(1)}, u32[]{:S(2)}, u32[]{:S(2)}) collective-permute-start(bf16[4,128,256]{2,1,0:T(8,128)(2,1)S(1)} %pad_maximum_fusion.14), channel_id=1, source_target_pairs={{0,16},{4,20},{8,24},{12,28},{16,0},{20,4},{24,8},{28,12},{1,17},{... | collective-permute-start | bytes 786440 | tf_op jit(solution)/shard_map/ppermute | solution.py:41
  212.2 8.2 %collective-permute-start.54 = (bf16[4,128,256]{2,1,0:T(8,128)(2,1)S(1)}, bf16[4,128,256]{2,1,0:T(8,128)(2,1)S(1)}, u32[]{:S(2)}, u32[]{:S(2)}) collective-permute-start(bf16[4,128,256]{2,1,0:T(8,128)(2,1)S(1)} %pad_maximum_fusion.13), channel_id=1, source_target_pairs={{0,8},{4,12},{8,0},{12,4},{16,24},{20,28},{24,16},{28,20},{1,9},{5... | collective-permute-start | bytes 786440 | tf_op jit(solution)/shard_map/ppermute | solution.py:41
  (24 other events, 113.9 us)

commit v4 on v3

--- a/solution.py
+++ b/solution.py
@@ -233,7 +233,7 @@
     grad_parts = gather_rows(cotangent)
     mixer_near, mixer_far = finish(*mixer_gather)
     normed = in_token_order(normed_parts)
-    normed, grad_parts = lax.optimization_barrier((normed, grad_parts))
+    (normed, grad_parts), ffn_gather = beside((normed, grad_parts), ffn_gather)
 
     normed_near, normed_far = halves(normed)
     projected = [
@@ -254,7 +254,6 @@
         [times_trans(gated, mixer_near[3]), times_trans(gated, mixer_far[3])], axis=1
     )
     middle = residual + scatter_rows(for_owners(mixer_part))
-    middle, ffn_gather = beside(middle, ffn_gather)
     grad_rows = jnp.concatenate(grad_parts, axis=0)
     hidden_in = jnp.concatenate(
         gather_rows(narrow(rms_norm(middle, second_gain))), axis=0
@@ -347,6 +346,7 @@
         ],
         axis=1,
     )
+    normed_back, mixer_scatter = beside(normed_back, mixer_scatter)
     grad_normed = scatter_rows(for_owners(normed_back))
     grad_normed, ffn_scatter, mixer_scatter = beside(grad_normed, ffn_scatter, mixer_scatter)
     first_back, first_part = rms_back(residual, first_gain, grad_normed)

time: 223 us -> 223 us (level)
  starting transfers between devices: 78.2 us -> 70.6 us
  waiting for transfers between devices: 78.3 us -> 82.4 us
  local copies, waits for them, and re-layouts: 18.3 us -> 20.7 us
    ppermute x54, starting transfers between devices: 74.7 us -> 67.9 us  [swapped(): return lax.ppermute(block, axis, [(i, i ^ mask) for i in devices])]
    ppermute x54, waiting for transfers between devices: 77.9 us -> 82 us  [swapped(): return lax.ppermute(block, axis, [(i, i ^ mask) for i in devices])]
    unnamed x77 -> x69, local copies, waits for them, and re-layouts: 8.79 us -> 10.7 us
  transfers between devices with their start and end apart: 56 -> 56, of which waited for: 26 -> 26; matrix products, arithmetic and copies ran while one was open for 14% -> 16% of each run, Pallas kernels for 0% -> 0%
where the time goes in v4:
time: 223 us; the launch traced here: 222 us
  waiting for transfers between devices  82.4 us (37%)
  starting transfers between devices  70.6 us (32%)
  matrix products  32.8 us (15%)
  local copies, waits for them, and re-layouts  20.7 us (9%)
  other arithmetic  13.2 us (6%)
    ppermute x54, waiting for transfers between devices, swapped(): return lax.ppermute(block, axis, [(i, i ^ mask) for i in devices])  82 us
    ppermute x54, starting transfers between devices, swapped(): return lax.ppermute(block, axis, [(i, i ^ mask) for i in devices])  67.9 us
    dot_general x14, matrix products, dot(): return jnp.dot(left, right, preferred_element_type=jnp.float32)  14.5 us
    dot_general x14, matrix products, times_trans(): lax.dot_general(left, right, (((1,), (1,)), ((), ())), preferred_element_...  12.9 us
    unnamed x69, local copies, waits for them, and re-layouts  10.7 us
    dot_general x14, matrix products, trans_times(): lax.dot_general(left, right, (((0,), (0,)), ((), ())), preferred_element_...  5.46 us
  transfers between devices with their start and end apart: 56, of which 26 were waited for; matrix products, arithmetic and copies ran while one was open for 16% of the time, Pallas kernels for 0%

profile of v4, /device:TPU:0, one launch (start us, length us, event | category | flops | bytes accessed | tf_op | source)
XLA Modules:
  0.0 221.8 jit_solution(4620722674898154576)
XLA Ops:
  6.1 3.1 %collective-permute-start = (bf16[64,1024]{1,0:T(8,128)(2,1)S(1)}, bf16[64,1024]{1,0:T(8,128)(2,1)S(1)}, u32[]{:S(2)}, u32[]{:S(2)}) collective-permute-start(bf16[64,1024]{1,0:T(8,128)(2,1)S(1)} %fusion.33), channel_id=1, source_target_pairs={{0,1},{1,0},{2,3},{3,2},{4,5},{5,4},{6,7},{7,6},{8,9},{9,8},{10,11... | collective-permute-start | bytes 393224 | tf_op jit(solution)/shard_map/ppermute | solution.py:41
  9.2 2.6 %collective-permute-start.1 = (bf16[64,1024]{1,0:T(8,128)(2,1)S(1)}, bf16[64,1024]{1,0:T(8,128)(2,1)}, u32[]{:S(2)}, u32[]{:S(2)}) collective-permute-start(bf16[64,1024]{1,0:T(8,128)(2,1)S(1)} %fusion.33), channel_id=1, source_target_pairs={{0,2},{1,3},{2,0},{3,1},{4,6},{5,7},{6,4},{7,5},{8,10},{9,11},{10,... | collective-permute-start | bytes 393224 | tf_op jit(solution)/shard_map/ppermute | solution.py:41
  11.8 1.7 collective-permute-start.3
  13.5 1.5 collective-permute-start.4
  17.7 4.6 %collective-permute-done.1 = bf16[64,1024]{1,0:T(8,128)(2,1)} collective-permute-done((bf16[64,1024]{1,0:T(8,128)(2,1)S(1)}, bf16[64,1024]{1,0:T(8,128)(2,1)}, u32[]{:S(2)}, u32[]{:S(2)}) %collective-permute-start.1) | collective-permute-done | bytes 131104 | tf_op jit(solution)/shard_map/ppermute | solution.py:41
  22.3 1.4 collective-permute-start.8
  23.7 1.6 collective-permute-start.10
  26.0 4.0 %collective-permute-done.10 = bf16[4,64,256]{2,1,0:T(8,128)(2,1)S(1)} collective-permute-done((bf16[4,64,256]{2,1,0:T(8,128)(2,1)S(1)}, bf16[4,64,256]{2,1,0:T(8,128)(2,1)S(1)}, u32[]{:S(2)}, u32[]{:S(2)}) %collective-permute-start.10) | collective-permute-done | bytes 131104 | tf_op jit(solution)/shard_map/ppermute | solution.py:41
  30.0 1.5 collective-permute-start.9
  31.6 12.6 %collective-permute-done.11 = bf16[4,64,256]{2,1,0:T(8,128)(2,1)S(1)} collective-permute-done((bf16[4,64,256]{2,1,0:T(8,128)(2,1)S(1)}, bf16[4,64,256]{2,1,0:T(8,128)(2,1)S(1)}, u32[]{:S(2)}, u32[]{:S(2)}) %collective-permute-start.11) | collective-permute-done | bytes 131104 | tf_op jit(solution)/shard_map/ppermute | solution.py:41
  45.8 1.7 collective-permute-start.7
  48.6 5.0 %collective-permute-done.7 = bf16[64,1024]{1,0:T(8,128)(2,1)S(1)} collective-permute-done((bf16[64,1024]{1,0:T(8,128)(2,1)S(1)}, bf16[64,1024]{1,0:T(8,128)(2,1)S(1)}, u32[]{:S(2)}, u32[]{:S(2)}) %collective-permute-start.7) | collective-permute-done | bytes 131104 | tf_op jit(solution)/shard_map/ppermute | solution.py:41
  54.7 1.6 collective-permute-start.14
  57.4 1.6 collective-permute-start.15
  58.9 2.2 constant_dynamic-update-slice_fusion.30
  61.1 2.2 constant_dynamic-update-slice_fusion.29
  65.0 1.5 collective-permute-start.13
  72.7 1.6 collective-permute-start.19
  74.3 3.2 %collective-permute-start.18 = (bf16[64,1024]{1,0:T(8,128)(2,1)S(1)}, bf16[64,1024]{1,0:T(8,128)(2,1)S(1)}, u32[]{:S(2)}, u32[]{:S(2)}) collective-permute-start(bf16[64,1024]{1,0:T(8,128)(2,1)S(1)} %get-tuple-element.207), channel_id=1, source_target_pairs={{0,2},{1,3},{2,0},{3,1},{4,6},{5,7},{6,4},{7,5},{8,10},{9,11},{10,... | collective-permute-start | bytes 393224 | tf_op jit(solution)/shard_map/ppermute | solution.py:41
  78.4 1.9 collective-permute-done.19
  80.3 8.0 %collective-permute-done.18 = bf16[64,1024]{1,0:T(8,128)(2,1)S(1)} collective-permute-done((bf16[64,1024]{1,0:T(8,128)(2,1)S(1)}, bf16[64,1024]{1,0:T(8,128)(2,1)S(1)}, u32[]{:S(2)}, u32[]{:S(2)}) %collective-permute-start.18) | collective-permute-done | bytes 131104 | tf_op jit(solution)/shard_map/ppermute | solution.py:41
  88.7 1.7 collective-permute-start.22
  90.4 2.7 %collective-permute-start.20 = (bf16[64,1024]{1,0:T(8,128)(2,1)S(1)}, bf16[64,1024]{1,0:T(8,128)(2,1)S(1)}, u32[]{:S(2)}, u32[]{:S(2)}) collective-permute-start(bf16[64,1024]{1,0:T(8,128)(2,1)S(1)} %multiply_convert_fusion.7), channel_id=1, source_target_pairs={{0,1},{1,0},{2,3},{3,2},{4,5},{5,4},{6,7},{7,6},{8,9},{9,8},{10,11... | collective-permute-start | bytes 393224 | tf_op jit(solution)/shard_map/ppermute | solution.py:41
  93.2 1.8 fusion.20
  95.0 2.1 collective-permute-done.22
  97.1 4.6 %collective-permute-done.21 = bf16[64,1024]{1,0:T(8,128)(2,1)S(1)} collective-permute-done((bf16[64,1024]{1,0:T(8,128)(2,1)S(1)}, bf16[64,1024]{1,0:T(8,128)(2,1)S(1)}, u32[]{:S(2)}, u32[]{:S(2)}) %collective-permute-start.21) | collective-permute-done | bytes 131104 | tf_op jit(solution)/shard_map/ppermute | solution.py:41
  101.8 1.8 fusion.25
  103.5 1.8 convolution_add_fusion
  105.3 1.8 fusion.23
  107.1 1.8 convolution_add_fusion.2
  108.9 2.2 multiply_convert_fusion
  111.1 1.8 fusion.19
  113.5 1.8 fusion.24
  118.1 1.8 fusion.21
  120.0 1.7 collective-permute-start.25
  121.7 2.8 %collective-permute-start.23 = (bf16[64,1024]{1,0:T(8,128)(2,1)S(1)}, bf16[64,1024]{1,0:T(8,128)(2,1)S(1)}, u32[]{:S(2)}, u32[]{:S(2)}) collective-permute-start(bf16[64,1024]{1,0:T(8,128)(2,1)S(1)} %get-tuple-element.218), channel_id=1, source_target_pairs={{0,1},{1,0},{2,3},{3,2},{4,5},{5,4},{6,7},{7,6},{8,9},{9,8},{10,11... | collective-permute-start | bytes 393224 | tf_op jit(solution)/shard_map/ppermute | solution.py:41
  125.1 1.8 fusion.22
  126.9 1.8 convolution_add_fusion.4
  128.7 1.8 convolution_add_fusion.3
  130.6 2.3 %collective-permute-done.24 = bf16[64,1024]{1,0:T(8,128)(2,1)S(1)} collective-permute-done((bf16[64,1024]{1,0:T(8,128)(2,1)S(1)}, bf16[64,1024]{1,0:T(8,128)(2,1)S(1)}, u32[]{:S(2)}, u32[]{:S(2)}) %collective-permute-start.24) | collective-permute-done | bytes 131104 | tf_op jit(solution)/shard_map/ppermute | solution.py:41
  133.1 2.1 collective-permute-start.28
  135.2 2.3 %collective-permute-start.26 = (bf16[64,1024]{1,0:T(8,128)(2,1)S(1)}, bf16[64,1024]{1,0:T(8,128)(2,1)S(1)}, u32[]{:S(2)}, u32[]{:S(2)}) collective-permute-start(bf16[64,1024]{1,0:T(8,128)(2,1)S(1)} %get-tuple-element.215), channel_id=1, source_target_pairs={{0,1},{1,0},{2,3},{3,2},{4,5},{5,4},{6,7},{7,6},{8,9},{9,8},{10,11... | collective-permute-start | bytes 393224 | tf_op jit(solution)/shard_map/ppermute | solution.py:41
  137.8 3.6 %collective-permute-done.28 = bf16[64,1024]{1,0:T(8,128)(2,1)S(1)} collective-permute-done((bf16[64,1024]{1,0:T(8,128)(2,1)S(1)}, bf16[64,1024]{1,0:T(8,128)(2,1)S(1)}, u32[]{:S(2)}, u32[]{:S(2)}) %collective-permute-start.28) | collective-permute-done | bytes 131104 | tf_op jit(solution)/shard_map/ppermute | solution.py:41
  141.5 4.6 %collective-permute-done.27 = bf16[64,1024]{1,0:T(8,128)(2,1)S(1)} collective-permute-done((bf16[64,1024]{1,0:T(8,128)(2,1)S(1)}, bf16[64,1024]{1,0:T(8,128)(2,1)S(1)}, u32[]{:S(2)}, u32[]{:S(2)}) %collective-permute-start.27) | collective-permute-done | bytes 131104 | tf_op jit(solution)/shard_map/ppermute | solution.py:41
  146.5 2.1 collective-permute-start.30
  148.6 2.3 %collective-permute-start.32 = (bf16[64,1024]{1,0:T(8,128)(2,1)S(1)}, bf16[64,1024]{1,0:T(8,128)(2,1)S(1)}, u32[]{:S(2)}, u32[]{:S(2)}) collective-permute-start(bf16[64,1024]{1,0:T(8,128)(2,1)S(1)} %fusion.102), channel_id=1, source_target_pairs={{0,1},{1,0},{2,3},{3,2},{4,5},{5,4},{6,7},{7,6},{8,9},{9,8},{10,11... | collective-permute-start | bytes 393224 | tf_op jit(solution)/shard_map/ppermute | solution.py:41
  152.1 2.7 %collective-permute-start.33 = (bf16[3,64,1152]{2,1,0:T(8,128)(2,1)S(1)}, bf16[3,64,1152]{2,1,0:T(8,128)(2,1)S(1)}, u32[]{:S(2)}, u32[]{:S(2)}) collective-permute-start(bf16[3,64,1152]{2,1,0:T(8,128)(2,1)S(1)} %get-tuple-element.192), channel_id=1, source_target_pairs={{0,8},{4,12},{8,0},{12,4},{16,24},{20,28},{24,16},{28,20},{1,9},{5... | collective-permute-start | bytes 1327112 | tf_op jit(solution)/shard_map/ppermute | solution.py:41
  155.9 3.6 %collective-permute-done.31 = bf16[64,1024]{1,0:T(8,128)(2,1)S(1)} collective-permute-done((bf16[64,1024]{1,0:T(8,128)(2,1)S(1)}, bf16[64,1024]{1,0:T(8,128)(2,1)S(1)}, u32[]{:S(2)}, u32[]{:S(2)}) %collective-permute-start.31) | collective-permute-done | bytes 131104 | tf_op jit(solution)/shard_map/ppermute | solution.py:41
  159.6 4.7 %collective-permute-done.33 = bf16[3,64,1152]{2,1,0:T(8,128)(2,1)S(1)} collective-permute-done((bf16[3,64,1152]{2,1,0:T(8,128)(2,1)S(1)}, bf16[3,64,1152]{2,1,0:T(8,128)(2,1)S(1)}, u32[]{:S(2)}, u32[]{:S(2)}) %collective-permute-start.33) | collective-permute-done | bytes 442400 | tf_op jit(solution)/shard_map/ppermute | solution.py:41
  164.3 1.5 collective-permute-done.34
  169.3 1.8 collective-permute-start.40
  171.3 1.8 collective-permute-start.41
  176.3 1.5 collective-permute-done.36
  177.8 2.1 collective-permute-start.39
  179.9 2.4 %collective-permute-start.37 = (bf16[64,1024]{1,0:T(8,128)(2,1)S(1)}, bf16[64,1024]{1,0:T(8,128)(2,1)S(1)}, u32[]{:S(2)}, u32[]{:S(2)}) collective-permute-start(bf16[64,1024]{1,0:T(8,128)(2,1)S(1)} %get-tuple-element.204), channel_id=1, source_target_pairs={{0,1},{1,0},{2,3},{3,2},{4,5},{5,4},{6,7},{7,6},{8,9},{9,8},{10,11... | collective-permute-start | bytes 393224 | tf_op jit(solution)/shard_map/ppermute | solution.py:41
  182.6 3.5 %collective-permute-done.39 = bf16[64,1024]{1,0:T(8,128)(2,1)S(1)} collective-permute-done((bf16[64,1024]{1,0:T(8,128)(2,1)S(1)}, bf16[64,1024]{1,0:T(8,128)(2,1)S(1)}, u32[]{:S(2)}, u32[]{:S(2)}) %collective-permute-start.39) | collective-permute-done | bytes 131104 | tf_op jit(solution)/shard_map/ppermute | solution.py:41
  186.5 5.0 %collective-permute-done.38 = bf16[64,1024]{1,0:T(8,128)(2,1)S(1)} collective-permute-done((bf16[64,1024]{1,0:T(8,128)(2,1)S(1)}, bf16[64,1024]{1,0:T(8,128)(2,1)S(1)}, u32[]{:S(2)}, u32[]{:S(2)}) %collective-permute-start.38) | collective-permute-done | bytes 131104 | tf_op jit(solution)/shard_map/ppermute | solution.py:41
  193.1 1.5 collective-permute-done.42
  194.6 2.0 collective-permute-done.43
  197.5 2.6 %collective-permute-start.45 = (f32[5,1024]{1,0:T(8,128)}, f32[5,1024]{1,0:T(8,128)}, u32[]{:S(2)}, u32[]{:S(2)}) collective-permute-start(f32[5,1024]{1,0:T(8,128)} %pad_maximum_fusion.15), channel_id=1, source_target_pairs={{0,2},{1,3},{2,0},{3,1},{4,6},{5,7},{6,4},{7,5},{8,10},{9,11},{10,... | collective-permute-start | bytes 61448 | tf_op jit(solution)/shard_map/ppermute | solution.py:41
  200.1 1.8 collective-permute-start.44
  209.3 1.7 collective-permute-start.54
  213.9 2.4 %collective-permute-start.50 = (f32[5,1024]{1,0:T(8,128)S(1)}, f32[5,1024]{1,0:T(8,128)S(1)}, u32[]{:S(2)}, u32[]{:S(2)}) collective-permute-start(f32[5,1024]{1,0:T(8,128)S(1)} %select_add_fusion.1), channel_id=1, source_target_pairs={{0,24},{4,28},{8,16},{12,20},{16,8},{20,12},{24,0},{28,4},{1,25},{... | collective-permute-start | bytes 61448 | tf_op jit(solution)/shard_map/ppermute | solution.py:41
  218.8 1.8 collective-permute-done.49
  (289 shorter events, 53.2 us)
Async XLA Ops:
  1.5 13.5 %copy-start.6 = (bf16[1152,128]{1,0:T(8,128)(2,1)S(1)}, bf16[1152,128]{1,0:T(8,128)(2,1)}, u32[]{:S(2)}) copy-start(bf16[1152,128]{1,0:T(8,128)(2,1)} %param.17) | copy-start | bytes 884740
  6.1 10.9 %collective-permute-start = (bf16[64,1024]{1,0:T(8,128)(2,1)S(1)}, bf16[64,1024]{1,0:T(8,128)(2,1)S(1)}, u32[]{:S(2)}, u32[]{:S(2)}) collective-permute-start(bf16[64,1024]{1,0:T(8,128)(2,1)S(1)} %fusion.33), channel_id=1, source_target_pairs={{0,1},{1,0},{2,3},{3,2},{4,5},{5,4},{6,7},{7,6},{8,9},{9,8},{10,11... | collective-permute-start | bytes 393224 | tf_op jit(solution)/shard_map/ppermute | solution.py:41
  9.2 13.1 %collective-permute-start.1 = (bf16[64,1024]{1,0:T(8,128)(2,1)S(1)}, bf16[64,1024]{1,0:T(8,128)(2,1)}, u32[]{:S(2)}, u32[]{:S(2)}) collective-permute-start(bf16[64,1024]{1,0:T(8,128)(2,1)S(1)} %fusion.33), channel_id=1, source_target_pairs={{0,2},{1,3},{2,0},{3,1},{4,6},{5,7},{6,4},{7,5},{8,10},{9,11},{10,... | collective-permute-start | bytes 393224 | tf_op jit(solution)/shard_map/ppermute | solution.py:41
  11.7 10.5 %collective-permute-start.2 = (bf16[64,1024]{1,0:T(8,128)(2,1)S(1)}, bf16[64,1024]{1,0:T(8,128)(2,1)}, u32[]{:S(2)}, u32[]{:S(2)}) collective-permute-start(bf16[64,1024]{1,0:T(8,128)(2,1)S(1)} %fusion.33), channel_id=1, source_target_pairs={{0,3},{1,2},{2,1},{3,0},{4,7},{5,6},{6,5},{7,4},{8,11},{9,10},{10,... | collective-permute-start | bytes 393224 | tf_op jit(solution)/shard_map/ppermute | solution.py:41
  11.8 12.0 %collective-permute-start.3 = (bf16[4,128,256]{2,1,0:T(8,128)(2,1)S(1)}, bf16[4,128,256]{2,1,0:T(8,128)(2,1)S(1)}, u32[]{:S(2)}, u32[]{:S(2)}) collective-permute-start(bf16[4,128,256]{2,1,0:T(8,128)(2,1)S(1)} %pad_maximum_fusion.12), channel_id=1, source_target_pairs={{0,8},{4,12},{8,0},{12,4},{16,24},{20,28},{24,16},{28,20},{1,9},{5... | collective-permute-start | bytes 786440 | tf_op jit(solution)/shard_map/ppermute | solution.py:41
  13.5 10.3 %collective-permute-start.4 = (bf16[4,128,256]{2,1,0:T(8,128)(2,1)S(1)}, bf16[4,128,256]{2,1,0:T(8,128)(2,1)S(1)}, u32[]{:S(2)}, u32[]{:S(2)}) collective-permute-start(bf16[4,128,256]{2,1,0:T(8,128)(2,1)S(1)} %pad_maximum_fusion.12), channel_id=1, source_target_pairs={{0,16},{4,20},{8,24},{12,28},{16,0},{20,4},{24,8},{28,12},{1,17},{... | collective-permute-start | bytes 786440 | tf_op jit(solution)/shard_map/ppermute | solution.py:41
  16.9 31.6 %copy-start.4 = (bf16[64,1024]{1,0:T(8,128)(2,1)}, bf16[64,1024]{1,0:T(8,128)(2,1)S(1)}, u32[]{:S(2)}) copy-start(bf16[64,1024]{1,0:T(8,128)(2,1)S(1)} %slice.208) | copy-start | bytes 393220
  17.0 28.8 %collective-permute-start.5 = (bf16[64,1024]{1,0:T(8,128)(2,1)S(1)}, bf16[64,1024]{1,0:T(8,128)(2,1)}, u32[]{:S(2)}, u32[]{:S(2)}) collective-permute-start(bf16[64,1024]{1,0:T(8,128)(2,1)S(1)} %slice.208), channel_id=1, source_target_pairs={{0,1},{1,0},{2,3},{3,2},{4,5},{5,4},{6,7},{7,6},{8,9},{9,8},{10,11... | collective-permute-start | bytes 393224 | tf_op jit(solution)/shard_map/ppermute | solution.py:41
  22.3 26.3 %collective-permute-start.6 = (bf16[64,1024]{1,0:T(8,128)(2,1)S(1)}, bf16[64,1024]{1,0:T(8,128)(2,1)}, u32[]{:S(2)}, u32[]{:S(2)}) collective-permute-start(bf16[64,1024]{1,0:T(8,128)(2,1)S(1)} %slice.208), channel_id=1, source_target_pairs={{0,2},{1,3},{2,0},{3,1},{4,6},{5,7},{6,4},{7,5},{8,10},{9,11},{10,... | collective-permute-start | bytes 393224 | tf_op jit(solution)/shard_map/ppermute | solution.py:41
  22.3 31.3 %collective-permute-start.8 = (bf16[3,128,1152]{2,1,0:T(8,128)(2,1)}, bf16[3,128,1152]{2,1,0:T(8,128)(2,1)}, u32[]{:S(2)}, u32[]{:S(2)}) collective-permute-start(bf16[3,128,1152]{2,1,0:T(8,128)(2,1)} %get-tuple-element.209), channel_id=1, source_target_pairs={{0,8},{4,12},{8,0},{12,4},{16,24},{20,28},{24,16},{28,20},{1,9},{5... | collective-permute-start | bytes 2654216 | tf_op jit(solution)/shard_map/ppermute | solution.py:41
  23.7 6.3 %collective-permute-start.10 = (bf16[4,64,256]{2,1,0:T(8,128)(2,1)S(1)}, bf16[4,64,256]{2,1,0:T(8,128)(2,1)S(1)}, u32[]{:S(2)}, u32[]{:S(2)}) collective-permute-start(bf16[4,64,256]{2,1,0:T(8,128)(2,1)S(1)} %split.306), channel_id=1, source_target_pairs={{0,16},{4,20},{8,24},{12,28},{16,0},{20,4},{24,8},{28,12},{1,17},{... | collective-permute-start | bytes 393224 | tf_op jit(solution)/shard_map/ppermute | solution.py:41
  25.3 18.8 %collective-permute-start.11 = (bf16[4,64,256]{2,1,0:T(8,128)(2,1)S(1)}, bf16[4,64,256]{2,1,0:T(8,128)(2,1)S(1)}, u32[]{:S(2)}, u32[]{:S(2)}) collective-permute-start(bf16[4,64,256]{2,1,0:T(8,128)(2,1)S(1)} %split.307), channel_id=1, source_target_pairs={{0,8},{4,12},{8,0},{12,4},{16,24},{20,28},{24,16},{28,20},{1,9},{5... | collective-permute-start | bytes 393224 | tf_op jit(solution)/shard_map/ppermute | solution.py:41
  30.0 23.6 %collective-permute-start.9 = (bf16[3,128,1152]{2,1,0:T(8,128)(2,1)}, bf16[3,128,1152]{2,1,0:T(8,128)(2,1)}, u32[]{:S(2)}, u32[]{:S(2)}) collective-permute-start(bf16[3,128,1152]{2,1,0:T(8,128)(2,1)} %get-tuple-element.209), channel_id=1, source_target_pairs={{0,16},{4,20},{8,24},{12,28},{16,0},{20,4},{24,8},{28,12},{1,17},{... | collective-permute-start | bytes 2654216 | tf_op jit(solution)/shard_map/ppermute | solution.py:41
  44.2 19.2 %collective-permute-start.12 = (bf16[4,512,256]{2,1,0:T(8,128)(2,1)S(1)}, bf16[4,512,256]{2,1,0:T(8,128)(2,1)S(1)}, u32[]{:S(2)}, u32[]{:S(2)}) collective-permute-start(bf16[4,512,256]{2,1,0:T(8,128)(2,1)S(1)} %constant_dynamic-update-slice_fusion.22), channel_id=1, source_target_pairs={{0,4},{4,0},{8,12},{12,8},{16,20},{20,16},{24,28},{28,24},{1,5},{5... | collective-permute-start | bytes 3145736 | tf_op jit(solution)/shard_map/ppermute | solution.py:41
  44.9 22.2 %copy-start.20 = (f32[256]{0:T(256)}, f32[256]{0:T(256)S(1)}, u32[]{:S(2)}) copy-start(f32[256]{0:T(256)S(1)} %get-tuple-element.239) | copy-start | bytes 3076
  44.9 22.2 %copy-start.22 = (f32[256]{0:T(256)}, f32[256]{0:T(256)S(1)}, u32[]{:S(2)}) copy-start(f32[256]{0:T(256)S(1)} %get-tuple-element.245) | copy-start | bytes 3076
  45.8 21.4 %copy-start.13 = (f32[1,256]{1,0:T(1,128)}, f32[1,256]{1,0:T(1,128)S(1)}, u32[]{:S(2)}) copy-start(f32[1,256]{1,0:T(1,128)S(1)} %get-tuple-element.231) | copy-start | bytes 3076
  45.8 21.4 %copy-start.15 = (f32[1,256]{1,0:T(1,128)}, f32[1,256]{1,0:T(1,128)S(1)}, u32[]{:S(2)}) copy-start(f32[1,256]{1,0:T(1,128)S(1)} %get-tuple-element.232) | copy-start | bytes 3076
  45.8 21.4 %copy-start.17 = (f32[1,256]{1,0:T(1,128)}, f32[1,256]{1,0:T(1,128)S(1)}, u32[]{:S(2)}) copy-start(f32[1,256]{1,0:T(1,128)S(1)} %get-tuple-element.233) | copy-start | bytes 3076
  45.8 7.8 %collective-permute-start.7 = (bf16[64,1024]{1,0:T(8,128)(2,1)S(1)}, bf16[64,1024]{1,0:T(8,128)(2,1)S(1)}, u32[]{:S(2)}, u32[]{:S(2)}) collective-permute-start(bf16[64,1024]{1,0:T(8,128)(2,1)S(1)} %slice.208), channel_id=1, source_target_pairs={{0,3},{1,2},{2,1},{3,0},{4,7},{5,6},{6,5},{7,4},{8,11},{9,10},{10,... | collective-permute-start | bytes 393224 | tf_op jit(solution)/shard_map/ppermute | solution.py:41
  54.7 13.5 %collective-permute-start.14 = (bf16[3,64,1152]{2,1,0:T(8,128)(2,1)S(1)}, bf16[3,64,1152]{2,1,0:T(8,128)(2,1)S(1)}, u32[]{:S(2)}, u32[]{:S(2)}) collective-permute-start(bf16[3,64,1152]{2,1,0:T(8,128)(2,1)S(1)} %split.309), channel_id=1, source_target_pairs={{0,16},{4,20},{8,24},{12,28},{16,0},{20,4},{24,8},{28,12},{1,17},{... | collective-permute-start | bytes 1327112 | tf_op jit(solution)/shard_map/ppermute | solution.py:41
  57.4 11.5 %collective-permute-start.15 = (bf16[3,64,1152]{2,1,0:T(8,128)(2,1)S(1)}, bf16[3,64,1152]{2,1,0:T(8,128)(2,1)S(1)}, u32[]{:S(2)}, u32[]{:S(2)}) collective-permute-start(bf16[3,64,1152]{2,1,0:T(8,128)(2,1)S(1)} %split.310), channel_id=1, source_target_pairs={{0,8},{4,12},{8,0},{12,4},{16,24},{20,28},{24,16},{28,20},{1,9},{5... | collective-permute-start | bytes 1327112 | tf_op jit(solution)/shard_map/ppermute | solution.py:41
  65.0 2.1 collective-permute-start.13
  70.5 31.3 %collective-permute-start.16 = (bf16[3,512,1152]{2,1,0:T(8,128)(2,1)}, bf16[3,512,1152]{2,1,0:T(8,128)(2,1)}, u32[]{:S(2)}, u32[]{:S(2)}) collective-permute-start(bf16[3,512,1152]{2,1,0:T(8,128)(2,1)} %constant_dynamic-update-slice_fusion.27), channel_id=1, source_target_pairs={{0,4},{4,0},{8,12},{12,8},{16,20},{20,16},{24,28},{28,24},{1,5},{5... | collective-permute-start | bytes 10616840 | tf_op jit(solution)/shard_map/ppermute | solution.py:41
  72.7 7.7 %collective-permute-start.19 = (bf16[64,1024]{1,0:T(8,128)(2,1)S(1)}, bf16[64,1024]{1,0:T(8,128)(2,1)S(1)}, u32[]{:S(2)}, u32[]{:S(2)}) collective-permute-start(bf16[64,1024]{1,0:T(8,128)(2,1)S(1)} %get-tuple-element.208), channel_id=1, source_target_pairs={{0,3},{1,2},{2,1},{3,0},{4,7},{5,6},{6,5},{7,4},{8,11},{9,10},{10,... | collective-permute-start | bytes 393224 | tf_op jit(solution)/shard_map/ppermute | solution.py:41
  74.3 14.1 %collective-permute-start.18 = (bf16[64,1024]{1,0:T(8,128)(2,1)S(1)}, bf16[64,1024]{1,0:T(8,128)(2,1)S(1)}, u32[]{:S(2)}, u32[]{:S(2)}) collective-permute-start(bf16[64,1024]{1,0:T(8,128)(2,1)S(1)} %get-tuple-element.207), channel_id=1, source_target_pairs={{0,2},{1,3},{2,0},{3,1},{4,6},{5,7},{6,4},{7,5},{8,10},{9,11},{10,... | collective-permute-start | bytes 393224 | tf_op jit(solution)/shard_map/ppermute | solution.py:41
  77.5 10.9 %collective-permute-start.17 = (bf16[64,1024]{1,0:T(8,128)(2,1)S(1)}, bf16[64,1024]{1,0:T(8,128)(2,1)S(1)}, u32[]{:S(2)}, u32[]{:S(2)}) collective-permute-start(bf16[64,1024]{1,0:T(8,128)(2,1)S(1)} %get-tuple-element.150), channel_id=1, source_target_pairs={{0,1},{1,0},{2,3},{3,2},{4,5},{5,4},{6,7},{7,6},{8,9},{9,8},{10,11... | collective-permute-start | bytes 393224 | tf_op jit(solution)/shard_map/ppermute | solution.py:41
  88.7 8.3 %collective-permute-start.22 = (bf16[64,1024]{1,0:T(8,128)(2,1)S(1)}, bf16[64,1024]{1,0:T(8,128)(2,1)S(1)}, u32[]{:S(2)}, u32[]{:S(2)}) collective-permute-start(bf16[64,1024]{1,0:T(8,128)(2,1)S(1)} %multiply_convert_fusion.7), channel_id=1, source_target_pairs={{0,3},{1,2},{2,1},{3,0},{4,7},{5,6},{6,5},{7,4},{8,11},{9,10},{10,... | collective-permute-start | bytes 393224 | tf_op jit(solution)/shard_map/ppermute | solution.py:41
  90.4 11.3 %collective-permute-start.21 = (bf16[64,1024]{1,0:T(8,128)(2,1)S(1)}, bf16[64,1024]{1,0:T(8,128)(2,1)S(1)}, u32[]{:S(2)}, u32[]{:S(2)}) collective-permute-start(bf16[64,1024]{1,0:T(8,128)(2,1)S(1)} %multiply_convert_fusion.7), channel_id=1, source_target_pairs={{0,2},{1,3},{2,0},{3,1},{4,6},{5,7},{6,4},{7,5},{8,10},{9,11},{10,... | collective-permute-start | bytes 393224 | tf_op jit(solution)/shard_map/ppermute | solution.py:41
  90.4 11.3 %collective-permute-start.20 = (bf16[64,1024]{1,0:T(8,128)(2,1)S(1)}, bf16[64,1024]{1,0:T(8,128)(2,1)S(1)}, u32[]{:S(2)}, u32[]{:S(2)}) collective-permute-start(bf16[64,1024]{1,0:T(8,128)(2,1)S(1)} %multiply_convert_fusion.7), channel_id=1, source_target_pairs={{0,1},{1,0},{2,3},{3,2},{4,5},{5,4},{6,7},{7,6},{8,9},{9,8},{10,11... | collective-permute-start | bytes 393224 | tf_op jit(solution)/shard_map/ppermute | solution.py:41
  120.0 10.6 %collective-permute-start.25 = (bf16[64,1024]{1,0:T(8,128)(2,1)S(1)}, bf16[64,1024]{1,0:T(8,128)(2,1)S(1)}, u32[]{:S(2)}, u32[]{:S(2)}) collective-permute-start(bf16[64,1024]{1,0:T(8,128)(2,1)S(1)} %get-tuple-element.219), channel_id=1, source_target_pairs={{0,3},{1,2},{2,1},{3,0},{4,7},{5,6},{6,5},{7,4},{8,11},{9,10},{10,... | collective-permute-start | bytes 393224 | tf_op jit(solution)/shard_map/ppermute | solution.py:41
  121.7 11.3 %collective-permute-start.24 = (bf16[64,1024]{1,0:T(8,128)(2,1)S(1)}, bf16[64,1024]{1,0:T(8,128)(2,1)S(1)}, u32[]{:S(2)}, u32[]{:S(2)}) collective-permute-start(bf16[64,1024]{1,0:T(8,128)(2,1)S(1)} %get-tuple-element.220), channel_id=1, source_target_pairs={{0,2},{1,3},{2,0},{3,1},{4,6},{5,7},{6,4},{7,5},{8,10},{9,11},{10,... | collective-permute-start | bytes 393224 | tf_op jit(solution)/shard_map/ppermute | solution.py:41
  121.7 11.3 %collective-permute-start.23 = (bf16[64,1024]{1,0:T(8,128)(2,1)S(1)}, bf16[64,1024]{1,0:T(8,128)(2,1)S(1)}, u32[]{:S(2)}, u32[]{:S(2)}) collective-permute-start(bf16[64,1024]{1,0:T(8,128)(2,1)S(1)} %get-tuple-element.218), channel_id=1, source_target_pairs={{0,1},{1,0},{2,3},{3,2},{4,5},{5,4},{6,7},{7,6},{8,9},{9,8},{10,11... | collective-permute-start | bytes 393224 | tf_op jit(solution)/shard_map/ppermute | solution.py:41
  125.0 21.2 %collective-permute-start.29 = (bf16[3,512,1152]{2,1,0:T(8,128)(2,1)S(1)}, bf16[3,512,1152]{2,1,0:T(8,128)(2,1)S(1)}, u32[]{:S(2)}, u32[]{:S(2)}) collective-permute-start(bf16[3,512,1152]{2,1,0:T(8,128)(2,1)S(1)} %pad_maximum_fusion), channel_id=1, source_target_pairs={{0,4},{4,0},{8,12},{12,8},{16,20},{20,16},{24,28},{28,24},{1,5},{5... | collective-permute-start | bytes 10616840 | tf_op jit(solution)/shard_map/ppermute | solution.py:41
  133.1 8.3 %collective-permute-start.28 = (bf16[64,1024]{1,0:T(8,128)(2,1)S(1)}, bf16[64,1024]{1,0:T(8,128)(2,1)S(1)}, u32[]{:S(2)}, u32[]{:S(2)}) collective-permute-start(bf16[64,1024]{1,0:T(8,128)(2,1)S(1)} %get-tuple-element.216), channel_id=1, source_target_pairs={{0,3},{1,2},{2,1},{3,0},{4,7},{5,6},{6,5},{7,4},{8,11},{9,10},{10,... | collective-permute-start | bytes 393224 | tf_op jit(solution)/shard_map/ppermute | solution.py:41
  135.2 10.8 %collective-permute-start.27 = (bf16[64,1024]{1,0:T(8,128)(2,1)S(1)}, bf16[64,1024]{1,0:T(8,128)(2,1)S(1)}, u32[]{:S(2)}, u32[]{:S(2)}) collective-permute-start(bf16[64,1024]{1,0:T(8,128)(2,1)S(1)} %get-tuple-element.217), channel_id=1, source_target_pairs={{0,2},{1,3},{2,0},{3,1},{4,6},{5,7},{6,4},{7,5},{8,10},{9,11},{10,... | collective-permute-start | bytes 393224 | tf_op jit(solution)/shard_map/ppermute | solution.py:41
  135.2 10.8 %collective-permute-start.26 = (bf16[64,1024]{1,0:T(8,128)(2,1)S(1)}, bf16[64,1024]{1,0:T(8,128)(2,1)S(1)}, u32[]{:S(2)}, u32[]{:S(2)}) collective-permute-start(bf16[64,1024]{1,0:T(8,128)(2,1)S(1)} %get-tuple-element.215), channel_id=1, source_target_pairs={{0,1},{1,0},{2,3},{3,2},{4,5},{5,4},{6,7},{7,6},{8,9},{9,8},{10,11... | collective-permute-start | bytes 393224 | tf_op jit(solution)/shard_map/ppermute | solution.py:41
  146.5 9.4 %collective-permute-start.30 = (bf16[64,1024]{1,0:T(8,128)(2,1)S(1)}, bf16[64,1024]{1,0:T(8,128)(2,1)S(1)}, u32[]{:S(2)}, u32[]{:S(2)}) collective-permute-start(bf16[64,1024]{1,0:T(8,128)(2,1)S(1)} %fusion.102), channel_id=1, source_target_pairs={{0,3},{1,2},{2,1},{3,0},{4,7},{5,6},{6,5},{7,4},{8,11},{9,10},{10,... | collective-permute-start | bytes 393224 | tf_op jit(solution)/shard_map/ppermute | solution.py:41
  148.6 10.9 %collective-permute-start.31 = (bf16[64,1024]{1,0:T(8,128)(2,1)S(1)}, bf16[64,1024]{1,0:T(8,128)(2,1)S(1)}, u32[]{:S(2)}, u32[]{:S(2)}) collective-permute-start(bf16[64,1024]{1,0:T(8,128)(2,1)S(1)} %fusion.102), channel_id=1, source_target_pairs={{0,2},{1,3},{2,0},{3,1},{4,6},{5,7},{6,4},{7,5},{8,10},{9,11},{10,... | collective-permute-start | bytes 393224 | tf_op jit(solution)/shard_map/ppermute | solution.py:41
  148.6 10.9 %collective-permute-start.32 = (bf16[64,1024]{1,0:T(8,128)(2,1)S(1)}, bf16[64,1024]{1,0:T(8,128)(2,1)S(1)}, u32[]{:S(2)}, u32[]{:S(2)}) collective-permute-start(bf16[64,1024]{1,0:T(8,128)(2,1)S(1)} %fusion.102), channel_id=1, source_target_pairs={{0,1},{1,0},{2,3},{3,2},{4,5},{5,4},{6,7},{7,6},{8,9},{9,8},{10,11... | collective-permute-start | bytes 393224 | tf_op jit(solution)/shard_map/ppermute | solution.py:41
  152.1 12.3 %collective-permute-start.33 = (bf16[3,64,1152]{2,1,0:T(8,128)(2,1)S(1)}, bf16[3,64,1152]{2,1,0:T(8,128)(2,1)S(1)}, u32[]{:S(2)}, u32[]{:S(2)}) collective-permute-start(bf16[3,64,1152]{2,1,0:T(8,128)(2,1)S(1)} %get-tuple-element.192), channel_id=1, source_target_pairs={{0,8},{4,12},{8,0},{12,4},{16,24},{20,28},{24,16},{28,20},{1,9},{5... | collective-permute-start | bytes 1327112 | tf_op jit(solution)/shard_map/ppermute | solution.py:41
  154.8 11.0 %collective-permute-start.34 = (bf16[3,64,1152]{2,1,0:T(8,128)(2,1)S(1)}, bf16[3,64,1152]{2,1,0:T(8,128)(2,1)S(1)}, u32[]{:S(2)}, u32[]{:S(2)}) collective-permute-start(bf16[3,64,1152]{2,1,0:T(8,128)(2,1)S(1)} %get-tuple-element.191), channel_id=1, source_target_pairs={{0,16},{4,20},{8,24},{12,28},{16,0},{20,4},{24,8},{28,12},{1,17},{... | collective-permute-start | bytes 1327112 | tf_op jit(solution)/shard_map/ppermute | solution.py:41
  167.7 5.7 %collective-permute-start.35 = (bf16[2,256]{1,0:T(2,128)(2,1)S(1)}, bf16[2,256]{1,0:T(2,128)(2,1)S(1)}, u32[]{:S(2)}, u32[]{:S(2)}) collective-permute-start(bf16[2,256]{1,0:T(2,128)(2,1)S(1)} %slice.227), channel_id=1, source_target_pairs={{4,0},{8,4},{12,8},{16,12},{20,16},{24,20},{28,24},{5,1},{9,5},{13... | collective-permute-start | bytes 3080 | tf_op jit(solution)/shard_map/ppermute | solution.py:12
  169.3 22.7 %collective-permute-start.40 = (bf16[3,128,1152]{2,1,0:T(8,128)(2,1)S(1)}, bf16[3,128,1152]{2,1,0:T(8,128)(2,1)S(1)}, u32[]{:S(2)}, u32[]{:S(2)}) collective-permute-start(bf16[3,128,1152]{2,1,0:T(8,128)(2,1)S(1)} %pad_maximum_fusion.6), channel_id=1, source_target_pairs={{0,8},{4,12},{8,0},{12,4},{16,24},{20,28},{24,16},{28,20},{1,9},{5... | collective-permute-start | bytes 2654216 | tf_op jit(solution)/shard_map/ppermute | solution.py:41
  171.3 21.8 %collective-permute-start.41 = (bf16[3,128,1152]{2,1,0:T(8,128)(2,1)S(1)}, bf16[3,128,1152]{2,1,0:T(8,128)(2,1)S(1)}, u32[]{:S(2)}, u32[]{:S(2)}) collective-permute-start(bf16[3,128,1152]{2,1,0:T(8,128)(2,1)S(1)} %pad_maximum_fusion.7), channel_id=1, source_target_pairs={{0,16},{4,20},{8,24},{12,28},{16,0},{20,4},{24,8},{28,12},{1,17},{... | collective-permute-start | bytes 2654216 | tf_op jit(solution)/shard_map/ppermute | solution.py:41
  175.0 2.7 %collective-permute-start.36 = (bf16[4,512,256]{2,1,0:T(8,128)(2,1)S(1)}, bf16[4,512,256]{2,1,0:T(8,128)(2,1)S(1)}, u32[]{:S(2)}, u32[]{:S(2)}) collective-permute-start(bf16[4,512,256]{2,1,0:T(8,128)(2,1)S(1)} %pad_maximum_fusion.4), channel_id=1, source_target_pairs={{0,4},{4,0},{8,12},{12,8},{16,20},{20,16},{24,28},{28,24},{1,5},{5... | collective-permute-start | bytes 3145736 | tf_op jit(solution)/shard_map/ppermute | solution.py:41
  177.8 8.3 %collective-permute-start.39 = (bf16[64,1024]{1,0:T(8,128)(2,1)S(1)}, bf16[64,1024]{1,0:T(8,128)(2,1)S(1)}, u32[]{:S(2)}, u32[]{:S(2)}) collective-permute-start(bf16[64,1024]{1,0:T(8,128)(2,1)S(1)} %get-tuple-element.206), channel_id=1, source_target_pairs={{0,3},{1,2},{2,1},{3,0},{4,7},{5,6},{6,5},{7,4},{8,11},{9,10},{10,... | collective-permute-start | bytes 393224 | tf_op jit(solution)/shard_map/ppermute | solution.py:41
  179.9 11.6 %collective-permute-start.38 = (bf16[64,1024]{1,0:T(8,128)(2,1)S(1)}, bf16[64,1024]{1,0:T(8,128)(2,1)S(1)}, u32[]{:S(2)}, u32[]{:S(2)}) collective-permute-start(bf16[64,1024]{1,0:T(8,128)(2,1)S(1)} %get-tuple-element.205), channel_id=1, source_target_pairs={{0,2},{1,3},{2,0},{3,1},{4,6},{5,7},{6,4},{7,5},{8,10},{9,11},{10,... | collective-permute-start | bytes 393224 | tf_op jit(solution)/shard_map/ppermute | solution.py:41
  179.9 12.0 %collective-permute-start.37 = (bf16[64,1024]{1,0:T(8,128)(2,1)S(1)}, bf16[64,1024]{1,0:T(8,128)(2,1)S(1)}, u32[]{:S(2)}, u32[]{:S(2)}) collective-permute-start(bf16[64,1024]{1,0:T(8,128)(2,1)S(1)} %get-tuple-element.204), channel_id=1, source_target_pairs={{0,1},{1,0},{2,3},{3,2},{4,5},{5,4},{6,7},{7,6},{8,9},{9,8},{10,11... | collective-permute-start | bytes 393224 | tf_op jit(solution)/shard_map/ppermute | solution.py:41
  182.6 14.0 %copy-start.12 = (f32[64]{0:T(128)S(1)}, f32[64]{0:T(128)}, u32[]{:S(2)}) copy-start(f32[64]{0:T(128)} %copy-done.11) | copy-start | bytes 772
  186.1 8.4 %collective-permute-start.42 = (bf16[4,64,256]{2,1,0:T(8,128)(2,1)S(1)}, bf16[4,64,256]{2,1,0:T(8,128)(2,1)S(1)}, u32[]{:S(2)}, u32[]{:S(2)}) collective-permute-start(bf16[4,64,256]{2,1,0:T(8,128)(2,1)S(1)} %get-tuple-element.203), channel_id=1, source_target_pairs={{0,8},{4,12},{8,0},{12,4},{16,24},{20,28},{24,16},{28,20},{1,9},{5... | collective-permute-start | bytes 393224 | tf_op jit(solution)/shard_map/ppermute | solution.py:41
  191.5 5.0 %collective-permute-start.43 = (bf16[4,64,256]{2,1,0:T(8,128)(2,1)S(1)}, bf16[4,64,256]{2,1,0:T(8,128)(2,1)S(1)}, u32[]{:S(2)}, u32[]{:S(2)}) collective-permute-start(bf16[4,64,256]{2,1,0:T(8,128)(2,1)S(1)} %get-tuple-element.202), channel_id=1, source_target_pairs={{0,16},{4,20},{8,24},{12,28},{16,0},{20,4},{24,8},{28,12},{1,17},{... | collective-permute-start | bytes 393224 | tf_op jit(solution)/shard_map/ppermute | solution.py:41
  197.5 9.7 %collective-permute-start.46 = (f32[5,1024]{1,0:T(8,128)}, f32[5,1024]{1,0:T(8,128)S(1)}, u32[]{:S(2)}, u32[]{:S(2)}) collective-permute-start(f32[5,1024]{1,0:T(8,128)} %pad_maximum_fusion.15), channel_id=1, source_target_pairs={{0,1},{1,0},{2,3},{3,2},{4,5},{5,4},{6,7},{7,6},{8,9},{9,8},{10,11... | collective-permute-start | bytes 61448 | tf_op jit(solution)/shard_map/ppermute | solution.py:41
  197.5 9.7 %collective-permute-start.45 = (f32[5,1024]{1,0:T(8,128)}, f32[5,1024]{1,0:T(8,128)}, u32[]{:S(2)}, u32[]{:S(2)}) collective-permute-start(f32[5,1024]{1,0:T(8,128)} %pad_maximum_fusion.15), channel_id=1, source_target_pairs={{0,2},{1,3},{2,0},{3,1},{4,6},{5,7},{6,4},{7,5},{8,10},{9,11},{10,... | collective-permute-start | bytes 61448 | tf_op jit(solution)/shard_map/ppermute | solution.py:41
  200.1 7.1 %collective-permute-start.44 = (f32[5,1024]{1,0:T(8,128)}, f32[5,1024]{1,0:T(8,128)}, u32[]{:S(2)}, u32[]{:S(2)}) collective-permute-start(f32[5,1024]{1,0:T(8,128)} %pad_maximum_fusion.15), channel_id=1, source_target_pairs={{0,3},{1,2},{2,1},{3,0},{4,7},{5,6},{6,5},{7,4},{8,11},{9,10},{10,... | collective-permute-start | bytes 61448 | tf_op jit(solution)/shard_map/ppermute | solution.py:41
  202.4 6.4 %collective-permute-start.47 = (bf16[4,128,256]{2,1,0:T(8,128)(2,1)S(1)}, bf16[4,128,256]{2,1,0:T(8,128)(2,1)S(1)}, u32[]{:S(2)}, u32[]{:S(2)}) collective-permute-start(bf16[4,128,256]{2,1,0:T(8,128)(2,1)S(1)} %pad_maximum_fusion.13), channel_id=1, source_target_pairs={{0,8},{4,12},{8,0},{12,4},{16,24},{20,28},{24,16},{28,20},{1,9},{5... | collective-permute-start | bytes 786440 | tf_op jit(solution)/shard_map/ppermute | solution.py:41
  202.8 6.5 %collective-permute-start.48 = (bf16[4,128,256]{2,1,0:T(8,128)(2,1)S(1)}, bf16[4,128,256]{2,1,0:T(8,128)(2,1)}, u32[]{:S(2)}, u32[]{:S(2)}) collective-permute-start(bf16[4,128,256]{2,1,0:T(8,128)(2,1)S(1)} %pad_maximum_fusion.14), channel_id=1, source_target_pairs={{0,16},{4,20},{8,24},{12,28},{16,0},{20,4},{24,8},{28,12},{1,17},{... | collective-permute-start | bytes 786440 | tf_op jit(solution)/shard_map/ppermute | solution.py:41
  209.3 4.5 %collective-permute-start.55 = (f32[5,1024]{1,0:T(8,128)S(1)}, f32[5,1024]{1,0:T(8,128)S(1)}, u32[]{:S(2)}, u32[]{:S(2)}) collective-permute-start(f32[5,1024]{1,0:T(8,128)S(1)} %select_add_fusion.1), channel_id=1, source_target_pairs={{0,4},{4,0},{8,12},{12,8},{16,20},{20,16},{24,28},{28,24},{1,5},{5... | collective-permute-start | bytes 61448 | tf_op jit(solution)/shard_map/ppermute | solution.py:41
  209.3 6.9 %collective-permute-start.54 = (f32[5,1024]{1,0:T(8,128)S(1)}, f32[5,1024]{1,0:T(8,128)S(1)}, u32[]{:S(2)}, u32[]{:S(2)}) collective-permute-start(f32[5,1024]{1,0:T(8,128)S(1)} %select_add_fusion.1), channel_id=1, source_target_pairs={{0,8},{4,12},{8,0},{12,4},{16,24},{20,28},{24,16},{28,20},{1,9},{5... | collective-permute-start | bytes 61448 | tf_op jit(solution)/shard_map/ppermute | solution.py:41
  211.0 7.2 %collective-permute-start.53 = (f32[5,1024]{1,0:T(8,128)S(1)}, f32[5,1024]{1,0:T(8,128)S(1)}, u32[]{:S(2)}, u32[]{:S(2)}) collective-permute-start(f32[5,1024]{1,0:T(8,128)S(1)} %select_add_fusion.1), channel_id=1, source_target_pairs={{0,12},{4,8},{8,4},{12,0},{16,28},{20,24},{24,20},{28,16},{1,13},{... | collective-permute-start | bytes 61448 | tf_op jit(solution)/shard_map/ppermute | solution.py:41
  211.2 7.0 %collective-permute-start.52 = (f32[5,1024]{1,0:T(8,128)S(1)}, f32[5,1024]{1,0:T(8,128)S(1)}, u32[]{:S(2)}, u32[]{:S(2)}) collective-permute-start(f32[5,1024]{1,0:T(8,128)S(1)} %select_add_fusion.1), channel_id=1, source_target_pairs={{0,16},{4,20},{8,24},{12,28},{16,0},{20,4},{24,8},{28,12},{1,17},{... | collective-permute-start | bytes 61448 | tf_op jit(solution)/shard_map/ppermute | solution.py:41
  212.5 5.7 %collective-permute-start.51 = (f32[5,1024]{1,0:T(8,128)S(1)}, f32[5,1024]{1,0:T(8,128)S(1)}, u32[]{:S(2)}, u32[]{:S(2)}) collective-permute-start(f32[5,1024]{1,0:T(8,128)S(1)} %select_add_fusion.1), channel_id=1, source_target_pairs={{0,20},{4,16},{8,28},{12,24},{16,4},{20,0},{24,12},{28,8},{1,21},{... | collective-permute-start | bytes 61448 | tf_op jit(solution)/shard_map/ppermute | solution.py:41
  213.9 4.9 %collective-permute-start.50 = (f32[5,1024]{1,0:T(8,128)S(1)}, f32[5,1024]{1,0:T(8,128)S(1)}, u32[]{:S(2)}, u32[]{:S(2)}) collective-permute-start(f32[5,1024]{1,0:T(8,128)S(1)} %select_add_fusion.1), channel_id=1, source_target_pairs={{0,24},{4,28},{8,16},{12,20},{16,8},{20,12},{24,0},{28,4},{1,25},{... | collective-permute-start | bytes 61448 | tf_op jit(solution)/shard_map/ppermute | solution.py:41
  216.3 4.2 %collective-permute-start.49 = (f32[5,1024]{1,0:T(8,128)S(1)}, f32[5,1024]{1,0:T(8,128)S(1)}, u32[]{:S(2)}, u32[]{:S(2)}) collective-permute-start(f32[5,1024]{1,0:T(8,128)S(1)} %select_add_fusion.1), channel_id=1, source_target_pairs={{0,28},{4,24},{8,20},{12,16},{16,12},{20,8},{24,4},{28,0},{1,29},{... | collective-permute-start | bytes 61448 | tf_op jit(solution)/shard_map/ppermute | solution.py:41
  (20 other events, 112.9 us)

commit v5 on v4

--- a/solution.py
+++ b/solution.py
@@ -249,11 +249,11 @@
         + kernel[0] * second_keep * extended[:-2]
     )
     gated = narrow(c_value * mixed)
-    gated, ffn_gather = beside(gated, ffn_gather)
     mixer_part = jnp.concatenate(
         [times_trans(gated, mixer_near[3]), times_trans(gated, mixer_far[3])], axis=1
     )
     middle = residual + scatter_rows(for_owners(mixer_part))
+    middle, ffn_gather = beside(middle, ffn_gather)
     grad_rows = jnp.concatenate(grad_parts, axis=0)
     hidden_in = jnp.concatenate(
         gather_rows(narrow(rms_norm(middle, second_gain))), axis=0

time: 223 us -> 222 us (level)
  starting transfers between devices: 70.6 us -> 68 us
    ppermute x54, starting transfers between devices: 67.9 us -> 65.3 us  [swapped(): return lax.ppermute(block, axis, [(i, i ^ mask) for i in devices])]
    unnamed x69 -> x73, local copies, waits for them, and re-layouts: 10.7 us -> 11.6 us
  transfers between devices with their start and end apart: 56 -> 56, of which waited for: 26 -> 27; matrix products, arithmetic and copies ran while one was open for 16% -> 17% of each run, Pallas kernels for 0% -> 0%
where the time goes in v5:
time: 222 us; the launch traced here: 221 us
  waiting for transfers between devices  82.7 us (37%)
  starting transfers between devices  68 us (31%)
  matrix products  32.9 us (15%)
  local copies, waits for them, and re-layouts  22.5 us (10%)
  other arithmetic  12.4 us (6%)
    ppermute x54, waiting for transfers between devices, swapped(): return lax.ppermute(block, axis, [(i, i ^ mask) for i in devices])  82.3 us
    ppermute x54, starting transfers between devices, swapped(): return lax.ppermute(block, axis, [(i, i ^ mask) for i in devices])  65.3 us
    dot_general x14, matrix products, dot(): return jnp.dot(left, right, preferred_element_type=jnp.float32)  14.5 us
    dot_general x14, matrix products, times_trans(): lax.dot_general(left, right, (((1,), (1,)), ((), ())), preferred_element_...  12.9 us
    unnamed x73, local copies, waits for them, and re-layouts  11.6 us
    dot_general x14, matrix products, trans_times(): lax.dot_general(left, right, (((0,), (0,)), ((), ())), preferred_element_...  5.44 us
  transfers between devices with their start and end apart: 56, of which 27 were waited for; matrix products, arithmetic and copies ran while one was open for 17% of the time, Pallas kernels for 0%

profile of v5, /device:TPU:0, one launch (start us, length us, event | category | flops | bytes accessed | tf_op | source)
XLA Modules:
  0.0 220.6 jit_solution(2744196437282606927)
XLA Ops:
  6.1 3.1 %collective-permute-start = (bf16[64,1024]{1,0:T(8,128)(2,1)S(1)}, bf16[64,1024]{1,0:T(8,128)(2,1)S(1)}, u32[]{:S(2)}, u32[]{:S(2)}) collective-permute-start(bf16[64,1024]{1,0:T(8,128)(2,1)S(1)} %fusion.33), channel_id=1, source_target_pairs={{0,1},{1,0},{2,3},{3,2},{4,5},{5,4},{6,7},{7,6},{8,9},{9,8},{10,11... | collective-permute-start | bytes 393224 | tf_op jit(solution)/shard_map/ppermute | solution.py:41
  9.2 2.6 %collective-permute-start.1 = (bf16[64,1024]{1,0:T(8,128)(2,1)S(1)}, bf16[64,1024]{1,0:T(8,128)(2,1)S(1)}, u32[]{:S(2)}, u32[]{:S(2)}) collective-permute-start(bf16[64,1024]{1,0:T(8,128)(2,1)S(1)} %fusion.33), channel_id=1, source_target_pairs={{0,2},{1,3},{2,0},{3,1},{4,6},{5,7},{6,4},{7,5},{8,10},{9,11},{10,... | collective-permute-start | bytes 393224 | tf_op jit(solution)/shard_map/ppermute | solution.py:41
  11.7 1.7 collective-permute-start.3
  13.5 1.5 collective-permute-start.4
  15.3 1.4 pad_maximum_fusion.5
  17.6 4.8 %collective-permute-done.1 = bf16[64,1024]{1,0:T(8,128)(2,1)S(1)} collective-permute-done((bf16[64,1024]{1,0:T(8,128)(2,1)S(1)}, bf16[64,1024]{1,0:T(8,128)(2,1)S(1)}, u32[]{:S(2)}, u32[]{:S(2)}) %collective-permute-start.1) | collective-permute-done | bytes 131104 | tf_op jit(solution)/shard_map/ppermute | solution.py:41
  22.4 1.2 collective-permute-start.8
  23.6 1.6 collective-permute-start.10
  25.9 4.0 %collective-permute-done.10 = bf16[4,64,256]{2,1,0:T(8,128)(2,1)S(1)} collective-permute-done((bf16[4,64,256]{2,1,0:T(8,128)(2,1)S(1)}, bf16[4,64,256]{2,1,0:T(8,128)(2,1)S(1)}, u32[]{:S(2)}, u32[]{:S(2)}) %collective-permute-start.10) | collective-permute-done | bytes 131104 | tf_op jit(solution)/shard_map/ppermute | solution.py:41
  29.9 1.5 collective-permute-start.9
  31.4 12.6 %collective-permute-done.11 = bf16[4,64,256]{2,1,0:T(8,128)(2,1)S(1)} collective-permute-done((bf16[4,64,256]{2,1,0:T(8,128)(2,1)S(1)}, bf16[4,64,256]{2,1,0:T(8,128)(2,1)S(1)}, u32[]{:S(2)}, u32[]{:S(2)}) %collective-permute-start.11) | collective-permute-done | bytes 131104 | tf_op jit(solution)/shard_map/ppermute | solution.py:41
  45.8 1.7 collective-permute-start.7
  47.6 6.0 %collective-permute-done.7 = bf16[64,1024]{1,0:T(8,128)(2,1)S(1)} collective-permute-done((bf16[64,1024]{1,0:T(8,128)(2,1)S(1)}, bf16[64,1024]{1,0:T(8,128)(2,1)S(1)}, u32[]{:S(2)}, u32[]{:S(2)}) %collective-permute-start.7) | collective-permute-done | bytes 131104 | tf_op jit(solution)/shard_map/ppermute | solution.py:41
  54.7 1.6 collective-permute-start.17
  57.4 1.6 collective-permute-start.18
  58.9 2.2 constant_dynamic-update-slice_fusion.30
  62.8 1.5 collective-permute-start.13
  66.7 1.6 collective-permute-start.16
  68.4 3.3 %collective-permute-start.15 = (bf16[64,1024]{1,0:T(8,128)(2,1)S(1)}, bf16[64,1024]{1,0:T(8,128)(2,1)S(1)}, u32[]{:S(2)}, u32[]{:S(2)}) collective-permute-start(bf16[64,1024]{1,0:T(8,128)(2,1)S(1)} %get-tuple-element.205), channel_id=1, source_target_pairs={{0,2},{1,3},{2,0},{3,1},{4,6},{5,7},{6,4},{7,5},{8,10},{9,11},{10,... | collective-permute-start | bytes 393224 | tf_op jit(solution)/shard_map/ppermute | solution.py:41
  71.7 2.2 constant_dynamic-update-slice_fusion.29
  74.7 8.6 %collective-permute-done.15 = bf16[64,1024]{1,0:T(8,128)(2,1)S(1)} collective-permute-done((bf16[64,1024]{1,0:T(8,128)(2,1)S(1)}, bf16[64,1024]{1,0:T(8,128)(2,1)S(1)}, u32[]{:S(2)}, u32[]{:S(2)}) %collective-permute-start.15) | collective-permute-done | bytes 131104 | tf_op jit(solution)/shard_map/ppermute | solution.py:41
  89.1 1.7 collective-permute-start.22
  90.8 2.8 %collective-permute-start.20 = (bf16[64,1024]{1,0:T(8,128)(2,1)S(1)}, bf16[64,1024]{1,0:T(8,128)(2,1)S(1)}, u32[]{:S(2)}, u32[]{:S(2)}) collective-permute-start(bf16[64,1024]{1,0:T(8,128)(2,1)S(1)} %multiply_convert_fusion.7), channel_id=1, source_target_pairs={{0,1},{1,0},{2,3},{3,2},{4,5},{5,4},{6,7},{7,6},{8,9},{9,8},{10,11... | collective-permute-start | bytes 393224 | tf_op jit(solution)/shard_map/ppermute | solution.py:41
  93.6 1.8 fusion.20
  95.4 2.1 collective-permute-done.22
  97.4 5.0 %collective-permute-done.21 = bf16[64,1024]{1,0:T(8,128)(2,1)S(1)} collective-permute-done((bf16[64,1024]{1,0:T(8,128)(2,1)S(1)}, bf16[64,1024]{1,0:T(8,128)(2,1)S(1)}, u32[]{:S(2)}, u32[]{:S(2)}) %collective-permute-start.21) | collective-permute-done | bytes 131104 | tf_op jit(solution)/shard_map/ppermute | solution.py:41
  102.5 1.8 fusion.25
  104.3 1.8 convolution_add_fusion
  106.1 1.8 fusion.23
  107.9 1.8 convolution_add_fusion.2
  109.7 2.2 multiply_convert_fusion
  111.9 1.8 fusion.19
  114.2 1.8 fusion.24
  118.8 1.8 fusion.21
  120.7 1.6 collective-permute-start.25
  122.4 2.8 %collective-permute-start.23 = (bf16[64,1024]{1,0:T(8,128)(2,1)S(1)}, bf16[64,1024]{1,0:T(8,128)(2,1)S(1)}, u32[]{:S(2)}, u32[]{:S(2)}) collective-permute-start(bf16[64,1024]{1,0:T(8,128)(2,1)S(1)} %get-tuple-element.216), channel_id=1, source_target_pairs={{0,1},{1,0},{2,3},{3,2},{4,5},{5,4},{6,7},{7,6},{8,9},{9,8},{10,11... | collective-permute-start | bytes 393224 | tf_op jit(solution)/shard_map/ppermute | solution.py:41
  125.8 1.8 fusion.22
  127.6 1.8 convolution_add_fusion.4
  129.4 1.8 convolution_add_fusion.3
  131.3 2.3 %collective-permute-done.24 = bf16[64,1024]{1,0:T(8,128)(2,1)S(1)} collective-permute-done((bf16[64,1024]{1,0:T(8,128)(2,1)S(1)}, bf16[64,1024]{1,0:T(8,128)(2,1)S(1)}, u32[]{:S(2)}, u32[]{:S(2)}) %collective-permute-start.24) | collective-permute-done | bytes 131104 | tf_op jit(solution)/shard_map/ppermute | solution.py:41
  133.8 2.1 collective-permute-start.28
  136.0 2.3 %collective-permute-start.26 = (bf16[64,1024]{1,0:T(8,128)(2,1)S(1)}, bf16[64,1024]{1,0:T(8,128)(2,1)S(1)}, u32[]{:S(2)}, u32[]{:S(2)}) collective-permute-start(bf16[64,1024]{1,0:T(8,128)(2,1)S(1)} %get-tuple-element.213), channel_id=1, source_target_pairs={{0,1},{1,0},{2,3},{3,2},{4,5},{5,4},{6,7},{7,6},{8,9},{9,8},{10,11... | collective-permute-start | bytes 393224 | tf_op jit(solution)/shard_map/ppermute | solution.py:41
  138.5 3.6 %collective-permute-done.28 = bf16[64,1024]{1,0:T(8,128)(2,1)S(1)} collective-permute-done((bf16[64,1024]{1,0:T(8,128)(2,1)S(1)}, bf16[64,1024]{1,0:T(8,128)(2,1)S(1)}, u32[]{:S(2)}, u32[]{:S(2)}) %collective-permute-start.28) | collective-permute-done | bytes 131104 | tf_op jit(solution)/shard_map/ppermute | solution.py:41
  142.2 4.6 %collective-permute-done.27 = bf16[64,1024]{1,0:T(8,128)(2,1)S(1)} collective-permute-done((bf16[64,1024]{1,0:T(8,128)(2,1)S(1)}, bf16[64,1024]{1,0:T(8,128)(2,1)S(1)}, u32[]{:S(2)}, u32[]{:S(2)}) %collective-permute-start.27) | collective-permute-done | bytes 131104 | tf_op jit(solution)/shard_map/ppermute | solution.py:41
  147.2 2.1 collective-permute-start.30
  149.3 2.3 %collective-permute-start.32 = (bf16[64,1024]{1,0:T(8,128)(2,1)S(1)}, bf16[64,1024]{1,0:T(8,128)(2,1)S(1)}, u32[]{:S(2)}, u32[]{:S(2)}) collective-permute-start(bf16[64,1024]{1,0:T(8,128)(2,1)S(1)} %fusion.102), channel_id=1, source_target_pairs={{0,1},{1,0},{2,3},{3,2},{4,5},{5,4},{6,7},{7,6},{8,9},{9,8},{10,11... | collective-permute-start | bytes 393224 | tf_op jit(solution)/shard_map/ppermute | solution.py:41
  152.8 1.8 collective-permute-start.33
  155.5 4.7 %collective-permute-done.31 = bf16[64,1024]{1,0:T(8,128)(2,1)S(1)} collective-permute-done((bf16[64,1024]{1,0:T(8,128)(2,1)S(1)}, bf16[64,1024]{1,0:T(8,128)(2,1)S(1)}, u32[]{:S(2)}, u32[]{:S(2)}) %collective-permute-start.31) | collective-permute-done | bytes 131104 | tf_op jit(solution)/shard_map/ppermute | solution.py:41
  160.3 3.8 %collective-permute-done.33 = bf16[3,64,1152]{2,1,0:T(8,128)(2,1)S(1)} collective-permute-done((bf16[3,64,1152]{2,1,0:T(8,128)(2,1)S(1)}, bf16[3,64,1152]{2,1,0:T(8,128)(2,1)S(1)}, u32[]{:S(2)}, u32[]{:S(2)}) %collective-permute-start.33) | collective-permute-done | bytes 442400 | tf_op jit(solution)/shard_map/ppermute | solution.py:41
  164.1 1.5 collective-permute-done.34
  167.5 1.3 collective-permute-start.35
  170.3 1.6 collective-permute-start.41
  175.1 1.4 collective-permute-done.36
  176.6 2.0 collective-permute-start.39
  178.6 2.5 %collective-permute-start.37 = (bf16[64,1024]{1,0:T(8,128)(2,1)S(1)}, bf16[64,1024]{1,0:T(8,128)(2,1)S(1)}, u32[]{:S(2)}, u32[]{:S(2)}) collective-permute-start(bf16[64,1024]{1,0:T(8,128)(2,1)S(1)} %get-tuple-element.202), channel_id=1, source_target_pairs={{0,1},{1,0},{2,3},{3,2},{4,5},{5,4},{6,7},{7,6},{8,9},{9,8},{10,11... | collective-permute-start | bytes 393224 | tf_op jit(solution)/shard_map/ppermute | solution.py:41
  181.4 3.5 %collective-permute-done.39 = bf16[64,1024]{1,0:T(8,128)(2,1)S(1)} collective-permute-done((bf16[64,1024]{1,0:T(8,128)(2,1)S(1)}, bf16[64,1024]{1,0:T(8,128)(2,1)S(1)}, u32[]{:S(2)}, u32[]{:S(2)}) %collective-permute-start.39) | collective-permute-done | bytes 131104 | tf_op jit(solution)/shard_map/ppermute | solution.py:41
  185.4 5.0 %collective-permute-done.38 = bf16[64,1024]{1,0:T(8,128)(2,1)S(1)} collective-permute-done((bf16[64,1024]{1,0:T(8,128)(2,1)S(1)}, bf16[64,1024]{1,0:T(8,128)(2,1)S(1)}, u32[]{:S(2)}, u32[]{:S(2)}) %collective-permute-start.38) | collective-permute-done | bytes 131104 | tf_op jit(solution)/shard_map/ppermute | solution.py:41
  192.1 2.3 %collective-permute-done.42 = bf16[4,64,256]{2,1,0:T(8,128)(2,1)S(1)} collective-permute-done((bf16[4,64,256]{2,1,0:T(8,128)(2,1)S(1)}, bf16[4,64,256]{2,1,0:T(8,128)(2,1)S(1)}, u32[]{:S(2)}, u32[]{:S(2)}) %collective-permute-start.42) | collective-permute-done | bytes 131104 | tf_op jit(solution)/shard_map/ppermute | solution.py:41
  196.3 2.5 %collective-permute-start.45 = (f32[5,1024]{1,0:T(8,128)}, f32[5,1024]{1,0:T(8,128)}, u32[]{:S(2)}, u32[]{:S(2)}) collective-permute-start(f32[5,1024]{1,0:T(8,128)} %pad_maximum_fusion.15), channel_id=1, source_target_pairs={{0,2},{1,3},{2,0},{3,1},{4,6},{5,7},{6,4},{7,5},{8,10},{9,11},{10,... | collective-permute-start | bytes 61448 | tf_op jit(solution)/shard_map/ppermute | solution.py:41
  198.8 1.9 collective-permute-start.44
  201.2 1.4 collective-permute-start.47
  208.1 1.2 collective-permute-done.48
  209.9 1.2 collective-permute-start.53
  215.1 1.7 collective-permute-start.49
  (294 shorter events, 53.6 us)
Async XLA Ops:
  1.5 13.5 %copy-start.5 = (bf16[1152,128]{1,0:T(8,128)(2,1)S(1)}, bf16[1152,128]{1,0:T(8,128)(2,1)}, u32[]{:S(2)}) copy-start(bf16[1152,128]{1,0:T(8,128)(2,1)} %param.17) | copy-start | bytes 884740
  6.1 10.8 %collective-permute-start = (bf16[64,1024]{1,0:T(8,128)(2,1)S(1)}, bf16[64,1024]{1,0:T(8,128)(2,1)S(1)}, u32[]{:S(2)}, u32[]{:S(2)}) collective-permute-start(bf16[64,1024]{1,0:T(8,128)(2,1)S(1)} %fusion.33), channel_id=1, source_target_pairs={{0,1},{1,0},{2,3},{3,2},{4,5},{5,4},{6,7},{7,6},{8,9},{9,8},{10,11... | collective-permute-start | bytes 393224 | tf_op jit(solution)/shard_map/ppermute | solution.py:41
  9.2 13.3 %collective-permute-start.1 = (bf16[64,1024]{1,0:T(8,128)(2,1)S(1)}, bf16[64,1024]{1,0:T(8,128)(2,1)S(1)}, u32[]{:S(2)}, u32[]{:S(2)}) collective-permute-start(bf16[64,1024]{1,0:T(8,128)(2,1)S(1)} %fusion.33), channel_id=1, source_target_pairs={{0,2},{1,3},{2,0},{3,1},{4,6},{5,7},{6,4},{7,5},{8,10},{9,11},{10,... | collective-permute-start | bytes 393224 | tf_op jit(solution)/shard_map/ppermute | solution.py:41
  11.7 10.7 %collective-permute-start.2 = (bf16[64,1024]{1,0:T(8,128)(2,1)S(1)}, bf16[64,1024]{1,0:T(8,128)(2,1)S(1)}, u32[]{:S(2)}, u32[]{:S(2)}) collective-permute-start(bf16[64,1024]{1,0:T(8,128)(2,1)S(1)} %fusion.33), channel_id=1, source_target_pairs={{0,3},{1,2},{2,1},{3,0},{4,7},{5,6},{6,5},{7,4},{8,11},{9,10},{10,... | collective-permute-start | bytes 393224 | tf_op jit(solution)/shard_map/ppermute | solution.py:41
  11.7 11.9 %collective-permute-start.3 = (bf16[4,128,256]{2,1,0:T(8,128)(2,1)S(1)}, bf16[4,128,256]{2,1,0:T(8,128)(2,1)S(1)}, u32[]{:S(2)}, u32[]{:S(2)}) collective-permute-start(bf16[4,128,256]{2,1,0:T(8,128)(2,1)S(1)} %pad_maximum_fusion.12), channel_id=1, source_target_pairs={{0,8},{4,12},{8,0},{12,4},{16,24},{20,28},{24,16},{28,20},{1,9},{5... | collective-permute-start | bytes 786440 | tf_op jit(solution)/shard_map/ppermute | solution.py:41
  13.5 10.1 %collective-permute-start.4 = (bf16[4,128,256]{2,1,0:T(8,128)(2,1)S(1)}, bf16[4,128,256]{2,1,0:T(8,128)(2,1)S(1)}, u32[]{:S(2)}, u32[]{:S(2)}) collective-permute-start(bf16[4,128,256]{2,1,0:T(8,128)(2,1)S(1)} %pad_maximum_fusion.12), channel_id=1, source_target_pairs={{0,16},{4,20},{8,24},{12,28},{16,0},{20,4},{24,8},{28,12},{1,17},{... | collective-permute-start | bytes 786440 | tf_op jit(solution)/shard_map/ppermute | solution.py:41
  16.8 30.7 %copy-start.4 = (bf16[64,1024]{1,0:T(8,128)(2,1)}, bf16[64,1024]{1,0:T(8,128)(2,1)S(1)}, u32[]{:S(2)}) copy-start(bf16[64,1024]{1,0:T(8,128)(2,1)S(1)} %slice.208) | copy-start | bytes 393220
  16.9 28.9 %collective-permute-start.5 = (bf16[64,1024]{1,0:T(8,128)(2,1)S(1)}, bf16[64,1024]{1,0:T(8,128)(2,1)}, u32[]{:S(2)}, u32[]{:S(2)}) collective-permute-start(bf16[64,1024]{1,0:T(8,128)(2,1)S(1)} %slice.208), channel_id=1, source_target_pairs={{0,1},{1,0},{2,3},{3,2},{4,5},{5,4},{6,7},{7,6},{8,9},{9,8},{10,11... | collective-permute-start | bytes 393224 | tf_op jit(solution)/shard_map/ppermute | solution.py:41
  22.4 25.2 %collective-permute-start.6 = (bf16[64,1024]{1,0:T(8,128)(2,1)S(1)}, bf16[64,1024]{1,0:T(8,128)(2,1)}, u32[]{:S(2)}, u32[]{:S(2)}) collective-permute-start(bf16[64,1024]{1,0:T(8,128)(2,1)S(1)} %slice.208), channel_id=1, source_target_pairs={{0,2},{1,3},{2,0},{3,1},{4,6},{5,7},{6,4},{7,5},{8,10},{9,11},{10,... | collective-permute-start | bytes 393224 | tf_op jit(solution)/shard_map/ppermute | solution.py:41
  22.4 31.1 %collective-permute-start.8 = (bf16[3,128,1152]{2,1,0:T(8,128)(2,1)}, bf16[3,128,1152]{2,1,0:T(8,128)(2,1)}, u32[]{:S(2)}, u32[]{:S(2)}) collective-permute-start(bf16[3,128,1152]{2,1,0:T(8,128)(2,1)} %get-tuple-element.207), channel_id=1, source_target_pairs={{0,8},{4,12},{8,0},{12,4},{16,24},{20,28},{24,16},{28,20},{1,9},{5... | collective-permute-start | bytes 2654216 | tf_op jit(solution)/shard_map/ppermute | solution.py:41
  23.6 6.3 %collective-permute-start.10 = (bf16[4,64,256]{2,1,0:T(8,128)(2,1)S(1)}, bf16[4,64,256]{2,1,0:T(8,128)(2,1)S(1)}, u32[]{:S(2)}, u32[]{:S(2)}) collective-permute-start(bf16[4,64,256]{2,1,0:T(8,128)(2,1)S(1)} %split.306), channel_id=1, source_target_pairs={{0,16},{4,20},{8,24},{12,28},{16,0},{20,4},{24,8},{28,12},{1,17},{... | collective-permute-start | bytes 393224 | tf_op jit(solution)/shard_map/ppermute | solution.py:41
  25.2 18.8 %collective-permute-start.11 = (bf16[4,64,256]{2,1,0:T(8,128)(2,1)S(1)}, bf16[4,64,256]{2,1,0:T(8,128)(2,1)S(1)}, u32[]{:S(2)}, u32[]{:S(2)}) collective-permute-start(bf16[4,64,256]{2,1,0:T(8,128)(2,1)S(1)} %split.307), channel_id=1, source_target_pairs={{0,8},{4,12},{8,0},{12,4},{16,24},{20,28},{24,16},{28,20},{1,9},{5... | collective-permute-start | bytes 393224 | tf_op jit(solution)/shard_map/ppermute | solution.py:41
  29.9 23.7 %collective-permute-start.9 = (bf16[3,128,1152]{2,1,0:T(8,128)(2,1)}, bf16[3,128,1152]{2,1,0:T(8,128)(2,1)}, u32[]{:S(2)}, u32[]{:S(2)}) collective-permute-start(bf16[3,128,1152]{2,1,0:T(8,128)(2,1)} %get-tuple-element.207), channel_id=1, source_target_pairs={{0,16},{4,20},{8,24},{12,28},{16,0},{20,4},{24,8},{28,12},{1,17},{... | collective-permute-start | bytes 2654216 | tf_op jit(solution)/shard_map/ppermute | solution.py:41
  44.1 17.1 %collective-permute-start.12 = (bf16[4,512,256]{2,1,0:T(8,128)(2,1)S(1)}, bf16[4,512,256]{2,1,0:T(8,128)(2,1)S(1)}, u32[]{:S(2)}, u32[]{:S(2)}) collective-permute-start(bf16[4,512,256]{2,1,0:T(8,128)(2,1)S(1)} %constant_dynamic-update-slice_fusion.22), channel_id=1, source_target_pairs={{0,4},{4,0},{8,12},{12,8},{16,20},{20,16},{24,28},{28,24},{1,5},{5... | collective-permute-start | bytes 3145736 | tf_op jit(solution)/shard_map/ppermute | solution.py:41
  45.8 19.2 %copy-start.15 = (f32[1,256]{1,0:T(1,128)}, f32[1,256]{1,0:T(1,128)S(1)}, u32[]{:S(2)}) copy-start(f32[1,256]{1,0:T(1,128)S(1)} %get-tuple-element.229) | copy-start | bytes 3076
  45.8 19.2 %copy-start.17 = (f32[1,256]{1,0:T(1,128)}, f32[1,256]{1,0:T(1,128)S(1)}, u32[]{:S(2)}) copy-start(f32[1,256]{1,0:T(1,128)S(1)} %get-tuple-element.230) | copy-start | bytes 3076
  45.8 19.2 %copy-start.19 = (f32[1,256]{1,0:T(1,128)}, f32[1,256]{1,0:T(1,128)S(1)}, u32[]{:S(2)}) copy-start(f32[1,256]{1,0:T(1,128)S(1)} %get-tuple-element.231) | copy-start | bytes 3076
  45.8 7.8 %collective-permute-start.7 = (bf16[64,1024]{1,0:T(8,128)(2,1)S(1)}, bf16[64,1024]{1,0:T(8,128)(2,1)S(1)}, u32[]{:S(2)}, u32[]{:S(2)}) collective-permute-start(bf16[64,1024]{1,0:T(8,128)(2,1)S(1)} %slice.208), channel_id=1, source_target_pairs={{0,3},{1,2},{2,1},{3,0},{4,7},{5,6},{6,5},{7,4},{8,11},{9,10},{10,... | collective-permute-start | bytes 393224 | tf_op jit(solution)/shard_map/ppermute | solution.py:41
  54.7 28.7 %collective-permute-start.17 = (bf16[3,64,1152]{2,1,0:T(8,128)(2,1)S(1)}, bf16[3,64,1152]{2,1,0:T(8,128)(2,1)S(1)}, u32[]{:S(2)}, u32[]{:S(2)}) collective-permute-start(bf16[3,64,1152]{2,1,0:T(8,128)(2,1)S(1)} %split.313), channel_id=1, source_target_pairs={{0,16},{4,20},{8,24},{12,28},{16,0},{20,4},{24,8},{28,12},{1,17},{... | collective-permute-start | bytes 1327112 | tf_op jit(solution)/shard_map/ppermute | solution.py:41
  57.4 26.1 %collective-permute-start.18 = (bf16[3,64,1152]{2,1,0:T(8,128)(2,1)S(1)}, bf16[3,64,1152]{2,1,0:T(8,128)(2,1)S(1)}, u32[]{:S(2)}, u32[]{:S(2)}) collective-permute-start(bf16[3,64,1152]{2,1,0:T(8,128)(2,1)S(1)} %split.314), channel_id=1, source_target_pairs={{0,8},{4,12},{8,0},{12,4},{16,24},{20,28},{24,16},{28,20},{1,9},{5... | collective-permute-start | bytes 1327112 | tf_op jit(solution)/shard_map/ppermute | solution.py:41
  62.8 2.1 collective-permute-start.13
  66.7 8.0 %collective-permute-start.16 = (bf16[64,1024]{1,0:T(8,128)(2,1)S(1)}, bf16[64,1024]{1,0:T(8,128)(2,1)S(1)}, u32[]{:S(2)}, u32[]{:S(2)}) collective-permute-start(bf16[64,1024]{1,0:T(8,128)(2,1)S(1)} %get-tuple-element.206), channel_id=1, source_target_pairs={{0,3},{1,2},{2,1},{3,0},{4,7},{5,6},{6,5},{7,4},{8,11},{9,10},{10,... | collective-permute-start | bytes 393224 | tf_op jit(solution)/shard_map/ppermute | solution.py:41
  68.4 14.9 %collective-permute-start.15 = (bf16[64,1024]{1,0:T(8,128)(2,1)S(1)}, bf16[64,1024]{1,0:T(8,128)(2,1)S(1)}, u32[]{:S(2)}, u32[]{:S(2)}) collective-permute-start(bf16[64,1024]{1,0:T(8,128)(2,1)S(1)} %get-tuple-element.205), channel_id=1, source_target_pairs={{0,2},{1,3},{2,0},{3,1},{4,6},{5,7},{6,4},{7,5},{8,10},{9,11},{10,... | collective-permute-start | bytes 393224 | tf_op jit(solution)/shard_map/ppermute | solution.py:41
  71.7 11.6 %collective-permute-start.14 = (bf16[64,1024]{1,0:T(8,128)(2,1)S(1)}, bf16[64,1024]{1,0:T(8,128)(2,1)S(1)}, u32[]{:S(2)}, u32[]{:S(2)}) collective-permute-start(bf16[64,1024]{1,0:T(8,128)(2,1)S(1)} %get-tuple-element.148), channel_id=1, source_target_pairs={{0,1},{1,0},{2,3},{3,2},{4,5},{5,4},{6,7},{7,6},{8,9},{9,8},{10,11... | collective-permute-start | bytes 393224 | tf_op jit(solution)/shard_map/ppermute | solution.py:41
  85.1 17.4 %collective-permute-start.19 = (bf16[3,512,1152]{2,1,0:T(8,128)(2,1)}, bf16[3,512,1152]{2,1,0:T(8,128)(2,1)}, u32[]{:S(2)}, u32[]{:S(2)}) collective-permute-start(bf16[3,512,1152]{2,1,0:T(8,128)(2,1)} %constant_dynamic-update-slice_fusion.27), channel_id=1, source_target_pairs={{0,4},{4,0},{8,12},{12,8},{16,20},{20,16},{24,28},{28,24},{1,5},{5... | collective-permute-start | bytes 10616840 | tf_op jit(solution)/shard_map/ppermute | solution.py:41
  89.1 8.4 %collective-permute-start.22 = (bf16[64,1024]{1,0:T(8,128)(2,1)S(1)}, bf16[64,1024]{1,0:T(8,128)(2,1)S(1)}, u32[]{:S(2)}, u32[]{:S(2)}) collective-permute-start(bf16[64,1024]{1,0:T(8,128)(2,1)S(1)} %multiply_convert_fusion.7), channel_id=1, source_target_pairs={{0,3},{1,2},{2,1},{3,0},{4,7},{5,6},{6,5},{7,4},{8,11},{9,10},{10,... | collective-permute-start | bytes 393224 | tf_op jit(solution)/shard_map/ppermute | solution.py:41
  90.8 11.6 %collective-permute-start.21 = (bf16[64,1024]{1,0:T(8,128)(2,1)S(1)}, bf16[64,1024]{1,0:T(8,128)(2,1)S(1)}, u32[]{:S(2)}, u32[]{:S(2)}) collective-permute-start(bf16[64,1024]{1,0:T(8,128)(2,1)S(1)} %multiply_convert_fusion.7), channel_id=1, source_target_pairs={{0,2},{1,3},{2,0},{3,1},{4,6},{5,7},{6,4},{7,5},{8,10},{9,11},{10,... | collective-permute-start | bytes 393224 | tf_op jit(solution)/shard_map/ppermute | solution.py:41
  90.8 11.6 %collective-permute-start.20 = (bf16[64,1024]{1,0:T(8,128)(2,1)S(1)}, bf16[64,1024]{1,0:T(8,128)(2,1)S(1)}, u32[]{:S(2)}, u32[]{:S(2)}) collective-permute-start(bf16[64,1024]{1,0:T(8,128)(2,1)S(1)} %multiply_convert_fusion.7), channel_id=1, source_target_pairs={{0,1},{1,0},{2,3},{3,2},{4,5},{5,4},{6,7},{7,6},{8,9},{9,8},{10,11... | collective-permute-start | bytes 393224 | tf_op jit(solution)/shard_map/ppermute | solution.py:41
  120.7 10.6 %collective-permute-start.25 = (bf16[64,1024]{1,0:T(8,128)(2,1)S(1)}, bf16[64,1024]{1,0:T(8,128)(2,1)S(1)}, u32[]{:S(2)}, u32[]{:S(2)}) collective-permute-start(bf16[64,1024]{1,0:T(8,128)(2,1)S(1)} %get-tuple-element.217), channel_id=1, source_target_pairs={{0,3},{1,2},{2,1},{3,0},{4,7},{5,6},{6,5},{7,4},{8,11},{9,10},{10,... | collective-permute-start | bytes 393224 | tf_op jit(solution)/shard_map/ppermute | solution.py:41
  122.4 11.3 %collective-permute-start.24 = (bf16[64,1024]{1,0:T(8,128)(2,1)S(1)}, bf16[64,1024]{1,0:T(8,128)(2,1)S(1)}, u32[]{:S(2)}, u32[]{:S(2)}) collective-permute-start(bf16[64,1024]{1,0:T(8,128)(2,1)S(1)} %get-tuple-element.218), channel_id=1, source_target_pairs={{0,2},{1,3},{2,0},{3,1},{4,6},{5,7},{6,4},{7,5},{8,10},{9,11},{10,... | collective-permute-start | bytes 393224 | tf_op jit(solution)/shard_map/ppermute | solution.py:41
  122.4 11.3 %collective-permute-start.23 = (bf16[64,1024]{1,0:T(8,128)(2,1)S(1)}, bf16[64,1024]{1,0:T(8,128)(2,1)S(1)}, u32[]{:S(2)}, u32[]{:S(2)}) collective-permute-start(bf16[64,1024]{1,0:T(8,128)(2,1)S(1)} %get-tuple-element.216), channel_id=1, source_target_pairs={{0,1},{1,0},{2,3},{3,2},{4,5},{5,4},{6,7},{7,6},{8,9},{9,8},{10,11... | collective-permute-start | bytes 393224 | tf_op jit(solution)/shard_map/ppermute | solution.py:41
  125.7 21.1 %collective-permute-start.29 = (bf16[3,512,1152]{2,1,0:T(8,128)(2,1)S(1)}, bf16[3,512,1152]{2,1,0:T(8,128)(2,1)S(1)}, u32[]{:S(2)}, u32[]{:S(2)}) collective-permute-start(bf16[3,512,1152]{2,1,0:T(8,128)(2,1)S(1)} %pad_maximum_fusion), channel_id=1, source_target_pairs={{0,4},{4,0},{8,12},{12,8},{16,20},{20,16},{24,28},{28,24},{1,5},{5... | collective-permute-start | bytes 10616840 | tf_op jit(solution)/shard_map/ppermute | solution.py:41
  133.8 8.3 %collective-permute-start.28 = (bf16[64,1024]{1,0:T(8,128)(2,1)S(1)}, bf16[64,1024]{1,0:T(8,128)(2,1)S(1)}, u32[]{:S(2)}, u32[]{:S(2)}) collective-permute-start(bf16[64,1024]{1,0:T(8,128)(2,1)S(1)} %get-tuple-element.214), channel_id=1, source_target_pairs={{0,3},{1,2},{2,1},{3,0},{4,7},{5,6},{6,5},{7,4},{8,11},{9,10},{10,... | collective-permute-start | bytes 393224 | tf_op jit(solution)/shard_map/ppermute | solution.py:41
  136.0 10.8 %collective-permute-start.27 = (bf16[64,1024]{1,0:T(8,128)(2,1)S(1)}, bf16[64,1024]{1,0:T(8,128)(2,1)S(1)}, u32[]{:S(2)}, u32[]{:S(2)}) collective-permute-start(bf16[64,1024]{1,0:T(8,128)(2,1)S(1)} %get-tuple-element.215), channel_id=1, source_target_pairs={{0,2},{1,3},{2,0},{3,1},{4,6},{5,7},{6,4},{7,5},{8,10},{9,11},{10,... | collective-permute-start | bytes 393224 | tf_op jit(solution)/shard_map/ppermute | solution.py:41
  136.0 10.8 %collective-permute-start.26 = (bf16[64,1024]{1,0:T(8,128)(2,1)S(1)}, bf16[64,1024]{1,0:T(8,128)(2,1)S(1)}, u32[]{:S(2)}, u32[]{:S(2)}) collective-permute-start(bf16[64,1024]{1,0:T(8,128)(2,1)S(1)} %get-tuple-element.213), channel_id=1, source_target_pairs={{0,1},{1,0},{2,3},{3,2},{4,5},{5,4},{6,7},{7,6},{8,9},{9,8},{10,11... | collective-permute-start | bytes 393224 | tf_op jit(solution)/shard_map/ppermute | solution.py:41
  147.2 8.3 %collective-permute-start.30 = (bf16[64,1024]{1,0:T(8,128)(2,1)S(1)}, bf16[64,1024]{1,0:T(8,128)(2,1)S(1)}, u32[]{:S(2)}, u32[]{:S(2)}) collective-permute-start(bf16[64,1024]{1,0:T(8,128)(2,1)S(1)} %fusion.102), channel_id=1, source_target_pairs={{0,3},{1,2},{2,1},{3,0},{4,7},{5,6},{6,5},{7,4},{8,11},{9,10},{10,... | collective-permute-start | bytes 393224 | tf_op jit(solution)/shard_map/ppermute | solution.py:41
  149.3 10.9 %collective-permute-start.31 = (bf16[64,1024]{1,0:T(8,128)(2,1)S(1)}, bf16[64,1024]{1,0:T(8,128)(2,1)S(1)}, u32[]{:S(2)}, u32[]{:S(2)}) collective-permute-start(bf16[64,1024]{1,0:T(8,128)(2,1)S(1)} %fusion.102), channel_id=1, source_target_pairs={{0,2},{1,3},{2,0},{3,1},{4,6},{5,7},{6,4},{7,5},{8,10},{9,11},{10,... | collective-permute-start | bytes 393224 | tf_op jit(solution)/shard_map/ppermute | solution.py:41
  149.3 10.9 %collective-permute-start.32 = (bf16[64,1024]{1,0:T(8,128)(2,1)S(1)}, bf16[64,1024]{1,0:T(8,128)(2,1)S(1)}, u32[]{:S(2)}, u32[]{:S(2)}) collective-permute-start(bf16[64,1024]{1,0:T(8,128)(2,1)S(1)} %fusion.102), channel_id=1, source_target_pairs={{0,1},{1,0},{2,3},{3,2},{4,5},{5,4},{6,7},{7,6},{8,9},{9,8},{10,11... | collective-permute-start | bytes 393224 | tf_op jit(solution)/shard_map/ppermute | solution.py:41
  152.8 11.3 %collective-permute-start.33 = (bf16[3,64,1152]{2,1,0:T(8,128)(2,1)S(1)}, bf16[3,64,1152]{2,1,0:T(8,128)(2,1)S(1)}, u32[]{:S(2)}, u32[]{:S(2)}) collective-permute-start(bf16[3,64,1152]{2,1,0:T(8,128)(2,1)S(1)} %get-tuple-element.190), channel_id=1, source_target_pairs={{0,8},{4,12},{8,0},{12,4},{16,24},{20,28},{24,16},{28,20},{1,9},{5... | collective-permute-start | bytes 1327112 | tf_op jit(solution)/shard_map/ppermute | solution.py:41
  154.6 11.0 %collective-permute-start.34 = (bf16[3,64,1152]{2,1,0:T(8,128)(2,1)S(1)}, bf16[3,64,1152]{2,1,0:T(8,128)(2,1)S(1)}, u32[]{:S(2)}, u32[]{:S(2)}) collective-permute-start(bf16[3,64,1152]{2,1,0:T(8,128)(2,1)S(1)} %get-tuple-element.189), channel_id=1, source_target_pairs={{0,16},{4,20},{8,24},{12,28},{16,0},{20,4},{24,8},{28,12},{1,17},{... | collective-permute-start | bytes 1327112 | tf_op jit(solution)/shard_map/ppermute | solution.py:41
  154.7 40.9 %copy-start.11 = (f32[1024]{0:T(1024)}, f32[1024]{0:T(1024)S(1)}, u32[]{:S(2)}) copy-start(f32[1024]{0:T(1024)S(1)} %constant_dynamic-update-slice_fusion.57) | copy-start | bytes 12292
  167.5 4.7 %collective-permute-start.35 = (bf16[2,256]{1,0:T(2,128)(2,1)S(1)}, bf16[2,256]{1,0:T(2,128)(2,1)S(1)}, u32[]{:S(2)}, u32[]{:S(2)}) collective-permute-start(bf16[2,256]{1,0:T(2,128)(2,1)S(1)} %slice.227), channel_id=1, source_target_pairs={{4,0},{8,4},{12,8},{16,12},{20,16},{24,20},{28,24},{5,1},{9,5},{13... | collective-permute-start | bytes 3080 | tf_op jit(solution)/shard_map/ppermute | solution.py:12
  169.2 22.4 %collective-permute-start.40 = (bf16[3,128,1152]{2,1,0:T(8,128)(2,1)S(1)}, bf16[3,128,1152]{2,1,0:T(8,128)(2,1)S(1)}, u32[]{:S(2)}, u32[]{:S(2)}) collective-permute-start(bf16[3,128,1152]{2,1,0:T(8,128)(2,1)S(1)} %pad_maximum_fusion.6), channel_id=1, source_target_pairs={{0,8},{4,12},{8,0},{12,4},{16,24},{20,28},{24,16},{28,20},{1,9},{5... | collective-permute-start | bytes 2654216 | tf_op jit(solution)/shard_map/ppermute | solution.py:41
  170.3 21.8 %collective-permute-start.41 = (bf16[3,128,1152]{2,1,0:T(8,128)(2,1)S(1)}, bf16[3,128,1152]{2,1,0:T(8,128)(2,1)S(1)}, u32[]{:S(2)}, u32[]{:S(2)}) collective-permute-start(bf16[3,128,1152]{2,1,0:T(8,128)(2,1)S(1)} %pad_maximum_fusion.7), channel_id=1, source_target_pairs={{0,16},{4,20},{8,24},{12,28},{16,0},{20,4},{24,8},{28,12},{1,17},{... | collective-permute-start | bytes 2654216 | tf_op jit(solution)/shard_map/ppermute | solution.py:41
  173.8 2.7 %collective-permute-start.36 = (bf16[4,512,256]{2,1,0:T(8,128)(2,1)S(1)}, bf16[4,512,256]{2,1,0:T(8,128)(2,1)S(1)}, u32[]{:S(2)}, u32[]{:S(2)}) collective-permute-start(bf16[4,512,256]{2,1,0:T(8,128)(2,1)S(1)} %pad_maximum_fusion.4), channel_id=1, source_target_pairs={{0,4},{4,0},{8,12},{12,8},{16,20},{20,16},{24,28},{28,24},{1,5},{5... | collective-permute-start | bytes 3145736 | tf_op jit(solution)/shard_map/ppermute | solution.py:41
  176.6 8.3 %collective-permute-start.39 = (bf16[64,1024]{1,0:T(8,128)(2,1)S(1)}, bf16[64,1024]{1,0:T(8,128)(2,1)S(1)}, u32[]{:S(2)}, u32[]{:S(2)}) collective-permute-start(bf16[64,1024]{1,0:T(8,128)(2,1)S(1)} %get-tuple-element.204), channel_id=1, source_target_pairs={{0,3},{1,2},{2,1},{3,0},{4,7},{5,6},{6,5},{7,4},{8,11},{9,10},{10,... | collective-permute-start | bytes 393224 | tf_op jit(solution)/shard_map/ppermute | solution.py:41
  178.6 11.8 %collective-permute-start.38 = (bf16[64,1024]{1,0:T(8,128)(2,1)S(1)}, bf16[64,1024]{1,0:T(8,128)(2,1)S(1)}, u32[]{:S(2)}, u32[]{:S(2)}) collective-permute-start(bf16[64,1024]{1,0:T(8,128)(2,1)S(1)} %get-tuple-element.203), channel_id=1, source_target_pairs={{0,2},{1,3},{2,0},{3,1},{4,6},{5,7},{6,4},{7,5},{8,10},{9,11},{10,... | collective-permute-start | bytes 393224 | tf_op jit(solution)/shard_map/ppermute | solution.py:41
  178.6 12.3 %collective-permute-start.37 = (bf16[64,1024]{1,0:T(8,128)(2,1)S(1)}, bf16[64,1024]{1,0:T(8,128)(2,1)S(1)}, u32[]{:S(2)}, u32[]{:S(2)}) collective-permute-start(bf16[64,1024]{1,0:T(8,128)(2,1)S(1)} %get-tuple-element.202), channel_id=1, source_target_pairs={{0,1},{1,0},{2,3},{3,2},{4,5},{5,4},{6,7},{7,6},{8,9},{9,8},{10,11... | collective-permute-start | bytes 393224 | tf_op jit(solution)/shard_map/ppermute | solution.py:41
  181.4 14.0 %copy-start.14 = (f32[64]{0:T(128)S(1)}, f32[64]{0:T(128)}, u32[]{:S(2)}) copy-start(f32[64]{0:T(128)} %copy-done.13) | copy-start | bytes 772
  181.4 14.2 %copy-start.9 = (f32[1024]{0:T(1024)S(1)}, f32[1024]{0:T(1024)}, u32[]{:S(2)}) copy-start(f32[1024]{0:T(1024)} %custom-call.1) | copy-start | bytes 12292
  185.0 9.4 %collective-permute-start.42 = (bf16[4,64,256]{2,1,0:T(8,128)(2,1)S(1)}, bf16[4,64,256]{2,1,0:T(8,128)(2,1)S(1)}, u32[]{:S(2)}, u32[]{:S(2)}) collective-permute-start(bf16[4,64,256]{2,1,0:T(8,128)(2,1)S(1)} %get-tuple-element.201), channel_id=1, source_target_pairs={{0,8},{4,12},{8,0},{12,4},{16,24},{20,28},{24,16},{28,20},{1,9},{5... | collective-permute-start | bytes 393224 | tf_op jit(solution)/shard_map/ppermute | solution.py:41
  190.4 5.0 %collective-permute-start.43 = (bf16[4,64,256]{2,1,0:T(8,128)(2,1)S(1)}, bf16[4,64,256]{2,1,0:T(8,128)(2,1)S(1)}, u32[]{:S(2)}, u32[]{:S(2)}) collective-permute-start(bf16[4,64,256]{2,1,0:T(8,128)(2,1)S(1)} %get-tuple-element.200), channel_id=1, source_target_pairs={{0,16},{4,20},{8,24},{12,28},{16,0},{20,4},{24,8},{28,12},{1,17},{... | collective-permute-start | bytes 393224 | tf_op jit(solution)/shard_map/ppermute | solution.py:41
  196.3 10.3 %collective-permute-start.46 = (f32[5,1024]{1,0:T(8,128)}, f32[5,1024]{1,0:T(8,128)S(1)}, u32[]{:S(2)}, u32[]{:S(2)}) collective-permute-start(f32[5,1024]{1,0:T(8,128)} %pad_maximum_fusion.15), channel_id=1, source_target_pairs={{0,1},{1,0},{2,3},{3,2},{4,5},{5,4},{6,7},{7,6},{8,9},{9,8},{10,11... | collective-permute-start | bytes 61448 | tf_op jit(solution)/shard_map/ppermute | solution.py:41
  196.3 10.3 %collective-permute-start.45 = (f32[5,1024]{1,0:T(8,128)}, f32[5,1024]{1,0:T(8,128)}, u32[]{:S(2)}, u32[]{:S(2)}) collective-permute-start(f32[5,1024]{1,0:T(8,128)} %pad_maximum_fusion.15), channel_id=1, source_target_pairs={{0,2},{1,3},{2,0},{3,1},{4,6},{5,7},{6,4},{7,5},{8,10},{9,11},{10,... | collective-permute-start | bytes 61448 | tf_op jit(solution)/shard_map/ppermute | solution.py:41
  198.8 7.8 %collective-permute-start.44 = (f32[5,1024]{1,0:T(8,128)}, f32[5,1024]{1,0:T(8,128)}, u32[]{:S(2)}, u32[]{:S(2)}) collective-permute-start(f32[5,1024]{1,0:T(8,128)} %pad_maximum_fusion.15), channel_id=1, source_target_pairs={{0,3},{1,2},{2,1},{3,0},{4,7},{5,6},{6,5},{7,4},{8,11},{9,10},{10,... | collective-permute-start | bytes 61448 | tf_op jit(solution)/shard_map/ppermute | solution.py:41
  201.2 6.9 %collective-permute-start.47 = (bf16[4,128,256]{2,1,0:T(8,128)(2,1)S(1)}, bf16[4,128,256]{2,1,0:T(8,128)(2,1)}, u32[]{:S(2)}, u32[]{:S(2)}) collective-permute-start(bf16[4,128,256]{2,1,0:T(8,128)(2,1)S(1)} %pad_maximum_fusion.13), channel_id=1, source_target_pairs={{0,8},{4,12},{8,0},{12,4},{16,24},{20,28},{24,16},{28,20},{1,9},{5... | collective-permute-start | bytes 786440 | tf_op jit(solution)/shard_map/ppermute | solution.py:41
  202.6 6.7 %collective-permute-start.48 = (bf16[4,128,256]{2,1,0:T(8,128)(2,1)S(1)}, bf16[4,128,256]{2,1,0:T(8,128)(2,1)}, u32[]{:S(2)}, u32[]{:S(2)}) collective-permute-start(bf16[4,128,256]{2,1,0:T(8,128)(2,1)S(1)} %pad_maximum_fusion.14), channel_id=1, source_target_pairs={{0,16},{4,20},{8,24},{12,28},{16,0},{20,4},{24,8},{28,12},{1,17},{... | collective-permute-start | bytes 786440 | tf_op jit(solution)/shard_map/ppermute | solution.py:41
  209.3 4.6 %collective-permute-start.55 = (f32[5,1024]{1,0:T(8,128)S(1)}, f32[5,1024]{1,0:T(8,128)S(1)}, u32[]{:S(2)}, u32[]{:S(2)}) collective-permute-start(f32[5,1024]{1,0:T(8,128)S(1)} %select_add_fusion.1), channel_id=1, source_target_pairs={{0,4},{4,0},{8,12},{12,8},{16,20},{20,16},{24,28},{28,24},{1,5},{5... | collective-permute-start | bytes 61448 | tf_op jit(solution)/shard_map/ppermute | solution.py:41
  209.3 5.8 %collective-permute-start.54 = (f32[5,1024]{1,0:T(8,128)S(1)}, f32[5,1024]{1,0:T(8,128)S(1)}, u32[]{:S(2)}, u32[]{:S(2)}) collective-permute-start(f32[5,1024]{1,0:T(8,128)S(1)} %select_add_fusion.1), channel_id=1, source_target_pairs={{0,8},{4,12},{8,0},{12,4},{16,24},{20,28},{24,16},{28,20},{1,9},{5... | collective-permute-start | bytes 61448 | tf_op jit(solution)/shard_map/ppermute | solution.py:41
  209.9 8.4 %collective-permute-start.53 = (f32[5,1024]{1,0:T(8,128)S(1)}, f32[5,1024]{1,0:T(8,128)S(1)}, u32[]{:S(2)}, u32[]{:S(2)}) collective-permute-start(f32[5,1024]{1,0:T(8,128)S(1)} %select_add_fusion.1), channel_id=1, source_target_pairs={{0,12},{4,8},{8,4},{12,0},{16,28},{20,24},{24,20},{28,16},{1,13},{... | collective-permute-start | bytes 61448 | tf_op jit(solution)/shard_map/ppermute | solution.py:41
  211.2 7.1 %collective-permute-start.52 = (f32[5,1024]{1,0:T(8,128)S(1)}, f32[5,1024]{1,0:T(8,128)S(1)}, u32[]{:S(2)}, u32[]{:S(2)}) collective-permute-start(f32[5,1024]{1,0:T(8,128)S(1)} %select_add_fusion.1), channel_id=1, source_target_pairs={{0,16},{4,20},{8,24},{12,28},{16,0},{20,4},{24,8},{28,12},{1,17},{... | collective-permute-start | bytes 61448 | tf_op jit(solution)/shard_map/ppermute | solution.py:41
  211.7 6.6 %collective-permute-start.51 = (f32[5,1024]{1,0:T(8,128)S(1)}, f32[5,1024]{1,0:T(8,128)S(1)}, u32[]{:S(2)}, u32[]{:S(2)}) collective-permute-start(f32[5,1024]{1,0:T(8,128)S(1)} %select_add_fusion.1), channel_id=1, source_target_pairs={{0,20},{4,16},{8,28},{12,24},{16,4},{20,0},{24,12},{28,8},{1,21},{... | collective-permute-start | bytes 61448 | tf_op jit(solution)/shard_map/ppermute | solution.py:41
  213.9 4.9 %collective-permute-start.50 = (f32[5,1024]{1,0:T(8,128)S(1)}, f32[5,1024]{1,0:T(8,128)S(1)}, u32[]{:S(2)}, u32[]{:S(2)}) collective-permute-start(f32[5,1024]{1,0:T(8,128)S(1)} %select_add_fusion.1), channel_id=1, source_target_pairs={{0,24},{4,28},{8,16},{12,20},{16,8},{20,12},{24,0},{28,4},{1,25},{... | collective-permute-start | bytes 61448 | tf_op jit(solution)/shard_map/ppermute | solution.py:41
  215.1 4.2 %collective-permute-start.49 = (f32[5,1024]{1,0:T(8,128)S(1)}, f32[5,1024]{1,0:T(8,128)S(1)}, u32[]{:S(2)}, u32[]{:S(2)}) collective-permute-start(f32[5,1024]{1,0:T(8,128)S(1)} %select_add_fusion.1), channel_id=1, source_target_pairs={{0,28},{4,24},{8,20},{12,16},{16,12},{20,8},{24,4},{28,0},{1,29},{... | collective-permute-start | bytes 61448 | tf_op jit(solution)/shard_map/ppermute | solution.py:41
  (22 other events, 115.9 us)
